TPU v7x, 256 devices: a whole 4x4x8 slice. The times are simulated.
256 devices in a mesh: gx: 32 (over x, y, core), gy: 8 (over z).
Axes of the slice: x: 4, y: 4, z: 8, core: 2. Of those that a mesh axis runs over, the one named last changes fastest.
Arguments:
- nodes: bfloat16 [262144, 128], P(('gx', 'gy')), may hold values from -6 to 6
- ghost_rows: int32 [256, 8, 256], P(('gx', 'gy')), may hold values from 0 to 1023
- ghost_count: int32 [256, 8], P(('gx', 'gy')), may hold values from 0 to 256, as said below
- edge_send: int32 [256, 4096], P(('gx', 'gy')), may hold values from 0 to 3071
- edge_recv: int32 [256, 4096], P(('gx', 'gy')), may hold values from 0 to 1023
- edge_count: int32 [256], P(('gx', 'gy')), may hold values from 512 to 4096, as said below
- pool_map: int32 [256, 1024], P(('gx', 'gy')), may hold values from 0 to 191, as said below
- w_edge_in: bfloat16 [256, 128], replicated, may hold values from -0.375 to 0.375
- w_edge_out: bfloat16 [128, 128], replicated, may hold values from -0.5 to 0.5
- w_node_in: bfloat16 [256, 128], replicated, may hold values from -0.375 to 0.375
- w_node_out: bfloat16 [128, 128], replicated, may hold values from -0.5 to 0.5
- w_coarse_in: bfloat16 [128, 128], replicated, may hold values from -0.5 to 0.5
- w_coarse_out: bfloat16 [128, 128], replicated, may hold values from -0.5 to 0.5
- d_fine: bfloat16 [262144, 128], P(('gx', 'gy')), may hold values from -6 to 6
- d_coarse: bfloat16 [32768, 128], P(('gx', 'gy')), may hold values from -6 to 6
Outputs:
- fine_out: bfloat16 [262144, 128], P(('gx', 'gy'))
- coarse_out: bfloat16 [32768, 128], P(('gx', 'gy'))
- grad_nodes: float32 [262144, 128], P(('gx', 'gy'))
- grad_edge_in: float32 [256, 128], replicated
- grad_edge_out: float32 [128, 128], replicated
- grad_node_in: float32 [256, 128], replicated
- grad_node_out: float32 [128, 128], replicated
- grad_coarse_in: float32 [128, 128], replicated
- grad_coarse_out: float32 [128, 128], replicated
Inputs may be any that keep to these rules, and one draw needn't show every extreme that they name: `ghost_count`: every device fills all 256 slots for at least one offset. `edge_count`: at least one device has all 4096 slots live. `pool_map`: values under 32 occur only on devices that are not first along gy, and values of 160 or more only on devices that are not last along gy, so every parent lies in the device's gx column.
All inputs are finite; a program needn't handle non-finite values.
Results may differ from a plain program's by a relative error of at most 0.012.
Values may be sent and summed in bfloat16 or wider, within the bound.
No kernel may reach another device: no remote copies, remote signals or barrier semaphores. Data moves between devices by JAX's collectives and lax.ppermute only.
A program may use at most 64 MiB of HBM per device.

v0:
```python
import jax
import jax.numpy as jnp
from jax import lax
from jax.sharding import Mesh
from jax.sharding import PartitionSpec as P

BAND = 32
GX_GY = ("gx_0", "gx_1", "gx_2", "gy")
GX = ("gx_0", "gx_1", "gx_2")


offset_across = (-1, -1, -1, 0, 0, 1, 1, 1)
offset_along = (-1, 0, 1, -1, 1, -1, 0, 1)


def with_halo(x, sides, width):
    for axis, dim in sides:
        devices, length = (lax.axis_size(axis), x.shape[dim])
        up = [(i, (i + 1) % devices) for i in range(devices - 1)]
        down = [(j, i) for i, j in up]
        last = lax.slice_in_dim(x, length - width, length, axis=dim)
        initial = lax.slice_in_dim(x, 0, width, axis=dim)
        before = lax.ppermute(last, axis, up)
        after = lax.ppermute(initial, axis, down)
        x = jnp.concatenate([before, x, after], axis=dim)
    return x


def padded_to(lines, devices):
    spare = -lines.shape[0] % devices
    if not spare:
        return lines
    return jnp.concatenate([lines, jnp.zeros((spare, *lines.shape[1:]), lines.dtype)])


def sent_to_all(x, axis):
    devices = lax.axis_size(axis)
    return lax.all_to_all(jnp.broadcast_to(x[None], (devices, *x.shape)), axis, 0, 0, tiled=True)


def laid_out(pieces, dim):
    pieces = jnp.moveaxis(pieces, 0, dim)
    shape = pieces.shape
    return pieces.reshape(*shape[:dim], shape[dim] * shape[dim + 1], *shape[dim + 2 :])


def whole_of(x, axes, dim):
    far, near = axes
    initial = sent_to_all(x, far)
    pieces = jnp.swapaxes(sent_to_all(initial, near), 0, 1)
    return laid_out(pieces.reshape(-1, *x.shape), dim)


def cut_along(x, dim, devices):
    before, after = (x.shape[:dim], x.shape[dim + 1 :])
    return jnp.moveaxis(x.reshape(*before, devices, -1, *after), dim, 0)


def sent_and_summed(x, axis, dim):
    pieces = cut_along(x, dim, lax.axis_size(axis))
    arrived = lax.all_to_all(pieces, axis, split_axis=0, concat_axis=0, tiled=True)
    return arrived.sum(axis=0)


def summed_rows(x, axes, dim):
    far, near = axes
    own = sent_and_summed(cut_along(x, dim, lax.axis_size(far)), near, dim + 1)
    return jnp.sum(lax.all_to_all(own, far, 0, 0, tiled=True), axis=0)


def total_of(x, axes):
    padded = padded_to(x, lax.axis_size(axes[0]) * lax.axis_size(axes[1]))
    whole = whole_of(summed_rows(padded, axes, 0), axes, 0)
    return lax.slice_in_dim(whole, 0, len(x)).reshape(x.shape)


def in_one(arrays, axis):
    ends = [0]
    for a in arrays:
        ends.append(ends[-1] + a.size)
    running = total_of(jnp.concatenate([a.ravel() for a in arrays]), axis)
    return tuple((running[b:e].reshape(a.shape) for a, b, e in zip(arrays, ends, ends[1:])))


def matmul(left, right):
    return jnp.dot(left, right, preferred_element_type=jnp.float32)


def silu_slope(pre_value):
    sigmoid_v = jax.nn.sigmoid(pre_value)
    return sigmoid_v * (1.0 + pre_value * (1.0 - sigmoid_v))


def fine_forward(owned, ghosts, send_index, recv_index, edge_live, weights):
    w_edge_in, w_edge_out, w_node_in, w_node_out = weights
    latent = owned.shape[1]
    lookup = jnp.concatenate([owned, ghosts], axis=0)
    senders = lookup[send_index]
    receivers = owned[recv_index]
    edge_pre = matmul(senders, w_edge_in[:latent]) + matmul(receivers, w_edge_in[latent:])
    edge_act = jax.nn.silu(edge_pre).astype(jnp.bfloat16)
    message = (matmul(edge_act, w_edge_out) * edge_live[:, None]).astype(jnp.bfloat16)
    summed = jax.ops.segment_sum(
        message.astype(jnp.float32), recv_index, num_segments=owned.shape[0]
    ).astype(jnp.bfloat16)
    node_pre = matmul(owned, w_node_in[:latent]) + matmul(summed, w_node_in[latent:])
    node_act = jax.nn.silu(node_pre).astype(jnp.bfloat16)
    fine_out = (owned.astype(jnp.float32) + matmul(node_act, w_node_out)).astype(jnp.bfloat16)
    return (fine_out, (senders, receivers, edge_pre, edge_act, summed, node_pre, node_act))


def fine_backward(owned, send_index, recv_index, edge_live, weights, stashed, d_total, lookup_rows):
    w_edge_in, w_edge_out, w_node_in, w_node_out = weights
    senders, receivers, edge_pre, edge_act, summed, node_pre, node_act = stashed
    rows_here, latent = owned.shape
    d_out16 = d_total.astype(jnp.bfloat16)
    g_node_out = matmul(node_act.T, d_out16)
    d_node_pre = (matmul(d_out16, w_node_out.T) * silu_slope(node_pre)).astype(jnp.bfloat16)
    g_node_in = jnp.concatenate([matmul(owned.T, d_node_pre), matmul(summed.T, d_node_pre)], axis=0)
    d_owned = d_total + matmul(d_node_pre, w_node_in[:latent].T)
    d_summed = matmul(d_node_pre, w_node_in[latent:].T).astype(jnp.bfloat16)
    d_message = d_summed[recv_index] * edge_live[:, None].astype(d_summed.dtype)
    g_edge_out = matmul(edge_act.T, d_message)
    d_edge_pre = (matmul(d_message, w_edge_out.T) * silu_slope(edge_pre)).astype(jnp.bfloat16)
    g_edge_in = jnp.concatenate(
        [matmul(senders.T, d_edge_pre), matmul(receivers.T, d_edge_pre)], axis=0
    )
    d_senders = matmul(d_edge_pre, w_edge_in[:latent].T)
    d_receivers = matmul(d_edge_pre, w_edge_in[latent:].T)
    d_lookup = jax.ops.segment_sum(d_senders, send_index, num_segments=lookup_rows)
    d_owned = (
        d_owned
        + d_lookup[:rows_here]
        + jax.ops.segment_sum(d_receivers, recv_index, num_segments=rows_here)
    )
    return (d_owned, d_lookup[rows_here:], (g_edge_in, g_edge_out, g_node_in, g_node_out))


def across_both(blocks):
    return with_halo(blocks, ((GX, 0), ("gy", 1)), 1)


def grid_blocks(blocks, flip):
    empty = jnp.zeros_like(blocks[0])
    table = [[empty, empty, empty], [empty, empty, empty], [empty, empty, empty]]
    for slot in range(8):
        table[1 + flip * offset_across[slot]][1 + flip * offset_along[slot]] = blocks[slot]
    return jnp.stack([jnp.stack(line) for line in table])


def spread_ghosts(outgoing):
    padded = across_both(grid_blocks(outgoing, 1))
    return jnp.stack(
        [padded[2 - 2 * offset_across[slot], 2 - 2 * offset_along[slot]] for slot in range(8)]
    )


def return_ghosts(d_blocks):
    padded = across_both(grid_blocks(d_blocks, -1))
    return jnp.stack(
        [padded[2 + 2 * offset_across[slot], 2 + 2 * offset_along[slot]] for slot in range(8)]
    )


def body(
    nodes,
    ghost_rows,
    ghost_count,
    edge_send,
    edge_recv,
    edge_count,
    pool_map,
    w_edge_in,
    w_edge_out,
    w_node_in,
    w_node_out,
    w_coarse_in,
    w_coarse_out,
    d_fine,
    d_coarse,
):
    rows_here, latent = nodes.shape
    ghost_lists = ghost_rows[0]
    peer_count, slot_count = ghost_lists.shape
    slot_live = jnp.arange(slot_count, dtype=jnp.int32)[None, :] < ghost_count[0][:, None]
    outgoing = jnp.where(slot_live[:, :, None], nodes[ghost_lists], jnp.zeros((), nodes.dtype))
    arrived = spread_ghosts(outgoing)
    send_index = edge_send[0]
    recv_index = edge_recv[0]
    edge_live = (jnp.arange(send_index.shape[0], dtype=jnp.int32) < edge_count[0]).astype(
        jnp.float32
    )
    weights = (w_edge_in, w_edge_out, w_node_in, w_node_out)
    fine_out, stashed = fine_forward(
        nodes,
        arrived.reshape(peer_count * slot_count, latent),
        send_index,
        recv_index,
        edge_live,
        weights,
    )
    groups = lax.axis_size("gy")
    coarse_rows = d_coarse.shape[0]
    fine_wide = fine_out.astype(jnp.float32)
    parents = pool_map[0]
    window = jax.ops.segment_sum(fine_wide, parents, num_segments=coarse_rows + 2 * BAND)
    rims = with_halo(
        jnp.stack([window[:BAND], window[coarse_rows + BAND :]]).astype(jnp.bfloat16),
        (("gy", 0),),
        1,
    ).astype(jnp.float32)
    pooled = (
        window[BAND : coarse_rows + BAND]
        .at[:BAND]
        .add(rims[0])
        .at[coarse_rows - BAND :]
        .add(rims[3])
    )
    coarse_in = (0.125 * pooled).astype(jnp.bfloat16)
    coarse_pre = matmul(coarse_in, w_coarse_in)
    coarse_act = jax.nn.silu(coarse_pre).astype(jnp.bfloat16)
    coarse_out = (coarse_in.astype(jnp.float32) + matmul(coarse_act, w_coarse_out)).astype(
        jnp.bfloat16
    )
    g_coarse_out = matmul(coarse_act.T, d_coarse)
    d_coarse_pre = (matmul(d_coarse, w_coarse_out.T) * silu_slope(coarse_pre)).astype(jnp.bfloat16)
    g_coarse_in = matmul(coarse_in.T, d_coarse_pre)
    d_coarse_in = (d_coarse.astype(jnp.float32) + matmul(d_coarse_pre, w_coarse_in.T)).astype(
        jnp.bfloat16
    )
    reach = with_halo(d_coarse_in, (("gy", 0),), BAND)
    parent_grad = reach[parents]
    d_total = d_fine.astype(jnp.float32) + 0.125 * parent_grad.astype(jnp.float32)
    d_owned, d_ghosts, partials = fine_backward(
        nodes,
        send_index,
        recv_index,
        edge_live,
        weights,
        stashed,
        d_total,
        rows_here + peer_count * slot_count,
    )
    returned = return_ghosts(d_ghosts.astype(jnp.bfloat16).reshape(peer_count, slot_count, latent))
    returned = jnp.where(slot_live[:, :, None], returned.astype(jnp.float32), 0.0)
    d_owned = d_owned + jax.ops.segment_sum(
        returned.reshape(peer_count * slot_count, latent),
        ghost_lists.reshape(peer_count * slot_count),
        num_segments=rows_here,
    )
    totals = in_one(
        (partials[0], partials[1], partials[2], partials[3], g_coarse_in, g_coarse_out),
        (("gx_0", "gx_1"), ("gx_2", "gy")),
    )
    grad_scale = 1.0 / (rows_here * lax.axis_size(GX) * groups) ** 0.5
    return (
        fine_out,
        coarse_out,
        d_owned,
        totals[0] * grad_scale,
        totals[1] * grad_scale,
        totals[2] * grad_scale,
        totals[3] * grad_scale,
        totals[4] * grad_scale,
        totals[5] * grad_scale,
    )


def solution(mesh):
    torus = Mesh(mesh.devices.reshape(4, 4, 2, mesh.shape["gy"]), ("gx_0", "gx_1", "gx_2", "gy"))
    in_specs = (
        P(GX_GY, None),
        P(GX_GY, None, None),
        P(GX_GY, None),
        P(GX_GY, None),
        P(GX_GY, None),
        P(GX_GY),
        P(GX_GY, None),
        P(),
        P(),
        P(),
        P(),
        P(),
        P(),
        P(GX_GY, None),
        P(GX_GY, None),
    )
    out_specs = (P(GX_GY, None), P(GX_GY, None), P(GX_GY, None), P(), P(), P(), P(), P(), P())
    return jax.shard_map(body, mesh=torus, in_specs=in_specs, out_specs=out_specs, check_vma=False)
```

profile of v0, /device:TPU:1, one launch (start us, length us, event | category | flops | bytes accessed | tf_op | source)
XLA Modules:
  0.0 279.6 jit_solution(15445813108119850936)
XLA Ops:
  0.7 0.7 iota_compare_fusion.1
  2.1 6.6 %gather_fusion = bf16[2048,128]{1,0:T(8,128)(2,1)S(1)} fusion(bf16[1024,128]{1,0:T(8,128)(2,1)} %param.19, s32[2048]{0:T(1024)S(1)} %broadcast_clamp_fusion.2), kind=kCustom, calls=%fused_computation | custom fusion | bytes 1056768 | tf_op jit(solution)/shard_map/gather | solution.py:186
  9.1 5.1 %collective-permute-start.1 = (bf16[1,3,256,128]{3,2,1,0:T(8,128)(2,1)S(1)}, bf16[1,3,256,128]{3,2,1,0:T(8,128)(2,1)S(1)}, u32[]{:S(2)}, u32[]{:S(2)}) collective-permute-start(bf16[1,3,256,128]{3,2,1,0:T(8,128)(2,1)S(1)} %get-tuple-element.51), channel_id=1, source_target_pairs={{8,0},{16,8},{24,16},{32,24},{40,32},{48,40},{56,48},{64,56},{72,6... | collective-permute-start | bytes 589832 | tf_op jit(solution)/shard_map/ppermute | solution.py:24
  14.3 1.9 collective-permute-start
  17.0 12.1 %gather_fusion.2 = bf16[4096,128]{1,0:T(8,128)(2,1)S(1)} fusion(bf16[1024,128]{1,0:T(8,128)(2,1)S(1)} %copy-done.1, s32[4096]{0:T(1024)S(1)} %get-tuple-element.61), kind=kCustom, calls=%fused_computation.2 | custom fusion | bytes 2113536 | tf_op jit(solution)/shard_map/gather | solution.py:99
  29.6 1.3 collective-permute-start.2
  31.5 1.0 fusion.64
  32.5 4.0 %collective-permute-start.3 = (bf16[5,1,256,128]{3,2,1,0:T(8,128)(2,1)S(1)}, bf16[5,1,256,128]{3,2,1,0:T(8,128)(2,1)S(1)}, u32[]{:S(2)}, u32[]{:S(2)}) collective-permute-start(bf16[5,1,256,128]{3,2,1,0:T(8,128)(2,1)S(1)} %get-tuple-element.35), channel_id=1, source_target_pairs={{0,1},{1,2},{2,3},{3,4},{4,5},{5,6},{6,7},{8,9},{9,10},{10,11},{11... | collective-permute-start | bytes 983048 | tf_op jit(solution)/shard_map/ppermute | solution.py:23
  36.5 3.7 %collective-permute-done.2 = bf16[5,1,256,128]{3,2,1,0:T(8,128)(2,1)S(1)} collective-permute-done((bf16[5,1,256,128]{3,2,1,0:T(8,128)(2,1)S(1)}, bf16[5,1,256,128]{3,2,1,0:T(8,128)(2,1)S(1)}, u32[]{:S(2)}, u32[]{:S(2)}) %collective-permute-start.2) | collective-permute-done | bytes 327712 | tf_op jit(solution)/shard_map/ppermute | solution.py:24
  40.2 2.4 collective-permute-done.3
  42.9 12.1 %gather_fusion.1 = bf16[4096,128]{1,0:T(8,128)(2,1)S(1)} fusion(bf16[3072,128]{1,0:T(8,128)(2,1)S(1)} %pad_maximum_fusion, s32[4096]{0:T(1024)S(1)} %get-tuple-element.62), kind=kCustom, calls=%fused_computation.1 | custom fusion | bytes 2113536 | tf_op jit(solution)/shard_map/gather | solution.py:98
  56.1 1.8 fusion.1
  57.9 22.8 %scatter_custom_fusion = f32[1024,128]{1,0:T(8,128)S(1)} fusion(s32[4096]{0:T(1024)S(1)} %bitcast.210, f32[4096,128]{1,0:T(8,128)} %fusion.1, f32[]{:T(128)} %constant.80.clone.1), kind=kCustom, calls=%fused_computation.61 | custom fusion | flops 524288 | bytes 524800 | tf_op jit(solution)/shard_map/scatter-add | solution.py:103
  81.0 1.1 fusion.8
  82.2 6.1 %scatter_custom_fusion.1 = f32[192,128]{1,0:T(8,128)S(1)} fusion(s32[1024]{0:T(1024)S(1)} %bitcast.219, bf16[1024,128]{1,0:T(8,128)(2,1)S(1)} %fusion.8, f32[]{:T(128)} %constant.80.clone.1), kind=kCustom, calls=%fused_computation.53 | custom fusion | flops 262144 | bytes 360452 | tf_op jit(solution)/shard_map/scatter-add | solution.py:206
  88.3 4.4 %collective-permute-start.4 = (bf16[1,32,128]{2,1,0:T(8,128)(2,1)S(1)}, bf16[1,32,128]{2,1,0:T(8,128)(2,1)S(1)}, u32[]{:S(2)}, u32[]{:S(2)}) collective-permute-start(bf16[1,32,128]{2,1,0:T(8,128)(2,1)S(1)} %get-tuple-element.55), channel_id=1, source_target_pairs={{0,1},{1,2},{2,3},{3,4},{4,5},{5,6},{6,7},{8,9},{9,10},{10,11},{11... | collective-permute-start | bytes 24584 | tf_op jit(solution)/shard_map/ppermute | solution.py:23
  92.7 1.3 collective-permute-start.5
  95.2 2.4 collective-permute-done.5
  97.8 0.9 fusion.11
  98.9 4.4 %collective-permute-start.6 = (bf16[32,128]{1,0:T(8,128)(2,1)S(1)}, bf16[32,128]{1,0:T(8,128)(2,1)S(1)}, u32[]{:S(2)}, u32[]{:S(2)}) collective-permute-start(bf16[32,128]{1,0:T(8,128)(2,1)S(1)} %get-tuple-element.57), channel_id=1, source_target_pairs={{0,1},{1,2},{2,3},{3,4},{4,5},{5,6},{6,7},{8,9},{9,10},{10,11},{11... | collective-permute-start | bytes 24584 | tf_op jit(solution)/shard_map/ppermute | solution.py:23
  103.3 1.5 collective-permute-start.7
  104.8 1.5 fusion.10
  106.3 3.2 %collective-permute-done.7 = bf16[32,128]{1,0:T(8,128)(2,1)S(1)} collective-permute-done((bf16[32,128]{1,0:T(8,128)(2,1)S(1)}, bf16[32,128]{1,0:T(8,128)(2,1)S(1)}, u32[]{:S(2)}, u32[]{:S(2)}) %collective-permute-start.7) | collective-permute-done | bytes 8224 | tf_op jit(solution)/shard_map/ppermute | solution.py:24
  109.5 3.2 %gather_fusion.3 = bf16[1024,128]{1,0:T(8,128)(2,1)S(1)} fusion(bf16[192,128]{1,0:T(8,128)(2,1)S(1)} %pad_maximum_fusion.1, s32[1024]{0:T(1024)S(1)} %broadcast_clamp_fusion.3), kind=kCustom, calls=%fused_computation.3 | custom fusion | bytes 528384 | tf_op jit(solution)/shard_map/gather | solution.py:232
  112.7 1.6 fusion.9
  114.3 0.9 fusion.32
  115.2 0.9 convolution_bitcast_fusion.4
  116.4 14.9 %gather_fusion.4 = bf16[4096,128]{1,0:T(8,128)(2,1)} fusion(bf16[1024,128]{1,0:T(8,128)(2,1)S(1)} %convolution_convert_fusion, s32[4096]{0:T(1024)S(1)} %get-tuple-element.61), kind=kCustom, calls=%fused_computation.4 | custom fusion | bytes 2113536 | tf_op jit(solution)/shard_map/gather | solution.py:122
  131.3 2.9 %fusion.2 = bf16[4096,128]{1,0:T(8,128)(2,1)S(1)} fusion(bf16[128,128]{1,0:T(8,128)(2,1)S(1)} %copy-done, f32[4096,128]{1,0:T(8,128)} %copy-done.5, bf16[4096,128]{1,0:T(8,128)(2,1)} %gather_fusion.4, bf16[4096]{0:T(1024)(128)(2,1)} %get-tuple-element.60), kind=kOutput, calls=%fused_computation.15 | convolution fusion | flops 139460608 | bytes 4235264 | tf_op jit(solution)/shard_map/dot_general | solution.py:86
  135.2 1.8 fusion.59
  137.8 1.8 fusion.6
  140.3 1.0 fusion.5
  141.3 0.8 fusion.4
  142.1 23.0 %scatter_custom_fusion.2 = f32[3072,128]{1,0:T(8,128)S(1)} fusion(s32[4096]{0:T(1024)} %bitcast.216, f32[4096,128]{1,0:T(8,128)} %fusion.59, f32[]{:T(128)} %constant.80.clone.1), kind=kCustom, calls=%fused_computation.46 | custom fusion | flops 524288 | bytes 1573376 | tf_op jit(solution)/shard_map/scatter-add | solution.py:130
  166.6 5.8 %collective-permute-start.8 = (bf16[1,3,256,128]{3,2,1,0:T(8,128)(2,1)}, bf16[1,3,256,128]{3,2,1,0:T(8,128)(2,1)}, u32[]{:S(2)}, u32[]{:S(2)}) collective-permute-start(bf16[1,3,256,128]{3,2,1,0:T(8,128)(2,1)} %maximum_bitcast_fusion.1), channel_id=1, source_target_pairs={{0,8},{8,16},{16,24},{24,32},{32,40},{40,48},{48,56},{56,64},{64,7... | collective-permute-start | bytes 589832 | tf_op jit(solution)/shard_map/ppermute | solution.py:23
  172.4 0.8 fusion.3
  173.2 1.1 reshape_reshape.4
  174.4 1.1 copy.31
  175.5 6.9 %all-to-all-start = ((f32[16,16,512]{2,1,0:T(8,128)}), f32[16,16,512]{2,1,0:T(8,128)}, u32[]{:S(2)}, u32[]{:S(2)}) async-start(f32[16,16,512]{2,1,0:T(8,128)} %copy.31), calls=%async_computation | async-start | bytes 1048576 | tf_op jit(solution)/shard_map/all_to_all | solution.py:61
  182.4 1.0 maximum_bitcast_fusion.2
  183.4 2.1 collective-permute-start.9
  185.5 0.9 constant_dynamic-update-slice_fusion.7
  186.4 0.9 constant_dynamic-update-slice_fusion.6
  187.4 1.0 fusion.29
  188.5 2.3 collective-permute-done.9
  190.8 0.9 fusion.75
  191.7 4.2 %collective-permute-start.10 = (bf16[5,1,256,128]{3,2,1,0:T(8,128)(2,1)}, bf16[5,1,256,128]{3,2,1,0:T(8,128)(2,1)}, u32[]{:S(2)}, u32[]{:S(2)}) collective-permute-start(bf16[5,1,256,128]{3,2,1,0:T(8,128)(2,1)} %get-tuple-element.34), channel_id=1, source_target_pairs={{0,1},{1,2},{2,3},{3,4},{4,5},{5,6},{6,7},{8,9},{9,10},{10,11},{11... | collective-permute-start | bytes 983048 | tf_op jit(solution)/shard_map/ppermute | solution.py:23
  196.1 1.8 fusion.56
  197.9 22.9 %scatter_fusion = f32[1024,128]{1,0:T(8,128)S(1)} fusion(f32[1024,128]{1,0:T(8,128)S(1)} %fusion.7, s32[4096]{0:T(1024)S(1)} %bitcast.211, f32[4096,128]{1,0:T(8,128)} %fusion.56), kind=kCustom, calls=%fused_computation.8 | custom fusion | flops 524288 | bytes 6307840 | tf_op jit(solution)/shard_map/scatter-add | solution.py:134
  220.8 1.3 collective-permute-start.11
  222.1 0.8 fusion.44
  223.0 1.1 reduce_sum.18
  224.7 7.8 %all-to-all-start.1 = ((f32[16,1,512]{2,1,0:T(1,128)}), f32[16,1,512]{2,1,0:T(1,128)S(1)}, u32[]{:S(2)}, u32[]{:S(2)}) async-start(f32[16,1,512]{2,1,0:T(1,128)} %all_to_all.17), calls=%async_computation.1 | async-start | bytes 65536 | tf_op jit(solution)/shard_map/all_to_all | solution.py:68
  232.5 0.9 fusion.43
  233.4 5.6 %all-to-all-done.1 = f32[16,1,512]{2,1,0:T(1,128)S(1)} async-done(((f32[16,1,512]{2,1,0:T(1,128)}), f32[16,1,512]{2,1,0:T(1,128)S(1)}, u32[]{:S(2)}, u32[]{:S(2)}) %all-to-all-start.1) | async-done | bytes 32800 | tf_op jit(solution)/shard_map/all_to_all | solution.py:68
  239.7 3.5 %all-to-all-start.2 = ((f32[16,1,512]{2,1,0:T(1,128)}), f32[16,1,512]{2,1,0:T(1,128)S(1)}, u32[]{:S(2)}, u32[]{:S(2)}) async-start(f32[16,1,512]{2,1,0:T(1,128)} %broadcast_in_dim.60), calls=%async_computation.2 | async-start | bytes 65536 | tf_op jit(solution)/shard_map/all_to_all | solution.py:38
  243.2 6.4 %all-to-all-done.2 = f32[16,1,512]{2,1,0:T(1,128)S(1)} async-done(((f32[16,1,512]{2,1,0:T(1,128)}), f32[16,1,512]{2,1,0:T(1,128)S(1)}, u32[]{:S(2)}, u32[]{:S(2)}) %all-to-all-start.2) | async-done | bytes 32800 | tf_op jit(solution)/shard_map/all_to_all | solution.py:38
  249.6 0.9 broadcast_in_dim.62
  250.4 8.6 %all-to-all-start.3 = ((f32[16,16,512]{2,1,0:T(8,128)}), f32[16,16,512]{2,1,0:T(8,128)S(1)}, u32[]{:S(2)}, u32[]{:S(2)}) async-start(f32[16,16,512]{2,1,0:T(8,128)} %broadcast_in_dim.62), calls=%async_computation.3 | async-start | bytes 1048576 | tf_op jit(solution)/shard_map/all_to_all | solution.py:38
  259.0 0.9 fusion.41
  259.9 0.9 fusion.39
  260.7 0.9 fusion.38
  261.6 12.9 %scatter_custom_fusion.4 = f32[1024,128]{1,0:T(8,128)S(1)} fusion(s32[2048]{0:T(1024)} %bitcast.218, bf16[2048,128]{1,0:T(8,128)(2,1)S(1)} %bitcast.208, f32[]{:T(128)} %constant.80.clone.1, pred[2048]{0:T(1024)(128)(4,1)S(1)} %copy-done.40), kind=kCustom, calls=%fused_computation.42 | custom fusion | flops 786432 | bytes 1051648 | tf_op jit(solution)/shard_map/scatter-add | solution.py:246
  274.5 0.8 add.150
  (168 shorter events, 15.3 us)
Async XLA Ops:
  0.6 55.2 %copy-start = (bf16[128,128]{1,0:T(8,128)(2,1)S(1)}, bf16[128,128]{1,0:T(8,128)(2,1)}, u32[]{:S(2)}) copy-start(bf16[128,128]{1,0:T(8,128)(2,1)} %param.27) | copy-start | bytes 98308
  8.7 8.2 %copy-start.38 = (s32[1,4096]{1,0:T(1,128)S(1)}, s32[1,4096]{1,0:T(1,128)}, u32[]{:S(2)}) copy-start(s32[1,4096]{1,0:T(1,128)} %param.22) | copy-start | bytes 49156
  8.7 8.2 %copy-start.31 = (s32[1,4096]{1,0:T(1,128)S(1)}, s32[1,4096]{1,0:T(1,128)}, u32[]{:S(2)}) copy-start(s32[1,4096]{1,0:T(1,128)} %param.23) | copy-start | bytes 49156
  8.7 8.2 %copy-start.1 = (bf16[1024,128]{1,0:T(8,128)(2,1)S(1)}, bf16[1024,128]{1,0:T(8,128)(2,1)}, u32[]{:S(2)}) copy-start(bf16[1024,128]{1,0:T(8,128)(2,1)} %param.19) | copy-start | bytes 786436
  9.1 20.3 %collective-permute-start.1 = (bf16[1,3,256,128]{3,2,1,0:T(8,128)(2,1)S(1)}, bf16[1,3,256,128]{3,2,1,0:T(8,128)(2,1)S(1)}, u32[]{:S(2)}, u32[]{:S(2)}) collective-permute-start(bf16[1,3,256,128]{3,2,1,0:T(8,128)(2,1)S(1)} %get-tuple-element.51), channel_id=1, source_target_pairs={{8,0},{16,8},{24,16},{32,24},{40,32},{48,40},{56,48},{64,56},{72,6... | collective-permute-start | bytes 589832 | tf_op jit(solution)/shard_map/ppermute | solution.py:24
  14.3 15.0 %collective-permute-start = (bf16[1,3,256,128]{3,2,1,0:T(8,128)(2,1)S(1)}, bf16[1,3,256,128]{3,2,1,0:T(8,128)(2,1)S(1)}, u32[]{:S(2)}, u32[]{:S(2)}) collective-permute-start(bf16[1,3,256,128]{3,2,1,0:T(8,128)(2,1)S(1)} %get-tuple-element.52), channel_id=1, source_target_pairs={{0,8},{8,16},{16,24},{24,32},{32,40},{40,48},{48,56},{56,64},{64,7... | collective-permute-start | bytes 589832 | tf_op jit(solution)/shard_map/ppermute | solution.py:23
  17.0 12.2 %copy-start.42 = (s32[1,1024]{1,0:T(1,128)S(1)}, s32[1,1024]{1,0:T(1,128)}, u32[]{:S(2)}) copy-start(s32[1,1024]{1,0:T(1,128)} %param.25) | copy-start | bytes 12292
  29.1 2.4 copy-start.22
  29.2 11.0 %copy-start.43 = (bf16[3]{0:T(256)(128)(2,1)}, bf16[3]{0:T(256)(128)(2,1)S(1)}, u32[]{:S(2)}) copy-start(bf16[3]{0:T(256)(128)(2,1)S(1)} %pad.27.clone) | copy-start | bytes 22
  29.6 10.7 %collective-permute-start.2 = (bf16[5,1,256,128]{3,2,1,0:T(8,128)(2,1)S(1)}, bf16[5,1,256,128]{3,2,1,0:T(8,128)(2,1)S(1)}, u32[]{:S(2)}, u32[]{:S(2)}) collective-permute-start(bf16[5,1,256,128]{3,2,1,0:T(8,128)(2,1)S(1)} %get-tuple-element.36), channel_id=1, source_target_pairs={{1,0},{2,1},{3,2},{4,3},{5,4},{6,5},{7,6},{9,8},{10,9},{11,10},{12... | collective-permute-start | bytes 983048 | tf_op jit(solution)/shard_map/ppermute | solution.py:24
  32.5 10.2 %collective-permute-start.3 = (bf16[5,1,256,128]{3,2,1,0:T(8,128)(2,1)S(1)}, bf16[5,1,256,128]{3,2,1,0:T(8,128)(2,1)S(1)}, u32[]{:S(2)}, u32[]{:S(2)}) collective-permute-start(bf16[5,1,256,128]{3,2,1,0:T(8,128)(2,1)S(1)} %get-tuple-element.35), channel_id=1, source_target_pairs={{0,1},{1,2},{2,3},{3,4},{4,5},{5,6},{6,7},{8,9},{9,10},{10,11},{11... | collective-permute-start | bytes 983048 | tf_op jit(solution)/shard_map/ppermute | solution.py:23
  42.8 12.2 %copy-start.19 = (bf16[256,128]{1,0:T(8,128)(2,1)S(1)}, bf16[256,128]{1,0:T(8,128)(2,1)}, u32[]{:S(2)}) copy-start(bf16[256,128]{1,0:T(8,128)(2,1)} %param.26) | copy-start | bytes 196612
  55.4 0.7 copy-start.39
  55.8 2.1 copy-start.5
  56.1 24.6 %copy-start.4 = (f32[1024,128]{1,0:T(8,128)S(1)}, f32[1024,128]{1,0:T(8,128)}, u32[]{:S(2)}) copy-start(f32[1024,128]{1,0:T(8,128)} %fusion.64) | copy-start | bytes 1572868
  80.7 13.9 %copy-start.35 = (s32[1,8,256]{2,1,0:T(8,128)S(1)}, s32[1,8,256]{2,1,0:T(8,128)}, u32[]{:S(2)}) copy-start(s32[1,8,256]{2,1,0:T(8,128)} %param.20) | copy-start | bytes 24580
  81.0 1.2 copy-start.15
  81.0 16.7 %copy-start.30 = (bf16[128,128]{1,0:T(8,128)(2,1)S(1)}, bf16[128,128]{1,0:T(8,128)(2,1)}, u32[]{:S(2)}) copy-start(bf16[128,128]{1,0:T(8,128)(2,1)} %param.30) | copy-start | bytes 98308
  81.0 16.8 %copy-start.36 = (bf16[128,128]{1,0:T(8,128)(2,1)S(1)}, bf16[128,128]{1,0:T(8,128)(2,1)}, u32[]{:S(2)}) copy-start(bf16[128,128]{1,0:T(8,128)(2,1)} %param.33) | copy-start | bytes 98308
  82.2 27.3 %copy-start.27 = (bf16[1024,128]{1,0:T(8,128)(2,1)}, bf16[1024,128]{1,0:T(8,128)(2,1)S(1)}, u32[]{:S(2)}) copy-start(bf16[1024,128]{1,0:T(8,128)(2,1)S(1)} %fusion.8) | copy-start | bytes 786436
  88.3 6.9 %collective-permute-start.4 = (bf16[1,32,128]{2,1,0:T(8,128)(2,1)S(1)}, bf16[1,32,128]{2,1,0:T(8,128)(2,1)S(1)}, u32[]{:S(2)}, u32[]{:S(2)}) collective-permute-start(bf16[1,32,128]{2,1,0:T(8,128)(2,1)S(1)} %get-tuple-element.55), channel_id=1, source_target_pairs={{0,1},{1,2},{2,3},{3,4},{4,5},{5,6},{6,7},{8,9},{9,10},{10,11},{11... | collective-permute-start | bytes 24584 | tf_op jit(solution)/shard_map/ppermute | solution.py:23
  92.7 5.0 %collective-permute-start.5 = (bf16[1,32,128]{2,1,0:T(8,128)(2,1)S(1)}, bf16[1,32,128]{2,1,0:T(8,128)(2,1)S(1)}, u32[]{:S(2)}, u32[]{:S(2)}) collective-permute-start(bf16[1,32,128]{2,1,0:T(8,128)(2,1)S(1)} %get-tuple-element.56), channel_id=1, source_target_pairs={{1,0},{2,1},{3,2},{4,3},{5,4},{6,5},{7,6},{9,8},{10,9},{11,10},{12... | collective-permute-start | bytes 24584 | tf_op jit(solution)/shard_map/ppermute | solution.py:24
  97.8 16.5 %copy-start.33 = (f32[128,128]{1,0:T(8,128)}, f32[128,128]{1,0:T(8,128)S(1)}, u32[]{:S(2)}) copy-start(f32[128,128]{1,0:T(8,128)S(1)} %fusion.74) | copy-start | bytes 196612
  98.9 7.4 %collective-permute-start.6 = (bf16[32,128]{1,0:T(8,128)(2,1)S(1)}, bf16[32,128]{1,0:T(8,128)(2,1)S(1)}, u32[]{:S(2)}, u32[]{:S(2)}) collective-permute-start(bf16[32,128]{1,0:T(8,128)(2,1)S(1)} %get-tuple-element.57), channel_id=1, source_target_pairs={{0,1},{1,2},{2,3},{3,4},{4,5},{5,6},{6,7},{8,9},{9,10},{10,11},{11... | collective-permute-start | bytes 24584 | tf_op jit(solution)/shard_map/ppermute | solution.py:23
  103.3 6.2 %collective-permute-start.7 = (bf16[32,128]{1,0:T(8,128)(2,1)S(1)}, bf16[32,128]{1,0:T(8,128)(2,1)S(1)}, u32[]{:S(2)}, u32[]{:S(2)}) collective-permute-start(bf16[32,128]{1,0:T(8,128)(2,1)S(1)} %get-tuple-element.58), channel_id=1, source_target_pairs={{1,0},{2,1},{3,2},{4,3},{5,4},{6,5},{7,6},{9,8},{10,9},{11,10},{12... | collective-permute-start | bytes 24584 | tf_op jit(solution)/shard_map/ppermute | solution.py:24
  112.7 2.5 copy-start.8
  112.7 3.4 %copy-start.23 = (bf16[256,128]{1,0:T(8,128)(2,1)S(1)}, bf16[256,128]{1,0:T(8,128)(2,1)}, u32[]{:S(2)}) copy-start(bf16[256,128]{1,0:T(8,128)(2,1)} %param.28) | copy-start | bytes 196612
  114.3 1.8 copy-start.2
  134.2 1.0 copy-start.20
  135.1 2.5 copy-start.6
  135.2 2.6 copy-start.7
  135.2 2.6 copy-start.41
  137.8 1.8 copy-start.28
  137.8 1.8 copy-start.29
  137.8 2.5 copy-start.9
  137.8 2.5 copy-start.16
  137.8 2.5 copy-start.25
  165.1 7.3 %copy-start.34 = (f32[128,128]{1,0:T(8,128)S(1)}, f32[128,128]{1,0:T(8,128)}, u32[]{:S(2)}) copy-start(f32[128,128]{1,0:T(8,128)} %copy-done.33) | copy-start | bytes 196612
  165.1 7.3 %copy-start.37 = (bf16[128,128]{1,0:T(8,128)(2,1)S(1)}, bf16[128,128]{1,0:T(8,128)(2,1)}, u32[]{:S(2)}) copy-start(bf16[128,128]{1,0:T(8,128)(2,1)} %param.33) | copy-start | bytes 98308
  165.9 8.5 %copy-start.11 = (bf16[1,256,128]{2,1,0:T(8,128)(2,1)}, bf16[1,256,128]{2,1,0:T(8,128)(2,1)S(1)}, u32[]{:S(2)}) copy-start(bf16[1,256,128]{2,1,0:T(8,128)(2,1)S(1)} %get-tuple-element.43) | copy-start | bytes 196612
  165.9 8.5 %copy-start.13 = (bf16[1,256,128]{2,1,0:T(8,128)(2,1)}, bf16[1,256,128]{2,1,0:T(8,128)(2,1)S(1)}, u32[]{:S(2)}) copy-start(bf16[1,256,128]{2,1,0:T(8,128)(2,1)S(1)} %get-tuple-element.44) | copy-start | bytes 196612
  166.6 18.8 %collective-permute-start.8 = (bf16[1,3,256,128]{3,2,1,0:T(8,128)(2,1)}, bf16[1,3,256,128]{3,2,1,0:T(8,128)(2,1)}, u32[]{:S(2)}, u32[]{:S(2)}) collective-permute-start(bf16[1,3,256,128]{3,2,1,0:T(8,128)(2,1)} %maximum_bitcast_fusion.1), channel_id=1, source_target_pairs={{0,8},{8,16},{16,24},{24,32},{32,40},{40,48},{48,56},{56,64},{64,7... | collective-permute-start | bytes 589832 | tf_op jit(solution)/shard_map/ppermute | solution.py:23
  173.2 14.1 %copy-start.44 = (bf16[3]{0:T(256)(128)(2,1)S(1)}, bf16[3]{0:T(256)(128)(2,1)}, u32[]{:S(2)}) copy-start(bf16[3]{0:T(256)(128)(2,1)} %copy-done.43) | copy-start | bytes 22
  175.5 12.9 %copy-start.12 = (bf16[1,256,128]{2,1,0:T(8,128)(2,1)S(1)}, bf16[1,256,128]{2,1,0:T(8,128)(2,1)}, u32[]{:S(2)}) copy-start(bf16[1,256,128]{2,1,0:T(8,128)(2,1)} %copy-done.11) | copy-start | bytes 196612
  175.5 12.9 %copy-start.14 = (bf16[1,256,128]{2,1,0:T(8,128)(2,1)S(1)}, bf16[1,256,128]{2,1,0:T(8,128)(2,1)}, u32[]{:S(2)}) copy-start(bf16[1,256,128]{2,1,0:T(8,128)(2,1)} %copy-done.13) | copy-start | bytes 196612
  175.5 20.4 %copy-start.3 = (bf16[1024,128]{1,0:T(8,128)(2,1)S(1)}, bf16[1024,128]{1,0:T(8,128)(2,1)}, u32[]{:S(2)}) copy-start(bf16[1024,128]{1,0:T(8,128)(2,1)} %copy-done.2) | copy-start | bytes 786436
  175.5 47.5 %all-to-all-start = ((f32[16,16,512]{2,1,0:T(8,128)}), f32[16,16,512]{2,1,0:T(8,128)}, u32[]{:S(2)}, u32[]{:S(2)}) async-start(f32[16,16,512]{2,1,0:T(8,128)} %copy.31), calls=%async_computation | async-start | bytes 1048576 | tf_op jit(solution)/shard_map/all_to_all | solution.py:61
  182.4 13.5 %copy-start.10 = (bf16[1024,128]{1,0:T(8,128)(2,1)S(1)}, bf16[1024,128]{1,0:T(8,128)(2,1)}, u32[]{:S(2)}) copy-start(bf16[1024,128]{1,0:T(8,128)(2,1)} %copy-done.8) | copy-start | bytes 786436
  182.4 13.5 %copy-start.24 = (bf16[256,128]{1,0:T(8,128)(2,1)S(1)}, bf16[256,128]{1,0:T(8,128)(2,1)}, u32[]{:S(2)}) copy-start(bf16[256,128]{1,0:T(8,128)(2,1)} %param.28) | copy-start | bytes 196612
  182.4 13.5 %copy-start.26 = (bf16[1024,128]{1,0:T(8,128)(2,1)S(1)}, bf16[1024,128]{1,0:T(8,128)(2,1)}, u32[]{:S(2)}) copy-start(bf16[1024,128]{1,0:T(8,128)(2,1)} %param.32) | copy-start | bytes 786436
  183.4 7.4 %collective-permute-start.9 = (bf16[1,3,256,128]{3,2,1,0:T(8,128)(2,1)S(1)}, bf16[1,3,256,128]{3,2,1,0:T(8,128)(2,1)S(1)}, u32[]{:S(2)}, u32[]{:S(2)}) collective-permute-start(bf16[1,3,256,128]{3,2,1,0:T(8,128)(2,1)S(1)} %maximum_bitcast_fusion.2), channel_id=1, source_target_pairs={{8,0},{16,8},{24,16},{32,24},{40,32},{48,40},{56,48},{64,56},{72,6... | collective-permute-start | bytes 589832 | tf_op jit(solution)/shard_map/ppermute | solution.py:24
  187.4 8.7 %copy-start.21 = (bf16[256,128]{1,0:T(8,128)(2,1)S(1)}, bf16[256,128]{1,0:T(8,128)(2,1)}, u32[]{:S(2)}) copy-start(bf16[256,128]{1,0:T(8,128)(2,1)} %param.26) | copy-start | bytes 196612
  190.8 0.9 copy-start.17
  191.7 6.2 %copy-start.32 = (s32[1,4096]{1,0:T(1,128)S(1)}, s32[1,4096]{1,0:T(1,128)}, u32[]{:S(2)}) copy-start(s32[1,4096]{1,0:T(1,128)} %param.23) | copy-start | bytes 49156
  191.7 30.4 %collective-permute-start.10 = (bf16[5,1,256,128]{3,2,1,0:T(8,128)(2,1)}, bf16[5,1,256,128]{3,2,1,0:T(8,128)(2,1)}, u32[]{:S(2)}, u32[]{:S(2)}) collective-permute-start(bf16[5,1,256,128]{3,2,1,0:T(8,128)(2,1)} %get-tuple-element.34), channel_id=1, source_target_pairs={{0,1},{1,2},{2,3},{3,4},{4,5},{5,6},{6,7},{8,9},{9,10},{10,11},{11... | collective-permute-start | bytes 983048 | tf_op jit(solution)/shard_map/ppermute | solution.py:23
  197.9 22.9 %copy-start.18 = (bf16[5,1,256,128]{3,2,1,0:T(8,128)(2,1)S(1)}, bf16[5,1,256,128]{3,2,1,0:T(8,128)(2,1)}, u32[]{:S(2)}) copy-start(bf16[5,1,256,128]{3,2,1,0:T(8,128)(2,1)} %get-tuple-element.33) | copy-start | bytes 983044
  220.8 40.8 %copy-start.40 = (pred[2048]{0:T(1024)(128)(4,1)S(1)}, pred[2048]{0:T(1024)(128)(4,1)}, u32[]{:S(2)}) copy-start(pred[2048]{0:T(1024)(128)(4,1)} %lt.95) | copy-start | bytes 6148
  220.8 22.4 %collective-permute-start.11 = (bf16[5,1,256,128]{3,2,1,0:T(8,128)(2,1)S(1)}, bf16[5,1,256,128]{3,2,1,0:T(8,128)(2,1)S(1)}, u32[]{:S(2)}, u32[]{:S(2)}) collective-permute-start(bf16[5,1,256,128]{3,2,1,0:T(8,128)(2,1)S(1)} %copy-done.18), channel_id=1, source_target_pairs={{1,0},{2,1},{3,2},{4,3},{5,4},{6,5},{7,6},{9,8},{10,9},{11,10},{12... | collective-permute-start | bytes 983048 | tf_op jit(solution)/shard_map/ppermute | solution.py:24
  224.7 14.3 %all-to-all-start.1 = ((f32[16,1,512]{2,1,0:T(1,128)}), f32[16,1,512]{2,1,0:T(1,128)S(1)}, u32[]{:S(2)}, u32[]{:S(2)}) async-start(f32[16,1,512]{2,1,0:T(1,128)} %all_to_all.17), calls=%async_computation.1 | async-start | bytes 65536 | tf_op jit(solution)/shard_map/all_to_all | solution.py:68
  239.7 9.9 %all-to-all-start.2 = ((f32[16,1,512]{2,1,0:T(1,128)}), f32[16,1,512]{2,1,0:T(1,128)S(1)}, u32[]{:S(2)}, u32[]{:S(2)}) async-start(f32[16,1,512]{2,1,0:T(1,128)} %broadcast_in_dim.60), calls=%async_computation.2 | async-start | bytes 65536 | tf_op jit(solution)/shard_map/all_to_all | solution.py:38
  250.4 24.9 %all-to-all-start.3 = ((f32[16,16,512]{2,1,0:T(8,128)}), f32[16,16,512]{2,1,0:T(8,128)S(1)}, u32[]{:S(2)}, u32[]{:S(2)}) async-start(f32[16,16,512]{2,1,0:T(8,128)} %broadcast_in_dim.62), calls=%async_computation.3 | async-start | bytes 1048576 | tf_op jit(solution)/shard_map/all_to_all | solution.py:38
where the time goes:
time: 281 us; the launch traced here: 280 us
  other arithmetic  97.4 us (35%)
  local copies, waits for them, and re-layouts  66.6 us (24%)
  starting transfers between devices  63.9 us (23%)
  waiting for transfers between devices  26.1 us (9%)
  matrix products  23.3 us (8%)
    ppermute x6, starting transfers between devices, with_halo(): before = lax.ppermute(last, axis, up)  24.6 us
    dot_general x24, matrix products, matmul(): return jnp.dot(left, right, preferred_element_type=jnp.float32)  23.3 us
    scatter-add x1, other arithmetic, fine_backward(): jax.ops.segment_sum(d_senders, send_index, num_segments=lookup_rows)  23 us
    scatter-add x1, other arithmetic, fine_backward(): jax.ops.segment_sum(d_receivers, recv_index, num_segments=rows_here)  22.9 us
    scatter-add x1, other arithmetic, fine_forward(): jax.ops.segment_sum(message.astype(jnp.float32), recv_index, num_segments...  22.8 us
    gather x1, local copies, waits for them, and re-layouts, fine_backward(): d_message = d_summed[recv_index] * edge_live[:, None].astype(d_summed.dtype)  14.9 us
    scatter-add x1, other arithmetic, body(): jax.ops.segment_sum(returned.reshape(peer_count * slot_count, latent), gh...  12.9 us
    ppermute x6, starting transfers between devices, with_halo(): after = lax.ppermute(initial, axis, down)  12.6 us
  transfers between devices with their start and end apart: 16, of which 7 were waited for; matrix products, arithmetic and copies ran while one was open for 25% of the time, Pallas kernels for 0%

commit v1 on v0

v1 whole, which is shorter than its diff:
```python
import jax
import jax.numpy as jnp
from jax import lax
from jax.experimental import pallas as pl
from jax.experimental.pallas import tpu as pltpu
from jax.sharding import Mesh
from jax.sharding import PartitionSpec as P

BAND = 32
LAT = 128
LOW = 512
BITS = 9
STEP = 512
GX_GY = ("gx_0", "gx_1", "gx_2", "gy")
GX = ("gx_0", "gx_1", "gx_2")
MIB = 1024 * 1024

f32 = jnp.float32
bf16 = jnp.bfloat16


def mm(left, right):
    return jnp.dot(left, right, preferred_element_type=f32)


def mm_nt(left, right):
    return lax.dot_general(left, right, (((1,), (1,)), ((), ())), preferred_element_type=f32)


def mm_tn(left, right):
    return lax.dot_general(left, right, (((0,), (0,)), ((), ())), preferred_element_type=f32)


def wide(table):
    groups = table.shape[0] // LOW
    return jnp.concatenate([table[i * LOW : (i + 1) * LOW] for i in range(groups)], axis=1)


def tall(table):
    groups = table.shape[1] // LAT
    return jnp.concatenate([table[:, i * LAT : (i + 1) * LAT] for i in range(groups)], axis=0)


def in_columns(row):
    parts = []
    for j in range(row.shape[1] // LAT):
        parts.append(jnp.broadcast_to(row[:, j * LAT : (j + 1) * LAT], (LAT, LAT)).T)
    return jnp.concatenate(parts, axis=0)


def one_hot(col, rows):
    lanes = lax.broadcasted_iota(jnp.int32, col.shape, 1)
    return jnp.concatenate(
        [(col == lanes + j * LAT).astype(f32).astype(bf16) for j in range(rows // LAT)], axis=1
    )


def one_hot_t(row, rows):
    ids = lax.broadcasted_iota(jnp.int32, (rows, row.shape[1]), 0)
    return (ids == row).astype(f32).astype(bf16)


def take(col, table):
    got = mm(one_hot(col & (LOW - 1), LOW), table)
    group = col >> BITS
    total = jnp.zeros((col.shape[0], LAT), f32)
    for i in range(table.shape[1] // LAT):
        total = jnp.where(group == i, got[:, i * LAT : (i + 1) * LAT], total)
    return total


def put(row, col, values, groups):
    group = col >> BITS
    spread = jnp.concatenate(
        [jnp.where(group == i, values, 0.0).astype(bf16) for i in range(groups)], axis=1
    )
    return mm(one_hot_t(row & (LOW - 1), LOW), spread)


def sigmoid(v):
    return 1.0 / (1.0 + jnp.exp(-v))


def act_and_slope(v):
    s = sigmoid(v)
    return v * s, s * (1.0 + v * (1.0 - s))


def live_row(row, first, count):
    ids = lax.broadcasted_iota(jnp.int32, row.shape, 1) + first
    return jnp.where(ids < count, row, -1)


def pick_kernel(count_ref, rows_ref, nodes_ref, up_ref, down_ref, mid_ref):
    table = wide(nodes_ref[...])
    slots = rows_ref.shape[2]
    for k in range(8):
        row = live_row(rows_ref[0, k : k + 1, :], 0, count_ref[0, k])
        got = take(in_columns(row), table).astype(bf16)
        if k < 3:
            down_ref[k * slots : (k + 1) * slots, :] = got
        elif k < 5:
            mid_ref[(k - 3) * slots : (k - 2) * slots, :] = got
        else:
            up_ref[(k - 5) * slots : (k - 4) * slots, :] = got


def own_kernel(count_ref, send_ref, recv_ref, nodes_ref, sown_ref, recvs_ref, table):
    step = pl.program_id(0)

    @pl.when(step == 0)
    def _():
        table[...] = wide(nodes_ref[...])

    first = step * STEP
    count = count_ref[0]
    sown_ref[...] = take(in_columns(live_row(send_ref[...], first, count)), table[...]).astype(bf16)
    recvs_ref[...] = take(in_columns(live_row(recv_ref[...], first, count)), table[...]).astype(bf16)


def forward_kernel(
    count_ref,
    send_ref,
    recv_ref,
    sown_ref,
    recvs_ref,
    up_ref,
    down_ref,
    yup_ref,
    ydown_ref,
    nodes_ref,
    pool_ref,
    wei_ref,
    weo_ref,
    wni_ref,
    wno_ref,
    senders_ref,
    act_ref,
    slope_ref,
    fine_ref,
    summed_ref,
    nact_ref,
    nslope_ref,
    window_ref,
    wlow_ref,
    whigh_ref,
    table,
    acc,
):
    step = pl.program_id(0)
    slots = up_ref.shape[0] // 3

    @pl.when(step == 0)
    def _():
        def block(ref, i):
            return ref[i * slots : (i + 1) * slots, :]

        blocks = (
            block(ydown_ref, 2),
            block(down_ref, 1),
            block(yup_ref, 2),
            block(ydown_ref, 1),
            block(yup_ref, 1),
            block(ydown_ref, 0),
            block(up_ref, 1),
            block(yup_ref, 0),
        )
        for k in range(8):
            table[(k % 2) * slots : (k % 2 + 1) * slots, (k // 2) * LAT : (k // 2 + 1) * LAT] = blocks[k]
        acc[...] = jnp.zeros_like(acc)

    first = step * STEP
    count = count_ref[0]
    owned = nodes_ref.shape[0]
    send = in_columns(live_row(send_ref[...], first, count)) - owned
    senders = (take(send, table[...]) + sown_ref[...].astype(f32)).astype(bf16)
    senders_ref[...] = senders
    pre = mm(jnp.concatenate([senders, recvs_ref[...]], axis=1), wei_ref[...])
    act, slope = act_and_slope(pre)
    act = act.astype(bf16)
    act_ref[...] = act
    slope_ref[...] = slope.astype(bf16)
    message = mm(act, weo_ref[...]).astype(bf16).astype(f32)
    recv = live_row(recv_ref[...], first, count)
    acc[...] += put(recv, in_columns(recv), message, owned // LOW)

    @pl.when(step == pl.num_programs(0) - 1)
    def _():
        summed = tall(acc[...]).astype(bf16)
        summed_ref[...] = summed
        nodes = nodes_ref[...]
        pre = mm(jnp.concatenate([nodes, summed], axis=1), wni_ref[...])
        act, slope = act_and_slope(pre)
        act = act.astype(bf16)
        nact_ref[...] = act
        nslope_ref[...] = slope.astype(bf16)
        fine = (nodes.astype(f32) + mm(act, wno_ref[...])).astype(bf16)
        fine_ref[...] = fine
        rows = window_ref.shape[0]
        window = mm(one_hot_t(pool_ref[...], rows), fine)
        window_ref[...] = window
        wlow_ref[...] = window[: 2 * BAND].astype(bf16)
        whigh_ref[...] = window[rows - 2 * BAND :].astype(bf16)


def backward_kernel(
    send_ref,
    recv_ref,
    count_ref,
    senders_ref,
    recvs_ref,
    act_ref,
    slope_ref,
    window_ref,
    nlow_ref,
    nhigh_ref,
    dcl_ref,
    dch_ref,
    dcoarse_ref,
    dfine_ref,
    pool_ref,
    nodes_ref,
    summed_ref,
    nact_ref,
    nslope_ref,
    wei_ref,
    weo_ref,
    wni_ref,
    wno_ref,
    wci_ref,
    wco_ref,
    coarse_ref,
    dnode_ref,
    dedge_ref,
    rdown_ref,
    rup_ref,
    rown_ref,
    grads_ref,
    table,
    acc,
    gacc,
):
    step = pl.program_id(0)
    owned = nodes_ref.shape[0]

    @pl.when(step == 0)
    def _():
        acc[...] = jnp.zeros_like(acc)
        gacc[...] = jnp.zeros_like(gacc)
        window = window_ref[...]
        rows = window.shape[0]
        total = jnp.concatenate(
            [
                window[: 2 * BAND] + nlow_ref[...].astype(f32),
                window[2 * BAND : rows - 2 * BAND],
                window[rows - 2 * BAND :] + nhigh_ref[...].astype(f32),
            ],
            axis=0,
        )
        coarse_in = (0.125 * total).astype(bf16)
        d_coarse = jnp.concatenate([dcl_ref[...], dcoarse_ref[...], dch_ref[...]], axis=0)
        act, slope = act_and_slope(mm(coarse_in, wci_ref[...]))
        act = act.astype(bf16)
        coarse_out = (coarse_in.astype(f32) + mm(act, wco_ref[...])).astype(bf16)
        coarse_ref[...] = coarse_out[BAND : rows - BAND]
        d_pre = (mm_nt(d_coarse, wco_ref[...]) * slope).astype(bf16)
        d_in = (d_coarse.astype(f32) + mm_nt(d_pre, wci_ref[...])).astype(bf16)
        inner = slice(BAND, rows - BAND)
        g_ci = mm_tn(coarse_in[inner], d_pre[inner])
        g_co = mm_tn(act[inner], d_coarse[inner])
        reach = jnp.concatenate([d_in, jnp.zeros((2 * LAT - rows, LAT), bf16)], axis=0)
        parent = mm(one_hot(in_columns(pool_ref[...]), 2 * LAT), reach)
        d_total = dfine_ref[...].astype(f32) + 0.125 * parent
        d_out = d_total.astype(bf16)
        d_node = (mm_nt(d_out, wno_ref[...]) * nslope_ref[...].astype(f32)).astype(bf16)
        back = mm_nt(d_node, wni_ref[...])
        dnode_ref[...] = d_total + back[:, :LAT]
        table[...] = wide(back[:, LAT:].astype(bf16))
        g_ni = mm_tn(jnp.concatenate([nodes_ref[...], summed_ref[...]], axis=1), d_node)
        g_no = mm_tn(nact_ref[...], d_out)
        grads_ref[3 * LAT : 5 * LAT, :] = g_ni.astype(bf16)
        grads_ref[5 * LAT : 6 * LAT, :] = g_no.astype(bf16)
        grads_ref[6 * LAT : 7 * LAT, :] = g_ci.astype(bf16)
        grads_ref[7 * LAT :, :] = g_co.astype(bf16)

    first = step * STEP
    count = count_ref[0]
    recv = in_columns(live_row(recv_ref[...], first, count))
    d_message = take(recv, table[...]).astype(bf16)
    d_pre = (mm_nt(d_message, weo_ref[...]) * slope_ref[...].astype(f32)).astype(bf16)
    dedge_ref[...] = d_pre
    gacc[: 2 * LAT, :] += mm_tn(jnp.concatenate([senders_ref[...], recvs_ref[...]], axis=1), d_pre)
    gacc[2 * LAT :, :] += mm_tn(act_ref[...], d_message)
    send = live_row(send_ref[...], first, count) - owned
    acc[...] += put(send, in_columns(send), d_pre.astype(f32), 4)

    @pl.when(step == pl.num_programs(0) - 1)
    def _():
        grads_ref[: 3 * LAT, :] = gacc[...].astype(bf16)
        ghosts = mm_nt(tall(acc[...]).astype(bf16), wei_ref[:LAT, :]).astype(bf16)
        slots = ghosts.shape[0] // 8
        for place, (ref, i) in enumerate(
            (
                (rup_ref, 2),
                (rown_ref, 0),
                (rdown_ref, 2),
                (rup_ref, 1),
                (rdown_ref, 1),
                (rup_ref, 0),
                (rown_ref, 1),
                (rdown_ref, 0),
            )
        ):
            ref[i * slots : (i + 1) * slots, :] = ghosts[place * slots : (place + 1) * slots]


def local_kernel(count_ref, send_ref, recv_ref, dedge_ref, dnode_ref, wei_ref, out_ref, acc_s, acc_r):
    step = pl.program_id(0)

    @pl.when(step == 0)
    def _():
        acc_s[...] = jnp.zeros_like(acc_s)
        acc_r[...] = jnp.zeros_like(acc_r)

    first = step * STEP
    count = count_ref[0]
    groups = out_ref.shape[0] // LOW
    d_pre = dedge_ref[...].astype(f32)
    send = live_row(send_ref[...], first, count)
    recv = live_row(recv_ref[...], first, count)
    acc_s[...] += put(send, in_columns(send), d_pre, groups)
    acc_r[...] += put(recv, in_columns(recv), d_pre, groups)

    @pl.when(step == pl.num_programs(0) - 1)
    def _():
        out_ref[...] = (
            dnode_ref[...]
            + mm_nt(tall(acc_s[...]).astype(bf16), wei_ref[:LAT, :])
            + mm_nt(tall(acc_r[...]).astype(bf16), wei_ref[LAT:, :])
        )


def return_kernel(count_ref, rows_ref, down_ref, up_ref, mid_low_ref, mid_high_ref, part_ref, out_ref):
    slots = rows_ref.shape[2]
    groups = out_ref.shape[0] // LOW
    total = jnp.zeros((LOW, groups * LAT), f32)
    for k in range(8):
        row = live_row(rows_ref[0, k : k + 1, :], 0, count_ref[0, k])
        if k < 3:
            got = down_ref[k * slots : (k + 1) * slots, :]
        elif k == 3:
            got = mid_low_ref[slots : 2 * slots, :]
        elif k == 4:
            got = mid_high_ref[slots : 2 * slots, :]
        else:
            got = up_ref[(k - 5) * slots : (k - 4) * slots, :]
        total = total + put(row, in_columns(row), got.astype(f32), groups)
    out_ref[...] = part_ref[...] + tall(total)


def scale_kernel(scale, sums_ref, *out_refs):
    first = 0
    for ref in out_refs:
        rows = ref.shape[0]
        ref[...] = sums_ref[first : first + rows, :].astype(f32) * scale
        first += rows


def whole(shape):
    return pl.BlockSpec(shape, lambda *_: (0,) * len(shape))


def scalars():
    return pl.BlockSpec(memory_space=pltpu.SMEM)


def edge_row():
    return pl.BlockSpec((1, STEP), lambda i: (0, i))


def edge_block():
    return pl.BlockSpec((STEP, LAT), lambda i: (i, 0))


def shape(dims, dtype):
    return jax.ShapeDtypeStruct(dims, dtype)


def params(mib):
    return pltpu.CompilerParams(vmem_limit_bytes=mib * MIB)


def cost(flops, moved):
    return pl.CostEstimate(flops=flops, bytes_accessed=moved, transcendentals=0)


def reduced(grads):
    rows = grads.shape[0]
    far, near = GX, ("gy",)
    n_far, n_near = 32, 8
    part = rows // n_far
    got = lax.all_to_all(grads.reshape(n_far, part, LAT), far, 0, 0, tiled=True)
    own = got.astype(f32).sum(axis=0).astype(bf16)
    got = lax.all_to_all(jnp.broadcast_to(own[None], (n_near, part, LAT)), near, 0, 0, tiled=True)
    own = got.astype(f32).sum(axis=0).astype(bf16)
    got = lax.all_to_all(jnp.broadcast_to(own[None], (n_far, part, LAT)), far, 0, 0, tiled=True)
    return got.reshape(rows, LAT)


def body(
    nodes,
    ghost_rows,
    ghost_count,
    edge_send,
    edge_recv,
    edge_count,
    pool_map,
    w_edge_in,
    w_edge_out,
    w_node_in,
    w_node_out,
    w_coarse_in,
    w_coarse_out,
    d_fine,
    d_coarse,
):
    owned = nodes.shape[0]
    edges = edge_send.shape[1]
    slots = ghost_rows.shape[2]
    coarse = d_coarse.shape[0]
    window_rows = coarse + 2 * BAND
    steps = edges // STEP
    n_gx, n_gy = lax.axis_size(GX), lax.axis_size("gy")
    x_up = [(i, i + 1) for i in range(n_gx - 1)]
    x_down = [(j, i) for i, j in x_up]
    y_up = [(i, i + 1) for i in range(n_gy - 1)]
    y_down = [(j, i) for i, j in y_up]

    out_up, out_down, out_mid = pl.pallas_call(
        pick_kernel,
        out_shape=(
            shape((3 * slots, LAT), bf16),
            shape((3 * slots, LAT), bf16),
            shape((2 * slots, LAT), bf16),
        ),
        in_specs=[scalars(), whole(ghost_rows.shape), whole(nodes.shape)],
        out_specs=(whole((3 * slots, LAT)), whole((3 * slots, LAT)), whole((2 * slots, LAT))),
        grid=(1,),
        compiler_params=params(32),
        cost_estimate=cost(2 * 2048 * 512 * 256, MIB),
        name="pick",
    )(ghost_count, ghost_rows, nodes)

    up = lax.ppermute(out_up, GX, x_up)
    down = lax.ppermute(out_down, GX, x_down)

    sown, recvs = pl.pallas_call(
        own_kernel,
        grid=(steps,),
        out_shape=(shape((edges, LAT), bf16), shape((edges, LAT), bf16)),
        in_specs=[scalars(), edge_row(), edge_row(), whole(nodes.shape)],
        out_specs=(edge_block(), edge_block()),
        scratch_shapes=[pltpu.VMEM((LOW, owned // LOW * LAT), bf16)],
        compiler_params=params(32),
        cost_estimate=cost(2 * 2 * 4096 * 512 * 256, 3 * MIB),
        name="own_rows",
    )(edge_count, edge_send, edge_recv, nodes)

    yup = lax.ppermute(
        jnp.concatenate(
            [up[2 * slots :], out_mid[slots:], down[2 * slots :], d_coarse[coarse - BAND :]]
        ),
        "gy",
        y_up,
    )
    ydown = lax.ppermute(
        jnp.concatenate([up[:slots], out_mid[:slots], down[:slots], d_coarse[:BAND]]), "gy", y_down
    )

    edge16 = shape((edges, LAT), bf16)
    node16 = shape((owned, LAT), bf16)
    (
        senders,
        act,
        slope,
        fine_out,
        summed,
        nact,
        nslope,
        window,
        wlow,
        whigh,
    ) = pl.pallas_call(
        forward_kernel,
        grid=(steps,),
        out_shape=(
            edge16,
            edge16,
            edge16,
            node16,
            node16,
            node16,
            node16,
            shape((window_rows, LAT), f32),
            shape((2 * BAND, LAT), bf16),
            shape((2 * BAND, LAT), bf16),
        ),
        in_specs=[
            scalars(),
            edge_row(),
            edge_row(),
            edge_block(),
            edge_block(),
            whole(up.shape),
            whole(down.shape),
            whole(yup.shape),
            whole(ydown.shape),
            whole(nodes.shape),
            whole(pool_map.shape),
            whole(w_edge_in.shape),
            whole(w_edge_out.shape),
            whole(w_node_in.shape),
            whole(w_node_out.shape),
        ],
        out_specs=(
            edge_block(),
            edge_block(),
            edge_block(),
            whole((owned, LAT)),
            whole((owned, LAT)),
            whole((owned, LAT)),
            whole((owned, LAT)),
            whole((window_rows, LAT)),
            whole((2 * BAND, LAT)),
            whole((2 * BAND, LAT)),
        ),
        scratch_shapes=[
            pltpu.VMEM((LOW, 4 * LAT), bf16),
            pltpu.VMEM((LOW, owned // LOW * LAT), f32),
        ],
        compiler_params=params(32),
        cost_estimate=cost(2 * 4096 * 512 * 1024, 8 * MIB),
        name="forward",
    )(
        edge_count,
        edge_send,
        edge_recv,
        sown,
        recvs,
        up,
        down,
        yup,
        ydown,
        nodes,
        pool_map,
        w_edge_in,
        w_edge_out,
        w_node_in,
        w_node_out,
    )

    nlow = lax.ppermute(whigh, "gy", y_up)
    nhigh = lax.ppermute(wlow, "gy", y_down)
    d_low = yup[3 * slots :]
    d_high = ydown[3 * slots :]

    (coarse_out, d_node, d_edge, r_down, r_up, r_own, grads) = pl.pallas_call(
        backward_kernel,
        grid=(steps,),
        out_shape=(
            shape((coarse, LAT), bf16),
            shape((owned, LAT), f32),
            edge16,
            shape((3 * slots, LAT), bf16),
            shape((3 * slots, LAT), bf16),
            shape((2 * slots, LAT), bf16),
            shape((8 * LAT, LAT), bf16),
        ),
        in_specs=[
            edge_row(),
            edge_row(),
            scalars(),
            edge_block(),
            edge_block(),
            edge_block(),
            edge_block(),
            whole(window.shape),
            whole(nlow.shape),
            whole(nhigh.shape),
            whole(d_low.shape),
            whole(d_high.shape),
            whole(d_coarse.shape),
            whole(d_fine.shape),
            whole(pool_map.shape),
            whole(nodes.shape),
            whole(summed.shape),
            whole(nact.shape),
            whole(nslope.shape),
            whole(w_edge_in.shape),
            whole(w_edge_out.shape),
            whole(w_node_in.shape),
            whole(w_node_out.shape),
            whole(w_coarse_in.shape),
            whole(w_coarse_out.shape),
        ],
        out_specs=(
            whole((coarse, LAT)),
            whole((owned, LAT)),
            edge_block(),
            whole((3 * slots, LAT)),
            whole((3 * slots, LAT)),
            whole((2 * slots, LAT)),
            whole((8 * LAT, LAT)),
        ),
        scratch_shapes=[
            pltpu.VMEM((LOW, owned // LOW * LAT), bf16),
            pltpu.VMEM((LOW, 4 * LAT), f32),
            pltpu.VMEM((3 * LAT, LAT), f32),
        ],
        compiler_params=params(32),
        cost_estimate=cost(2 * 4096 * 512 * 1024, 8 * MIB),
        name="backward",
    )(
        edge_send,
        edge_recv,
        edge_count,
        senders,
        recvs,
        act,
        slope,
        window,
        nlow,
        nhigh,
        d_low,
        d_high,
        d_coarse,
        d_fine,
        pool_map,
        nodes,
        summed,
        nact,
        nslope,
        w_edge_in,
        w_edge_out,
        w_node_in,
        w_node_out,
        w_coarse_in,
        w_coarse_out,
    )

    high = lax.ppermute(r_down, "gy", y_down)
    low = lax.ppermute(r_up, "gy", y_up)

    d_own = pl.pallas_call(
        local_kernel,
        grid=(steps,),
        out_shape=shape((owned, LAT), f32),
        in_specs=[
            scalars(),
            edge_row(),
            edge_row(),
            edge_block(),
            whole((owned, LAT)),
            whole(w_edge_in.shape),
        ],
        out_specs=whole((owned, LAT)),
        scratch_shapes=[pltpu.VMEM((LOW, owned // LOW * LAT), f32)] * 2,
        compiler_params=params(32),
        cost_estimate=cost(2 * 2 * 4096 * 512 * 256, 3 * MIB),
        name="local",
    )(edge_count, edge_send, edge_recv, d_edge, d_node, w_edge_in)

    ret_up = lax.ppermute(
        jnp.concatenate([low[:slots], r_own[slots:], high[:slots]]), GX, x_down
    )
    ret_down = lax.ppermute(
        jnp.concatenate([low[2 * slots :], r_own[:slots], high[2 * slots :]]), GX, x_up
    )

    grad_nodes = pl.pallas_call(
        return_kernel,
        grid=(1,),
        out_shape=shape((owned, LAT), f32),
        in_specs=[
            scalars(),
            whole(ghost_rows.shape),
            whole(ret_down.shape),
            whole(ret_up.shape),
            whole(low.shape),
            whole(high.shape),
            whole(d_own.shape),
        ],
        out_specs=whole((owned, LAT)),
        compiler_params=params(32),
        cost_estimate=cost(2 * 2048 * 512 * 256, 2 * MIB),
        name="returned",
    )(ghost_count, ghost_rows, ret_down, ret_up, low, high, d_own)

    sums = reduced(grads)
    grad_scale = 1.0 / (owned * n_gx * n_gy) ** 0.5
    heights = (2 * LAT, LAT, 2 * LAT, LAT, LAT, LAT)
    scaled = pl.pallas_call(
        lambda *refs: scale_kernel(grad_scale, *refs),
        out_shape=tuple(shape((h, LAT), f32) for h in heights),
        name="scaled",
    )(sums)
    return (fine_out, coarse_out, grad_nodes, *scaled)


def solution(mesh):
    torus = Mesh(mesh.devices.reshape(4, 4, 2, mesh.shape["gy"]), GX_GY)
    in_specs = (
        P(GX_GY, None),
        P(GX_GY, None, None),
        P(GX_GY, None),
        P(GX_GY, None),
        P(GX_GY, None),
        P(GX_GY),
        P(GX_GY, None),
        P(),
        P(),
        P(),
        P(),
        P(),
        P(),
        P(GX_GY, None),
        P(GX_GY, None),
    )
    out_specs = (P(GX_GY, None), P(GX_GY, None), P(GX_GY, None), P(), P(), P(), P(), P(), P())
    return jax.shard_map(body, mesh=torus, in_specs=in_specs, out_specs=out_specs, check_vma=False)
```

time: 281 us -> 120 us (0.43)
  other arithmetic: 97.4 us -> 0.13 us
  local copies, waits for them, and re-layouts: 66.6 us -> 5.27 us
  Pallas kernels: 0 us -> 37.9 us
  matrix products: 23.3 us -> 0 us
  starting transfers between devices: 63.9 us -> 53.7 us
  waiting for transfers between devices: 26.1 us -> 20 us
    scatter-add x7 -> x0, other arithmetic: 87.7 us -> none  [the longest x1 23 us: fine_backward(): jax.ops.segment_sum(d_senders, send_index, num_segments=lookup_rows)]
    gather x5 -> x0, local copies, waits for them, and re-layouts: 49 us -> none  [the longest x1 14.9 us: fine_backward(): d_message = d_summed[recv_index] * edge_live[:, None].astype(d_summed.dtype)]
    pallas_call x0 -> x7, Pallas kernels: none -> 37.9 us  [the longest x1 11.7 us: body(): pl.pallas_call(backward_kernel, grid=(steps,), out_shape=(shape((coarse,...]
    dot_general x24 -> x0, matrix products: 23.3 us -> none  [matmul(): return jnp.dot(left, right, preferred_element_type=jnp.float32)]
    all_to_all x4 -> x3, waiting for transfers between devices: 12 us -> 2.7 us  [the longest x1 2.7 us: reduced(): lax.all_to_all(jnp.broadcast_to(own[None], (n_near, part, LAT)), near, 0,...]
    ppermute x12 -> x10, starting transfers between devices: 37.1 us -> 29.9 us  [the longest x1 5.05 us: body(): low = lax.ppermute(r_up, 'gy', y_up)]
    unnamed x7 -> x0, other arithmetic: 4.14 us -> none
    mul x6 -> x0, local copies, waits for them, and re-layouts: 3.86 us -> none  [the longest x1 0.66 us: body(): totals[2] * grad_scale]
  transfers between devices with their start and end apart: 16 -> 13, of which waited for: 7 -> 7; matrix products, arithmetic and copies ran while one was open for 25% -> 1% of each run, Pallas kernels for 0% -> 10%
where the time goes in v1:
time: 120 us; the launch traced here: 119 us
  starting transfers between devices  53.7 us (45%)
  Pallas kernels  37.9 us (32%)
  waiting for transfers between devices  20 us (17%)
  local copies, waits for them, and re-layouts  5.27 us (4%)
  between operations  1.69 us (1%)
    pallas_call x1, Pallas kernels, body(): pl.pallas_call(backward_kernel, grid=(steps,), out_shape=(shape((coarse,...  11.7 us
    pallas_call x1, Pallas kernels, body(): pl.pallas_call(forward_kernel, grid=(steps,), out_shape=(edge16, edge16,...  11.6 us
    all_to_all x1, starting transfers between devices, reduced(): got = lax.all_to_all(grads.reshape(n_far, part, LAT), far, 0, 0, tiled=True)  9.73 us
    all_to_all x1, starting transfers between devices, reduced(): lax.all_to_all(jnp.broadcast_to(own[None], (n_far, part, LAT)), far, 0, 0...  9.5 us
    ppermute x1, starting transfers between devices, body(): low = lax.ppermute(r_up, 'gy', y_up)  5.05 us
    pallas_call x1, Pallas kernels, body(): pl.pallas_call(local_kernel, grid=(steps,), out_shape=shape((owned, LAT),...  4.93 us
    ppermute x1, starting transfers between devices, body(): up = lax.ppermute(out_up, GX, x_up)  4.6 us
    all_to_all x1, starting transfers between devices, reduced(): lax.all_to_all(jnp.broadcast_to(own[None], (n_near, part, LAT)), near, 0,...  4.58 us
  transfers between devices with their start and end apart: 13, of which 7 were waited for; matrix products, arithmetic and copies ran while one was open for 1% of the time, Pallas kernels for 10%

profile of v1, /device:TPU:1, one launch (start us, length us, event | category | flops | bytes accessed | tf_op | source)
XLA Modules:
  0.0 118.7 jit_solution(13857695270576478528)
XLA Ops:
  0.6 0.0 copy-start.1
  0.7 0.9 copy-done.1
  1.6 0.7 copy-done.12
  2.3 0.7 copy-done.15
  2.9 1.4 %pick.1 = (bf16[768,128]{1,0:T(8,128)(2,1)S(1)}, bf16[768,128]{1,0:T(8,128)(2,1)S(1)}, bf16[512,128]{1,0:T(8,128)(2,1)S(1)}) custom-call(s32[1,8]{1,0:T(1,128)S(1)} %copy-done.15, s32[1,8,256]{2,1,0:T(8,128)S(1)} %copy-done.12, bf16[1024,128]{1,0:T(8,128)(2,1)S(1)} %copy-done.1), custom_call_target="tpu_custom_call" | custom-call | flops 536870912 | bytes 1048576 | tf_op jit(solution)/shard_map/pick/pallas_call | solution.py:439
  4.4 4.6 %collective-permute-start = (bf16[768,128]{1,0:T(8,128)(2,1)S(1)}, bf16[768,128]{1,0:T(8,128)(2,1)S(1)}, u32[]{:S(2)}, u32[]{:S(2)}) collective-permute-start(bf16[768,128]{1,0:T(8,128)(2,1)S(1)} %get-tuple-element.39), channel_id=1, source_target_pairs={{0,8},{8,16},{16,24},{24,32},{32,40},{40,48},{48,56},{56,64},{64,7... | collective-permute-start | bytes 589832 | tf_op jit(solution)/shard_map/ppermute | solution.py:454
  9.0 1.9 %collective-permute-start.1 = (bf16[768,128]{1,0:T(8,128)(2,1)S(1)}, bf16[768,128]{1,0:T(8,128)(2,1)S(1)}, u32[]{:S(2)}, u32[]{:S(2)}) collective-permute-start(bf16[768,128]{1,0:T(8,128)(2,1)S(1)} %get-tuple-element.40), channel_id=1, source_target_pairs={{8,0},{16,8},{24,16},{32,24},{40,32},{48,40},{56,48},{64,56},{72,6... | collective-permute-start | bytes 589832 | tf_op jit(solution)/shard_map/ppermute | solution.py:455
  10.9 0.0 copy-start
  10.9 0.7 copy-done
  11.7 0.0 collective-permute-done.up_ref
  11.7 4.3 %collective-permute-done.1.down_ref = bf16[768,128]{1,0:T(8,128)(2,1)S(1)} collective-permute-done((bf16[768,128]{1,0:T(8,128)(2,1)S(1)}, bf16[768,128]{1,0:T(8,128)(2,1)S(1)}, u32[]{:S(2)}, u32[]{:S(2)}) %collective-permute-start.1) | collective-permute-done | bytes 196640 | tf_op jit(solution)/shard_map/ppermute | solution.py:455
  16.0 0.0 copy-start.2
  16.0 3.7 %collective-permute-start.2 = (bf16[800,128]{1,0:T(8,128)(2,1)S(1)}, bf16[800,128]{1,0:T(8,128)(2,1)S(1)}, u32[]{:S(2)}, u32[]{:S(2)}) collective-permute-start(bf16[800,128]{1,0:T(8,128)(2,1)S(1)} %pad_maximum_fusion), channel_id=1, source_target_pairs={{0,1},{1,2},{2,3},{3,4},{4,5},{5,6},{6,7},{8,9},{9,10},{10,11},{11... | collective-permute-start | bytes 614408 | tf_op jit(solution)/shard_map/ppermute | solution.py:469
  19.7 0.0 copy-start.10
  19.7 0.0 copy-start.11
  19.7 1.3 %collective-permute-start.3 = (bf16[800,128]{1,0:T(8,128)(2,1)S(1)}, bf16[800,128]{1,0:T(8,128)(2,1)S(1)}, u32[]{:S(2)}, u32[]{:S(2)}) collective-permute-start(bf16[800,128]{1,0:T(8,128)(2,1)S(1)} %pad_maximum_fusion.1), channel_id=1, source_target_pairs={{1,0},{2,1},{3,2},{4,3},{5,4},{6,5},{7,6},{9,8},{10,9},{11,10},{12... | collective-permute-start | bytes 614408 | tf_op jit(solution)/shard_map/ppermute | solution.py:476
  21.7 0.0 copy-done.2
  21.7 0.0 copy-done.10
  21.7 0.0 copy-done.11
  21.7 0.0 copy-start.4
  21.7 0.0 copy-start.5
  21.7 0.0 copy-start.6
  21.8 0.0 copy-start.7
  21.8 0.0 copy-start.14
  21.8 4.4 %own_rows.1 = (bf16[4096,128]{1,0:T(8,128)(2,1)S(1)}, bf16[4096,128]{1,0:T(8,128)(2,1)S(1)}) custom-call(s32[1]{0:T(128)S(6)} %copy.24.count_ref, s32[1,4096]{1,0:T(1,128)S(1)} %copy-done.10, s32[1,4096]{1,0:T(1,128)S(1)} %copy-done.11, bf16[1024,128]{1,0:T(8,128)(2,1)S(1)} %copy-done.2), custom_call_target="tpu_custom_call" | custom-call | flops 2147483648 | bytes 3145728 | tf_op jit(solution)/shard_map/own_rows/pallas_call | solution.py:457
  26.2 0.0 collective-permute-done.2.yup_ref
  26.2 0.2 collective-permute-done.3.ydown_ref
  26.4 0.0 copy-done.4
  26.4 0.0 copy-done.5
  26.4 0.0 copy-done.6
  26.4 0.0 copy-done.7
  26.4 0.0 copy-done.14
  26.4 0.0 copy-start.3
  26.5 0.0 copy-start.9
  26.5 11.6 %forward.1 = (bf16[4096,128]{1,0:T(8,128)(2,1)S(1)}, bf16[4096,128]{1,0:T(8,128)(2,1)S(1)}, bf16[4096,128]{1,0:T(8,128)(2,1)S(1)}, bf16[1024,128]{1,0:T(8,128)(2...) custom-call(s32[1]{0:T(128)S(6)} %copy.24.count_ref, ...), custom_call_target="tpu_custom_call" | custom-call | flops 4294967296 | bytes 8388608 | tf_op jit(solution)/shard_map/forward/pallas_call | solution.py:493
  38.0 4.1 %collective-permute-start.4 = (bf16[64,128]{1,0:T(8,128)(2,1)S(1)}, bf16[64,128]{1,0:T(8,128)(2,1)S(1)}, u32[]{:S(2)}, u32[]{:S(2)}) collective-permute-start(bf16[64,128]{1,0:T(8,128)(2,1)S(1)} %get-tuple-element.47), channel_id=1, source_target_pairs={{0,1},{1,2},{2,3},{3,4},{4,5},{5,6},{6,7},{8,9},{9,10},{10,11},{11... | collective-permute-start | bytes 49160 | tf_op jit(solution)/shard_map/ppermute | solution.py:562
  42.1 1.3 %collective-permute-start.5 = (bf16[64,128]{1,0:T(8,128)(2,1)S(1)}, bf16[64,128]{1,0:T(8,128)(2,1)S(1)}, u32[]{:S(2)}, u32[]{:S(2)}) collective-permute-start(bf16[64,128]{1,0:T(8,128)(2,1)S(1)} %get-tuple-element.48), channel_id=1, source_target_pairs={{1,0},{2,1},{3,2},{4,3},{5,4},{6,5},{7,6},{9,8},{10,9},{11,10},{12... | collective-permute-start | bytes 49160 | tf_op jit(solution)/shard_map/ppermute | solution.py:563
  43.4 0.0 collective-permute-done.4.nlow_ref
  43.5 4.1 %collective-permute-done.5.nhigh_ref = bf16[64,128]{1,0:T(8,128)(2,1)S(1)} collective-permute-done((bf16[64,128]{1,0:T(8,128)(2,1)S(1)}, bf16[64,128]{1,0:T(8,128)(2,1)S(1)}, u32[]{:S(2)}, u32[]{:S(2)}) %collective-permute-start.5) | collective-permute-done | bytes 16416 | tf_op jit(solution)/shard_map/ppermute | solution.py:563
  47.6 0.0 copy-done.3
  47.6 11.7 %backward.1 = (bf16[128,128]{1,0:T(8,128)(2,1)}, f32[1024,128]{1,0:T(8,128)S(1)}, bf16[4096,128]{1,0:T(8,128)(2,1)S(1)}, bf16[768,128]{1,0:T(8,128)(2,1)S(1)}, b...) custom-call(s32[1,4096]{1,0:T(1,128)S(1)} %copy-done.10, ...), custom_call_target="tpu_custom_call" | custom-call | flops 4294967296 | bytes 8388608 | tf_op jit(solution)/shard_map/backward/pallas_call | solution.py:567
  59.2 9.7 %all-to-all-start = ((bf16[32,32,128]{2,1,0:T(8,128)(2,1)}), bf16[32,32,128]{2,1,0:T(8,128)(2,1)S(1)}, u32[]{:S(2)}, u32[]{:S(2)}) async-start(bf16[32,32,128]{2,1,0:T(8,128)(2,1)} %bitcast), calls=%async_computation | async-start | bytes 524288 | tf_op jit(solution)/shard_map/all_to_all | solution.py:402
  69.0 5.1 %collective-permute-start.6 = (bf16[768,128]{1,0:T(8,128)(2,1)S(1)}, bf16[768,128]{1,0:T(8,128)(2,1)S(1)}, u32[]{:S(2)}, u32[]{:S(2)}) collective-permute-start(bf16[768,128]{1,0:T(8,128)(2,1)S(1)} %get-tuple-element.53), channel_id=1, source_target_pairs={{0,1},{1,2},{2,3},{3,4},{4,5},{5,6},{6,7},{8,9},{9,10},{10,11},{11... | collective-permute-start | bytes 589832 | tf_op jit(solution)/shard_map/ppermute | solution.py:652
  74.0 1.3 %collective-permute-start.7 = (bf16[768,128]{1,0:T(8,128)(2,1)S(1)}, bf16[768,128]{1,0:T(8,128)(2,1)S(1)}, u32[]{:S(2)}, u32[]{:S(2)}) collective-permute-start(bf16[768,128]{1,0:T(8,128)(2,1)S(1)} %get-tuple-element.55), channel_id=1, source_target_pairs={{1,0},{2,1},{3,2},{4,3},{5,4},{6,5},{7,6},{9,8},{10,9},{11,10},{12... | collective-permute-start | bytes 589832 | tf_op jit(solution)/shard_map/ppermute | solution.py:651
  75.4 2.7 %collective-permute-done.6.mid_low_ref = bf16[768,128]{1,0:T(8,128)(2,1)S(1)} collective-permute-done((bf16[768,128]{1,0:T(8,128)(2,1)S(1)}, bf16[768,128]{1,0:T(8,128)(2,1)S(1)}, u32[]{:S(2)}, u32[]{:S(2)}) %collective-permute-start.6) | collective-permute-done | bytes 196640 | tf_op jit(solution)/shard_map/ppermute | solution.py:652
  78.1 4.4 %collective-permute-done.7.mid_high_ref = bf16[768,128]{1,0:T(8,128)(2,1)S(1)} collective-permute-done((bf16[768,128]{1,0:T(8,128)(2,1)S(1)}, bf16[768,128]{1,0:T(8,128)(2,1)S(1)}, u32[]{:S(2)}, u32[]{:S(2)}) %collective-permute-start.7) | collective-permute-done | bytes 196640 | tf_op jit(solution)/shard_map/ppermute | solution.py:651
  82.5 0.0 all-to-all-done
  82.5 0.1 reduce_sum.24
  82.6 0.6 broadcast_in_dim.4
  83.2 4.6 %all-to-all-start.1 = ((bf16[8,32,128]{2,1,0:T(8,128)(2,1)}), bf16[8,32,128]{2,1,0:T(8,128)(2,1)S(1)}, u32[]{:S(2)}, u32[]{:S(2)}) async-start(bf16[8,32,128]{2,1,0:T(8,128)(2,1)} %broadcast_in_dim.4), calls=%async_computation.1 | async-start | bytes 131072 | tf_op jit(solution)/shard_map/all_to_all | solution.py:404
  87.8 4.5 %collective-permute-start.8 = (bf16[768,128]{1,0:T(8,128)(2,1)S(1)}, bf16[768,128]{1,0:T(8,128)(2,1)S(1)}, u32[]{:S(2)}, u32[]{:S(2)}) collective-permute-start(bf16[768,128]{1,0:T(8,128)(2,1)S(1)} %pad_maximum_fusion.2), channel_id=1, source_target_pairs={{0,8},{8,16},{16,24},{24,32},{32,40},{40,48},{48,56},{56,64},{64,7... | collective-permute-start | bytes 589832 | tf_op jit(solution)/shard_map/ppermute | solution.py:676
  92.3 2.7 %all-to-all-done.1 = bf16[8,32,128]{2,1,0:T(8,128)(2,1)S(1)} async-done(((bf16[8,32,128]{2,1,0:T(8,128)(2,1)}), bf16[8,32,128]{2,1,0:T(8,128)(2,1)S(1)}, u32[]{:S(2)}, u32[]{:S(2)}) %all-to-all-start.1) | async-done | bytes 65568 | tf_op jit(solution)/shard_map/all_to_all | solution.py:404
  95.0 0.7 broadcast_in_dim.5
  95.8 9.5 %all-to-all-start.2 = ((bf16[32,32,128]{2,1,0:T(8,128)(2,1)}), bf16[32,32,128]{2,1,0:T(8,128)(2,1)S(1)}, u32[]{:S(2)}, u32[]{:S(2)}) async-start(bf16[32,32,128]{2,1,0:T(8,128)(2,1)} %broadcast_in_dim.5), calls=%async_computation.2 | async-start | bytes 524288 | tf_op jit(solution)/shard_map/all_to_all | solution.py:406
  105.3 2.1 %collective-permute-start.9 = (bf16[768,128]{1,0:T(8,128)(2,1)S(1)}, bf16[768,128]{1,0:T(8,128)(2,1)S(1)}, u32[]{:S(2)}, u32[]{:S(2)}) collective-permute-start(bf16[768,128]{1,0:T(8,128)(2,1)S(1)} %pad_maximum_fusion.3), channel_id=1, source_target_pairs={{8,0},{16,8},{24,16},{32,24},{40,32},{48,40},{56,48},{64,56},{72,6... | collective-permute-start | bytes 589832 | tf_op jit(solution)/shard_map/ppermute | solution.py:673
  107.5 0.0 copy-start.13
  107.5 0.0 copy-start.16
  107.5 4.9 %local.1.part_ref = f32[1024,128]{1,0:T(8,128)S(1)} custom-call(s32[1]{0:T(128)S(6)} %copy.24.count_ref, s32[1,4096]{1,0:T(1,128)S(1)} %copy-done.10, s32[1,4096]{1,0:T(1,128)S(1)} %copy-done.11, bf16[4096,128]{1,0:T(8,128)(2,1)S(1)} %get-tuple-element.56.dedge_ref, f32[1024,128]{1,0:T(8,128)S(1)} %get-tuple-element.57.dnode_ref, bf16[256,128]{1,0:T(8,128)(2,1)S(1)} %copy-done.5), custom_call_target="tpu_custom_call" | custom-call | flops 2147483648 | bytes 3145728 | tf_op jit(solution)/shard_map/local/pallas_call | solution.py:654
  112.4 0.0 collective-permute-done.8.down_ref
  112.4 1.6 %collective-permute-done.9.up_ref = bf16[768,128]{1,0:T(8,128)(2,1)S(1)} collective-permute-done((bf16[768,128]{1,0:T(8,128)(2,1)S(1)}, bf16[768,128]{1,0:T(8,128)(2,1)S(1)}, u32[]{:S(2)}, u32[]{:S(2)}) %collective-permute-start.9) | collective-permute-done | bytes 196640 | tf_op jit(solution)/shard_map/ppermute | solution.py:673
  114.0 2.2 %returned.1 = f32[1024,128]{1,0:T(8,128)} custom-call(s32[1,8]{1,0:T(1,128)S(1)} %copy-done.16, s32[1,8,256]{2,1,0:T(8,128)S(1)} %copy-done.13, bf16[768,128]{1,0:T(8,128)(2,1)S(1)} %collective-permute-done.8.down_ref, bf16[768,128]{1,0:T(8,128)(2,1)S(1)} %collective-permute-done.9.up_ref, bf16[768,128]{1,0:T(8,128)(2,1)S(1)} %collective-permute-done.6.mid_low_ref, ...), custom_call_target="tpu_custom_call" | custom-call | flops 536870912 | bytes 2097152 | tf_op jit(solution)/shard_map/returned/pallas_call | solution.py:680
  116.3 0.0 all-to-all-done.2
  116.3 0.7 copy-done.17
  117.0 1.7 %scaled.1 = (f32[256,128]{1,0:T(8,128)}, f32[128,128]{1,0:T(8,128)}, f32[256,128]{1,0:T(8,128)}, f32[128,128]{1,0:T(8,128)}, f32[128,128]{1,0:T(8,128)}, /*index=5*/f32[128,128]{1,0:T(8,128)}) custom-call(bf16[1024,128]{1,0:T(8,128)(2,1)} %bitcast.2), custom_call_target="tpu_custom_call" | custom-call | tf_op jit(solution)/shard_map/scaled/pallas_call | solution.py:702
  (22 shorter events, 0.2 us)
Async XLA Ops:
  0.6 1.0 copy-start.1
  1.6 0.7 copy-start.12
  2.3 0.7 copy-start.15
  4.4 7.3 %collective-permute-start = (bf16[768,128]{1,0:T(8,128)(2,1)S(1)}, bf16[768,128]{1,0:T(8,128)(2,1)S(1)}, u32[]{:S(2)}, u32[]{:S(2)}) collective-permute-start(bf16[768,128]{1,0:T(8,128)(2,1)S(1)} %get-tuple-element.39), channel_id=1, source_target_pairs={{0,8},{8,16},{16,24},{24,32},{32,40},{40,48},{48,56},{56,64},{64,7... | collective-permute-start | bytes 589832 | tf_op jit(solution)/shard_map/ppermute | solution.py:454
  9.0 7.0 %collective-permute-start.1 = (bf16[768,128]{1,0:T(8,128)(2,1)S(1)}, bf16[768,128]{1,0:T(8,128)(2,1)S(1)}, u32[]{:S(2)}, u32[]{:S(2)}) collective-permute-start(bf16[768,128]{1,0:T(8,128)(2,1)S(1)} %get-tuple-element.40), channel_id=1, source_target_pairs={{8,0},{16,8},{24,16},{32,24},{40,32},{48,40},{56,48},{64,56},{72,6... | collective-permute-start | bytes 589832 | tf_op jit(solution)/shard_map/ppermute | solution.py:455
  10.9 0.8 copy-start
  16.0 5.7 %copy-start.2 = (bf16[1024,128]{1,0:T(8,128)(2,1)S(1)}, bf16[1024,128]{1,0:T(8,128)(2,1)}, u32[]{:S(2)}) copy-start(bf16[1024,128]{1,0:T(8,128)(2,1)} %nodes_ref.7) | copy-start | bytes 786436
  16.0 10.2 %collective-permute-start.2 = (bf16[800,128]{1,0:T(8,128)(2,1)S(1)}, bf16[800,128]{1,0:T(8,128)(2,1)S(1)}, u32[]{:S(2)}, u32[]{:S(2)}) collective-permute-start(bf16[800,128]{1,0:T(8,128)(2,1)S(1)} %pad_maximum_fusion), channel_id=1, source_target_pairs={{0,1},{1,2},{2,3},{3,4},{4,5},{5,6},{6,7},{8,9},{9,10},{10,11},{11... | collective-permute-start | bytes 614408 | tf_op jit(solution)/shard_map/ppermute | solution.py:469
  19.7 2.0 %copy-start.10 = (s32[1,4096]{1,0:T(1,128)S(1)}, s32[1,4096]{1,0:T(1,128)}, u32[]{:S(2)}) copy-start(s32[1,4096]{1,0:T(1,128)} %send_ref.7) | copy-start | bytes 49156
  19.7 2.0 %copy-start.11 = (s32[1,4096]{1,0:T(1,128)S(1)}, s32[1,4096]{1,0:T(1,128)}, u32[]{:S(2)}) copy-start(s32[1,4096]{1,0:T(1,128)} %recv_ref.7) | copy-start | bytes 49156
  19.7 6.7 %collective-permute-start.3 = (bf16[800,128]{1,0:T(8,128)(2,1)S(1)}, bf16[800,128]{1,0:T(8,128)(2,1)S(1)}, u32[]{:S(2)}, u32[]{:S(2)}) collective-permute-start(bf16[800,128]{1,0:T(8,128)(2,1)S(1)} %pad_maximum_fusion.1), channel_id=1, source_target_pairs={{1,0},{2,1},{3,2},{4,3},{5,4},{6,5},{7,6},{9,8},{10,9},{11,10},{12... | collective-permute-start | bytes 614408 | tf_op jit(solution)/shard_map/ppermute | solution.py:476
  21.7 4.7 %copy-start.4 = (bf16[256,128]{1,0:T(8,128)(2,1)S(1)}, bf16[256,128]{1,0:T(8,128)(2,1)}, u32[]{:S(2)}) copy-start(bf16[256,128]{1,0:T(8,128)(2,1)} %wni_ref.3) | copy-start | bytes 196612
  21.7 4.7 %copy-start.5 = (bf16[256,128]{1,0:T(8,128)(2,1)S(1)}, bf16[256,128]{1,0:T(8,128)(2,1)}, u32[]{:S(2)}) copy-start(bf16[256,128]{1,0:T(8,128)(2,1)} %wei_ref.5) | copy-start | bytes 196612
  21.7 4.7 %copy-start.6 = (bf16[128,128]{1,0:T(8,128)(2,1)S(1)}, bf16[128,128]{1,0:T(8,128)(2,1)}, u32[]{:S(2)}) copy-start(bf16[128,128]{1,0:T(8,128)(2,1)} %weo_ref.3) | copy-start | bytes 98308
  21.8 4.7 %copy-start.7 = (bf16[128,128]{1,0:T(8,128)(2,1)S(1)}, bf16[128,128]{1,0:T(8,128)(2,1)}, u32[]{:S(2)}) copy-start(bf16[128,128]{1,0:T(8,128)(2,1)} %wno_ref.3) | copy-start | bytes 98308
  21.8 4.7 %copy-start.14 = (s32[1,1024]{1,0:T(1,128)S(1)}, s32[1,1024]{1,0:T(1,128)}, u32[]{:S(2)}) copy-start(s32[1,1024]{1,0:T(1,128)} %pool_ref.3) | copy-start | bytes 12292
  26.4 21.1 %copy-start.3 = (bf16[1024,128]{1,0:T(8,128)(2,1)S(1)}, bf16[1024,128]{1,0:T(8,128)(2,1)}, u32[]{:S(2)}) copy-start(bf16[1024,128]{1,0:T(8,128)(2,1)} %dfine_ref.1) | copy-start | bytes 786436
  26.5 21.1 %copy-start.9 = (bf16[128,128]{1,0:T(8,128)(2,1)S(1)}, bf16[128,128]{1,0:T(8,128)(2,1)}, u32[]{:S(2)}) copy-start(bf16[128,128]{1,0:T(8,128)(2,1)} %wco_ref.1) | copy-start | bytes 98308
  38.0 9.6 %copy-start.8 = (bf16[128,128]{1,0:T(8,128)(2,1)S(1)}, bf16[128,128]{1,0:T(8,128)(2,1)}, u32[]{:S(2)}) copy-start(bf16[128,128]{1,0:T(8,128)(2,1)} %wci_ref.1) | copy-start | bytes 98308
  38.0 5.4 %collective-permute-start.4 = (bf16[64,128]{1,0:T(8,128)(2,1)S(1)}, bf16[64,128]{1,0:T(8,128)(2,1)S(1)}, u32[]{:S(2)}, u32[]{:S(2)}) collective-permute-start(bf16[64,128]{1,0:T(8,128)(2,1)S(1)} %get-tuple-element.47), channel_id=1, source_target_pairs={{0,1},{1,2},{2,3},{3,4},{4,5},{5,6},{6,7},{8,9},{9,10},{10,11},{11... | collective-permute-start | bytes 49160 | tf_op jit(solution)/shard_map/ppermute | solution.py:562
  42.1 5.5 %collective-permute-start.5 = (bf16[64,128]{1,0:T(8,128)(2,1)S(1)}, bf16[64,128]{1,0:T(8,128)(2,1)S(1)}, u32[]{:S(2)}, u32[]{:S(2)}) collective-permute-start(bf16[64,128]{1,0:T(8,128)(2,1)S(1)} %get-tuple-element.48), channel_id=1, source_target_pairs={{1,0},{2,1},{3,2},{4,3},{5,4},{6,5},{7,6},{9,8},{10,9},{11,10},{12... | collective-permute-start | bytes 49160 | tf_op jit(solution)/shard_map/ppermute | solution.py:563
  59.2 23.3 %all-to-all-start = ((bf16[32,32,128]{2,1,0:T(8,128)(2,1)}), bf16[32,32,128]{2,1,0:T(8,128)(2,1)S(1)}, u32[]{:S(2)}, u32[]{:S(2)}) async-start(bf16[32,32,128]{2,1,0:T(8,128)(2,1)} %bitcast), calls=%async_computation | async-start | bytes 524288 | tf_op jit(solution)/shard_map/all_to_all | solution.py:402
  69.0 9.1 %collective-permute-start.6 = (bf16[768,128]{1,0:T(8,128)(2,1)S(1)}, bf16[768,128]{1,0:T(8,128)(2,1)S(1)}, u32[]{:S(2)}, u32[]{:S(2)}) collective-permute-start(bf16[768,128]{1,0:T(8,128)(2,1)S(1)} %get-tuple-element.53), channel_id=1, source_target_pairs={{0,1},{1,2},{2,3},{3,4},{4,5},{5,6},{6,7},{8,9},{9,10},{10,11},{11... | collective-permute-start | bytes 589832 | tf_op jit(solution)/shard_map/ppermute | solution.py:652
  74.0 8.5 %collective-permute-start.7 = (bf16[768,128]{1,0:T(8,128)(2,1)S(1)}, bf16[768,128]{1,0:T(8,128)(2,1)S(1)}, u32[]{:S(2)}, u32[]{:S(2)}) collective-permute-start(bf16[768,128]{1,0:T(8,128)(2,1)S(1)} %get-tuple-element.55), channel_id=1, source_target_pairs={{1,0},{2,1},{3,2},{4,3},{5,4},{6,5},{7,6},{9,8},{10,9},{11,10},{12... | collective-permute-start | bytes 589832 | tf_op jit(solution)/shard_map/ppermute | solution.py:651
  83.2 11.8 %all-to-all-start.1 = ((bf16[8,32,128]{2,1,0:T(8,128)(2,1)}), bf16[8,32,128]{2,1,0:T(8,128)(2,1)S(1)}, u32[]{:S(2)}, u32[]{:S(2)}) async-start(bf16[8,32,128]{2,1,0:T(8,128)(2,1)} %broadcast_in_dim.4), calls=%async_computation.1 | async-start | bytes 131072 | tf_op jit(solution)/shard_map/all_to_all | solution.py:404
  87.8 24.6 %collective-permute-start.8 = (bf16[768,128]{1,0:T(8,128)(2,1)S(1)}, bf16[768,128]{1,0:T(8,128)(2,1)S(1)}, u32[]{:S(2)}, u32[]{:S(2)}) collective-permute-start(bf16[768,128]{1,0:T(8,128)(2,1)S(1)} %pad_maximum_fusion.2), channel_id=1, source_target_pairs={{0,8},{8,16},{16,24},{24,32},{32,40},{40,48},{48,56},{56,64},{64,7... | collective-permute-start | bytes 589832 | tf_op jit(solution)/shard_map/ppermute | solution.py:676
  95.8 20.5 %all-to-all-start.2 = ((bf16[32,32,128]{2,1,0:T(8,128)(2,1)}), bf16[32,32,128]{2,1,0:T(8,128)(2,1)S(1)}, u32[]{:S(2)}, u32[]{:S(2)}) async-start(bf16[32,32,128]{2,1,0:T(8,128)(2,1)} %broadcast_in_dim.5), calls=%async_computation.2 | async-start | bytes 524288 | tf_op jit(solution)/shard_map/all_to_all | solution.py:406
  105.3 8.7 %collective-permute-start.9 = (bf16[768,128]{1,0:T(8,128)(2,1)S(1)}, bf16[768,128]{1,0:T(8,128)(2,1)S(1)}, u32[]{:S(2)}, u32[]{:S(2)}) collective-permute-start(bf16[768,128]{1,0:T(8,128)(2,1)S(1)} %pad_maximum_fusion.3), channel_id=1, source_target_pairs={{8,0},{16,8},{24,16},{32,24},{40,32},{48,40},{56,48},{64,56},{72,6... | collective-permute-start | bytes 589832 | tf_op jit(solution)/shard_map/ppermute | solution.py:673
  107.5 6.6 %copy-start.13 = (s32[1,8,256]{2,1,0:T(8,128)S(1)}, s32[1,8,256]{2,1,0:T(8,128)}, u32[]{:S(2)}) copy-start(s32[1,8,256]{2,1,0:T(8,128)} %rows_ref.3) | copy-start | bytes 24580
  107.5 6.6 %copy-start.16 = (s32[1,8]{1,0:T(1,128)S(1)}, s32[1,8]{1,0:T(1,128)}, u32[]{:S(2)}) copy-start(s32[1,8]{1,0:T(1,128)} %count_ref.7) | copy-start | bytes 100
  116.3 0.7 copy-start.17

commit v2 on v1

v2 whole, which is shorter than its diff:
```python
import jax
import jax.numpy as jnp
from jax import lax
from jax.experimental import pallas as pl
from jax.experimental.pallas import tpu as pltpu
from jax.sharding import Mesh
from jax.sharding import PartitionSpec as P

BAND = 32
LAT = 128
LOW = 512
BITS = 9
OWN_STEP = FWD_STEP = BWD_STEP = GHOST_STEP = LOCAL_STEP = 512
GX_GY = ("gx_0", "gx_1", "gx_2", "gy")
GX = ("gx_0", "gx_1", "gx_2")
ACROSS = (-1, -1, -1, 0, 0, 1, 1, 1)
ALONG = (-1, 0, 1, -1, 1, -1, 0, 1)
MIB = 1024 * 1024

f32 = jnp.float32
bf16 = jnp.bfloat16


def mm(left, right):
    return jnp.dot(left, right, preferred_element_type=f32)


def mm_nt(left, right):
    return lax.dot_general(left, right, (((1,), (1,)), ((), ())), preferred_element_type=f32)


def mm_tn(left, right):
    return lax.dot_general(left, right, (((0,), (0,)), ((), ())), preferred_element_type=f32)


def wide(table):
    groups = table.shape[0] // LOW
    return jnp.concatenate([table[i * LOW : (i + 1) * LOW] for i in range(groups)], axis=1)


def tall(table):
    groups = table.shape[1] // LAT
    return jnp.concatenate([table[:, i * LAT : (i + 1) * LAT] for i in range(groups)], axis=0)


def in_columns(row):
    parts = []
    for j in range(row.shape[1] // LAT):
        parts.append(jnp.broadcast_to(row[:, j * LAT : (j + 1) * LAT], (LAT, LAT)).T)
    return jnp.concatenate(parts, axis=0)


def one_hot(col, rows):
    lanes = lax.broadcasted_iota(jnp.int32, col.shape, 1)
    return jnp.concatenate(
        [(col == lanes + j * LAT).astype(f32).astype(bf16) for j in range(rows // LAT)], axis=1
    )


def one_hot_t(row, rows):
    ids = lax.broadcasted_iota(jnp.int32, (rows, row.shape[1]), 0)
    return (ids == row).astype(f32).astype(bf16)


def take(col, table):
    got = mm(one_hot(col & (LOW - 1), LOW), table)
    group = col >> BITS
    total = jnp.zeros((col.shape[0], LAT), f32)
    for i in range(table.shape[1] // LAT):
        total = jnp.where(group == i, got[:, i * LAT : (i + 1) * LAT], total)
    return total


def put(row, col, values, groups):
    group = col >> BITS
    spread = jnp.concatenate(
        [jnp.where(group == i, values, 0.0).astype(bf16) for i in range(groups)], axis=1
    )
    return mm(one_hot_t(row & (LOW - 1), LOW), spread)


def sigmoid(v):
    return 1.0 / (1.0 + jnp.exp(-v))


def act_and_slope(v):
    s = sigmoid(v)
    return v * s, s * (1.0 + v * (1.0 - s))


def live_row(row, first, count):
    ids = lax.broadcasted_iota(jnp.int32, row.shape, 1) + first
    return jnp.where(ids < count, row, -1)


def live_slots(place_ref, count_ref, k):
    a = place_ref[0] + ACROSS[k]
    b = place_ref[1] + ALONG[k]
    inside = (a >= 0) & (a < place_ref[2]) & (b >= 0) & (b < place_ref[3])
    return jnp.where(inside, count_ref[0, k], 0)


def pick_kernel(place_ref, count_ref, rows_hbm, nodes_hbm, up_ref, down_ref, mid_ref, rows, nodes, sems):
    copies = (
        pltpu.make_async_copy(nodes_hbm, nodes, sems.at[0]),
        pltpu.make_async_copy(rows_hbm, rows, sems.at[1]),
    )
    for copy in copies:
        copy.start()
    for copy in copies:
        copy.wait()
    table = wide(nodes[...])
    slots = rows.shape[2]
    for k in range(8):
        row = live_row(rows[0, k : k + 1, :], 0, live_slots(place_ref, count_ref, k))
        got = take(in_columns(row), table).astype(bf16)
        if k < 3:
            down_ref[k * slots : (k + 1) * slots, :] = got
        elif k < 5:
            mid_ref[(k - 3) * slots : (k - 2) * slots, :] = got
        else:
            up_ref[(k - 5) * slots : (k - 4) * slots, :] = got


def own_kernel(count_ref, index_ref, nodes_ref, out_ref):
    table = wide(nodes_ref[...])
    first = pl.program_id(0) * index_ref.shape[1]
    row = live_row(index_ref[...], first, count_ref[0])
    out_ref[...] = take(in_columns(row), table).astype(bf16)


def forward_kernel(
    count_ref,
    send_ref,
    recv_ref,
    sown_ref,
    recvs_ref,
    up_ref,
    down_ref,
    yup_ref,
    ydown_ref,
    nodes_ref,
    pool_ref,
    wei_ref,
    weo_ref,
    wni_ref,
    wno_ref,
    senders_ref,
    act_ref,
    slope_ref,
    fine_ref,
    summed_ref,
    nact_ref,
    nslope_ref,
    window_ref,
    wlow_ref,
    whigh_ref,
    table,
    acc,
):
    step = pl.program_id(0)
    slots = up_ref.shape[0] // 3

    @pl.when(step == 0)
    def _():
        def block(ref, i):
            return ref[i * slots : (i + 1) * slots, :]

        blocks = (
            block(ydown_ref, 2),
            block(down_ref, 1),
            block(yup_ref, 2),
            block(ydown_ref, 1),
            block(yup_ref, 1),
            block(ydown_ref, 0),
            block(up_ref, 1),
            block(yup_ref, 0),
        )
        for k in range(8):
            table[(k % 2) * slots : (k % 2 + 1) * slots, (k // 2) * LAT : (k // 2 + 1) * LAT] = blocks[k]
        acc[...] = jnp.zeros_like(acc)

    first = step * send_ref.shape[1]
    count = count_ref[0]
    owned = nodes_ref.shape[0]
    send = in_columns(live_row(send_ref[...], first, count)) - owned
    senders = (take(send, table[...]) + sown_ref[...].astype(f32)).astype(bf16)
    senders_ref[...] = senders
    pre = mm(jnp.concatenate([senders, recvs_ref[...]], axis=1), wei_ref[...])
    act, slope = act_and_slope(pre)
    act = act.astype(bf16)
    act_ref[...] = act
    slope_ref[...] = slope.astype(bf16)
    message = mm(act, weo_ref[...]).astype(bf16).astype(f32)
    recv = live_row(recv_ref[...], first, count)
    acc[...] += put(recv, in_columns(recv), message, owned // LOW)

    @pl.when(step == pl.num_programs(0) - 1)
    def _():
        summed = tall(acc[...]).astype(bf16)
        summed_ref[...] = summed
        nodes = nodes_ref[...]
        pre = mm(jnp.concatenate([nodes, summed], axis=1), wni_ref[...])
        act, slope = act_and_slope(pre)
        act = act.astype(bf16)
        nact_ref[...] = act
        nslope_ref[...] = slope.astype(bf16)
        fine = (nodes.astype(f32) + mm(act, wno_ref[...])).astype(bf16)
        fine_ref[...] = fine
        rows = window_ref.shape[0]
        window = mm(one_hot_t(pool_ref[...], rows), fine)
        window_ref[...] = window
        wlow_ref[...] = window[: 2 * BAND].astype(bf16)
        whigh_ref[...] = window[rows - 2 * BAND :].astype(bf16)


def backward_kernel(
    recv_ref,
    count_ref,
    senders_ref,
    recvs_ref,
    act_ref,
    slope_ref,
    window_ref,
    nlow_ref,
    nhigh_ref,
    dcl_ref,
    dch_ref,
    dcoarse_ref,
    dfine_ref,
    pool_ref,
    nodes_ref,
    summed_ref,
    nact_ref,
    nslope_ref,
    wei_ref,
    weo_ref,
    wni_ref,
    wno_ref,
    wci_ref,
    wco_ref,
    coarse_ref,
    dnode_ref,
    dedge_ref,
    grads_ref,
    table,
    gacc,
):
    step = pl.program_id(0)

    @pl.when(step == 0)
    def _():
        gacc[...] = jnp.zeros_like(gacc)
        window = window_ref[...]
        rows = window.shape[0]
        total = jnp.concatenate(
            [
                window[: 2 * BAND] + nlow_ref[...].astype(f32),
                window[2 * BAND : rows - 2 * BAND],
                window[rows - 2 * BAND :] + nhigh_ref[...].astype(f32),
            ],
            axis=0,
        )
        coarse_in = (0.125 * total).astype(bf16)
        d_coarse = jnp.concatenate([dcl_ref[...], dcoarse_ref[...], dch_ref[...]], axis=0)
        act, slope = act_and_slope(mm(coarse_in, wci_ref[...]))
        act = act.astype(bf16)
        coarse_out = (coarse_in.astype(f32) + mm(act, wco_ref[...])).astype(bf16)
        coarse_ref[...] = coarse_out[BAND : rows - BAND]
        d_pre = (mm_nt(d_coarse, wco_ref[...]) * slope).astype(bf16)
        d_in = (d_coarse.astype(f32) + mm_nt(d_pre, wci_ref[...])).astype(bf16)
        inner = slice(BAND, rows - BAND)
        g_ci = mm_tn(coarse_in[inner], d_pre[inner])
        g_co = mm_tn(act[inner], d_coarse[inner])
        reach = jnp.concatenate([d_in, jnp.zeros((2 * LAT - rows, LAT), bf16)], axis=0)
        parent = mm(one_hot(in_columns(pool_ref[...]), 2 * LAT), reach)
        d_total = dfine_ref[...].astype(f32) + 0.125 * parent
        d_out = d_total.astype(bf16)
        d_node = (mm_nt(d_out, wno_ref[...]) * nslope_ref[...].astype(f32)).astype(bf16)
        back = mm_nt(d_node, wni_ref[...])
        dnode_ref[...] = d_total + back[:, :LAT]
        table[...] = wide(back[:, LAT:].astype(bf16))
        g_ni = mm_tn(jnp.concatenate([nodes_ref[...], summed_ref[...]], axis=1), d_node)
        g_no = mm_tn(nact_ref[...], d_out)
        grads_ref[3 * LAT : 5 * LAT, :] = g_ni.astype(bf16)
        grads_ref[5 * LAT : 6 * LAT, :] = g_no.astype(bf16)
        grads_ref[6 * LAT : 7 * LAT, :] = g_ci.astype(bf16)
        grads_ref[7 * LAT :, :] = g_co.astype(bf16)

    first = step * recv_ref.shape[1]
    count = count_ref[0]
    recv = in_columns(live_row(recv_ref[...], first, count))
    d_message = take(recv, table[...]).astype(bf16)
    d_pre = (mm_nt(d_message, weo_ref[...]) * slope_ref[...].astype(f32)).astype(bf16)
    dedge_ref[...] = d_pre
    gacc[: 2 * LAT, :] += mm_tn(jnp.concatenate([senders_ref[...], recvs_ref[...]], axis=1), d_pre)
    gacc[2 * LAT :, :] += mm_tn(act_ref[...], d_message)

    @pl.when(step == pl.num_programs(0) - 1)
    def _():
        grads_ref[: 3 * LAT, :] = gacc[...].astype(bf16)


def ghost_kernel(
    count_ref, send_ref, dedge_ref, wei_ref, rdown_ref, rup_ref, rown_ref, acc, *, owned
):
    step = pl.program_id(0)

    @pl.when(step == 0)
    def _():
        acc[...] = jnp.zeros_like(acc)

    first = step * send_ref.shape[1]
    send = live_row(send_ref[...], first, count_ref[0]) - owned
    acc[...] += put(send, in_columns(send), dedge_ref[...].astype(f32), 4)

    @pl.when(step == pl.num_programs(0) - 1)
    def _():
        ghosts = mm_nt(tall(acc[...]).astype(bf16), wei_ref[:LAT, :]).astype(bf16)
        slots = ghosts.shape[0] // 8
        for place, (ref, i) in enumerate(
            (
                (rup_ref, 2),
                (rown_ref, 0),
                (rdown_ref, 2),
                (rup_ref, 1),
                (rdown_ref, 1),
                (rup_ref, 0),
                (rown_ref, 1),
                (rdown_ref, 0),
            )
        ):
            ref[i * slots : (i + 1) * slots, :] = ghosts[place * slots : (place + 1) * slots]


def local_kernel(count_ref, send_ref, recv_ref, dedge_ref, dnode_ref, wei_ref, out_ref, acc_s, acc_r):
    step = pl.program_id(0)

    @pl.when(step == 0)
    def _():
        acc_s[...] = jnp.zeros_like(acc_s)
        acc_r[...] = jnp.zeros_like(acc_r)

    first = step * send_ref.shape[1]
    count = count_ref[0]
    groups = out_ref.shape[0] // LOW
    d_pre = dedge_ref[...].astype(f32)
    send = live_row(send_ref[...], first, count)
    recv = live_row(recv_ref[...], first, count)
    acc_s[...] += put(send, in_columns(send), d_pre, groups)
    acc_r[...] += put(recv, in_columns(recv), d_pre, groups)

    @pl.when(step == pl.num_programs(0) - 1)
    def _():
        out_ref[...] = (
            dnode_ref[...]
            + mm_nt(tall(acc_s[...]).astype(bf16), wei_ref[:LAT, :])
            + mm_nt(tall(acc_r[...]).astype(bf16), wei_ref[LAT:, :])
        )


def final_kernel(
    scale,
    place_ref,
    count_ref,
    rows_ref,
    down_ref,
    up_ref,
    mid_low_ref,
    mid_high_ref,
    part_ref,
    sums_ref,
    out_ref,
    *grad_refs,
):
    slots = rows_ref.shape[2]
    groups = out_ref.shape[0] // LOW
    total = jnp.zeros((LOW, groups * LAT), f32)
    for k in range(8):
        row = live_row(rows_ref[0, k : k + 1, :], 0, live_slots(place_ref, count_ref, k))
        if k < 3:
            got = down_ref[k * slots : (k + 1) * slots, :]
        elif k == 3:
            got = mid_low_ref[slots : 2 * slots, :]
        elif k == 4:
            got = mid_high_ref[slots : 2 * slots, :]
        else:
            got = up_ref[(k - 5) * slots : (k - 4) * slots, :]
        total = total + put(row, in_columns(row), got.astype(f32), groups)
    out_ref[...] = part_ref[...] + tall(total)
    first = 0
    for ref in grad_refs:
        rows = ref.shape[0]
        ref[...] = sums_ref[first : first + rows, :].astype(f32) * scale
        first += rows


def whole(shape):
    return pl.BlockSpec(shape, lambda *_: (0,) * len(shape))


def scalars():
    return pl.BlockSpec(memory_space=pltpu.SMEM)


def edge_row(step):
    return pl.BlockSpec((1, step), lambda i: (0, i))


def edge_block(step):
    return pl.BlockSpec((step, LAT), lambda i: (i, 0))


def hbm():
    return pl.BlockSpec(memory_space=pltpu.HBM)


def shape(dims, dtype):
    return jax.ShapeDtypeStruct(dims, dtype)


def params(mib):
    return pltpu.CompilerParams(vmem_limit_bytes=mib * MIB)


def cost(flops, moved):
    return pl.CostEstimate(flops=flops, bytes_accessed=moved, transcendentals=0)


def reduced(grads):
    rows = grads.shape[0]
    far, near = GX, ("gy",)
    n_far, n_near = 32, 8
    part = rows // n_far
    got = lax.all_to_all(grads.reshape(n_far, part, LAT), far, 0, 0, tiled=True)
    own = got.astype(f32).sum(axis=0).astype(bf16)
    got = lax.all_to_all(jnp.broadcast_to(own[None], (n_near, part, LAT)), near, 0, 0, tiled=True)
    own = got.astype(f32).sum(axis=0).astype(bf16)
    got = lax.all_to_all(jnp.broadcast_to(own[None], (n_far, part, LAT)), far, 0, 0, tiled=True)
    return got.reshape(rows, LAT)


def call_pick(place, ghost_count, ghost_rows, nodes):
    slots = ghost_rows.shape[2]
    return pl.pallas_call(
        pick_kernel,
        out_shape=(
            shape((3 * slots, LAT), bf16),
            shape((3 * slots, LAT), bf16),
            shape((2 * slots, LAT), bf16),
        ),
        in_specs=[scalars(), scalars(), hbm(), hbm()],
        scratch_shapes=[
            pltpu.VMEM(ghost_rows.shape, jnp.int32),
            pltpu.VMEM(nodes.shape, bf16),
            pltpu.SemaphoreType.DMA((2,)),
        ],
        compiler_params=params(32),
        cost_estimate=cost(2 * 2048 * 512 * 256, MIB),
        name="pick",
    )(place, ghost_count, ghost_rows, nodes)


def call_own(edge_count, index, nodes):
    edges = index.shape[1]
    step = OWN_STEP
    return pl.pallas_call(
        own_kernel,
        grid=(edges // step,),
        out_shape=shape((edges, LAT), bf16),
        in_specs=[scalars(), edge_row(step), whole(nodes.shape)],
        out_specs=edge_block(step),
        compiler_params=params(32),
        cost_estimate=cost(2 * 4096 * 512 * 256, 2 * MIB),
        name="own_rows",
    )(edge_count, index, nodes)


def call_forward(edge_count, send, recv, sown, recvs, up, down, yup, ydown, nodes, pool, rows, *weights):
    edges, owned, step = send.shape[1], nodes.shape[0], FWD_STEP
    edge16 = shape((edges, LAT), bf16)
    node16 = shape((owned, LAT), bf16)
    band = shape((2 * BAND, LAT), bf16)
    outs = (edge16,) * 3 + (node16,) * 4 + (shape((rows, LAT), f32), band, band)
    plain = (up, down, yup, ydown, nodes, pool, *weights)
    return pl.pallas_call(
        forward_kernel,
        grid=(edges // step,),
        out_shape=outs,
        in_specs=[
            scalars(),
            edge_row(step),
            edge_row(step),
            edge_block(step),
            edge_block(step),
            *(whole(x.shape) for x in plain),
        ],
        out_specs=(edge_block(step),) * 3 + tuple(whole(x.shape) for x in outs[3:]),
        scratch_shapes=[
            pltpu.VMEM((LOW, 4 * LAT), bf16),
            pltpu.VMEM((LOW, owned // LOW * LAT), f32),
        ],
        compiler_params=params(40),
        cost_estimate=cost(2 * 4096 * 512 * 1024, 8 * MIB),
        name="forward",
    )(edge_count, send, recv, sown, recvs, *plain)


def call_backward(recv, edge_count, edge_arrays, plain):
    edges, step = recv.shape[1], BWD_STEP
    owned, coarse = plain[8].shape[0], plain[5].shape[0]
    return pl.pallas_call(
        backward_kernel,
        grid=(edges // step,),
        out_shape=(
            shape((coarse, LAT), bf16),
            shape((owned, LAT), f32),
            shape((edges, LAT), bf16),
            shape((8 * LAT, LAT), bf16),
        ),
        in_specs=[
            edge_row(step),
            scalars(),
            *(edge_block(step) for _ in edge_arrays),
            *(whole(x.shape) for x in plain),
        ],
        out_specs=(
            whole((coarse, LAT)),
            whole((owned, LAT)),
            edge_block(step),
            whole((8 * LAT, LAT)),
        ),
        scratch_shapes=[
            pltpu.VMEM((LOW, owned // LOW * LAT), bf16),
            pltpu.VMEM((3 * LAT, LAT), f32),
        ],
        compiler_params=params(40),
        cost_estimate=cost(2 * 4096 * 512 * 512, 8 * MIB),
        name="backward",
    )(recv, edge_count, *edge_arrays, *plain)


def call_ghost(edge_count, send, d_edge, w_edge_in, owned, slots):
    edges, step = send.shape[1], GHOST_STEP
    outs = (
        shape((3 * slots, LAT), bf16),
        shape((3 * slots, LAT), bf16),
        shape((2 * slots, LAT), bf16),
    )
    return pl.pallas_call(
        lambda *refs: ghost_kernel(*refs, owned=owned),
        grid=(edges // step,),
        out_shape=outs,
        in_specs=[scalars(), edge_row(step), edge_block(step), whole(w_edge_in.shape)],
        out_specs=tuple(whole(x.shape) for x in outs),
        scratch_shapes=[pltpu.VMEM((LOW, 4 * LAT), f32)],
        compiler_params=params(32),
        cost_estimate=cost(2 * 4096 * 512 * 512, 3 * MIB),
        name="ghost_grads",
    )(edge_count, send, d_edge, w_edge_in)


def call_local(edge_count, send, recv, d_edge, d_node, w_edge_in):
    edges, step, owned = send.shape[1], LOCAL_STEP, d_node.shape[0]
    return pl.pallas_call(
        local_kernel,
        grid=(edges // step,),
        out_shape=shape((owned, LAT), f32),
        in_specs=[
            scalars(),
            edge_row(step),
            edge_row(step),
            edge_block(step),
            whole((owned, LAT)),
            whole(w_edge_in.shape),
        ],
        out_specs=whole((owned, LAT)),
        scratch_shapes=[pltpu.VMEM((LOW, owned // LOW * LAT), f32)] * 2,
        compiler_params=params(32),
        cost_estimate=cost(2 * 2 * 4096 * 512 * 256, 3 * MIB),
        name="local",
    )(edge_count, send, recv, d_edge, d_node, w_edge_in)


def call_final(scale, place, ghost_count, ghost_rows, *arrays):
    owned = arrays[4].shape[0]
    heights = (2 * LAT, LAT, 2 * LAT, LAT, LAT, LAT)
    return pl.pallas_call(
        lambda *refs: final_kernel(scale, *refs),
        out_shape=(shape((owned, LAT), f32), *(shape((h, LAT), f32) for h in heights)),
        in_specs=[
            scalars(),
            scalars(),
            whole(ghost_rows.shape),
            *(whole(x.shape) for x in arrays),
        ],
        compiler_params=params(32),
        cost_estimate=cost(2 * 2048 * 512 * 256, 2 * MIB),
        name="final",
    )(place, ghost_count, ghost_rows, *arrays)


def ring(n, shift):
    return [(i, (i + shift) % n) for i in range(n)]


def body(
    nodes,
    ghost_rows,
    ghost_count,
    edge_send,
    edge_recv,
    edge_count,
    pool_map,
    w_edge_in,
    w_edge_out,
    w_node_in,
    w_node_out,
    w_coarse_in,
    w_coarse_out,
    d_fine,
    d_coarse,
):
    owned = nodes.shape[0]
    slots = ghost_rows.shape[2]
    coarse = d_coarse.shape[0]
    n_gx, n_gy = lax.axis_size(GX), lax.axis_size("gy")
    place = jnp.stack([lax.axis_index(GX), lax.axis_index("gy"), n_gx, n_gy]).astype(jnp.int32)

    out_up, out_down, out_mid = call_pick(place, ghost_count, ghost_rows, nodes)
    up = lax.ppermute(out_up, GX, ring(n_gx, 1))
    down = lax.ppermute(out_down, GX, ring(n_gx, -1))
    recvs = call_own(edge_count, edge_recv, nodes)
    up, down, recvs = lax.optimization_barrier((up, down, recvs))

    yup = lax.ppermute(
        jnp.concatenate(
            [up[2 * slots :], out_mid[slots:], down[2 * slots :], d_coarse[coarse - BAND :]]
        ),
        "gy",
        ring(n_gy, 1),
    )
    ydown = lax.ppermute(
        jnp.concatenate([up[:slots], out_mid[:slots], down[:slots], d_coarse[:BAND]]),
        "gy",
        ring(n_gy, -1),
    )
    sown = call_own(edge_count, edge_send, nodes)

    (senders, act, slope, fine_out, summed, nact, nslope, window, wlow, whigh) = call_forward(
        edge_count,
        edge_send,
        edge_recv,
        sown,
        recvs,
        up,
        down,
        yup,
        ydown,
        nodes,
        pool_map,
        coarse + 2 * BAND,
        w_edge_in,
        w_edge_out,
        w_node_in,
        w_node_out,
    )

    nlow = lax.ppermute(whigh, "gy", ring(n_gy, 1))
    nhigh = lax.ppermute(wlow, "gy", ring(n_gy, -1))

    coarse_out, d_node, d_edge, grads = call_backward(
        edge_recv,
        edge_count,
        (senders, recvs, act, slope),
        (
            window,
            nlow,
            nhigh,
            yup[3 * slots :],
            ydown[3 * slots :],
            d_coarse,
            d_fine,
            pool_map,
            nodes,
            summed,
            nact,
            nslope,
            w_edge_in,
            w_edge_out,
            w_node_in,
            w_node_out,
            w_coarse_in,
            w_coarse_out,
        ),
    )
    r_down, r_up, r_own = call_ghost(edge_count, edge_send, d_edge, w_edge_in, owned, slots)
    high = lax.ppermute(r_down, "gy", ring(n_gy, -1))
    low = lax.ppermute(r_up, "gy", ring(n_gy, 1))
    d_own = call_local(edge_count, edge_send, edge_recv, d_edge, d_node, w_edge_in)
    high, low, d_own = lax.optimization_barrier((high, low, d_own))

    ret_up = lax.ppermute(
        jnp.concatenate([low[:slots], r_own[slots:], high[:slots]]), GX, ring(n_gx, -1)
    )
    ret_down = lax.ppermute(
        jnp.concatenate([low[2 * slots :], r_own[:slots], high[2 * slots :]]), GX, ring(n_gx, 1)
    )

    sums = reduced(grads)
    grad_scale = 1.0 / (owned * n_gx * n_gy) ** 0.5
    grad_nodes, *scaled = call_final(
        grad_scale, place, ghost_count, ghost_rows, ret_down, ret_up, low, high, d_own, sums
    )
    return (fine_out, coarse_out, grad_nodes, *scaled)


def solution(mesh):
    torus = Mesh(mesh.devices.reshape(4, 4, 2, mesh.shape["gy"]), GX_GY)
    in_specs = (
        P(GX_GY, None),
        P(GX_GY, None, None),
        P(GX_GY, None),
        P(GX_GY, None),
        P(GX_GY, None),
        P(GX_GY),
        P(GX_GY, None),
        P(),
        P(),
        P(),
        P(),
        P(),
        P(),
        P(GX_GY, None),
        P(GX_GY, None),
    )
    out_specs = (P(GX_GY, None), P(GX_GY, None), P(GX_GY, None), P(), P(), P(), P(), P(), P())
    return jax.shard_map(body, mesh=torus, in_specs=in_specs, out_specs=out_specs, check_vma=False)
```

time: 120 us -> 107 us (0.89)
  starting transfers between devices: 53.7 us -> 44.1 us
  waiting for transfers between devices: 20 us -> 16.5 us
  Pallas kernels: 37.9 us -> 40 us
  local copies, waits for them, and re-layouts: 5.27 us -> 3.76 us
    ppermute x6, waiting for transfers between devices: 15.5 us -> 3.5 us  [the longest x1 2.23 us: body(): low = lax.ppermute(r_up, 'gy', ring(n_gy, 1))]
    ppermute x6, starting transfers between devices: 18.2 us -> 9.28 us  [the longest x1 3.02 us: body(): high = lax.ppermute(r_down, 'gy', ring(n_gy, -1))]
    ppermute x1, waiting for transfers between devices: 1.59 us -> 7.41 us  [body(): lax.ppermute(jnp.concatenate([low[:slots], r_own[slots:], high[:slots]]),...]
    ppermute x1, starting transfers between devices: 1.29 us -> 4.04 us  [body(): lax.ppermute(jnp.concatenate([up[:slots], out_mid[:slots], down[:slots],...]
    pallas_call x7 -> x8, Pallas kernels: 37.9 us -> 40 us  [the longest x1 11.6 us: call_forward(): pl.pallas_call(forward_kernel, grid=(edges // step,), out_shape=outs, in_...]
    ppermute x1, starting transfers between devices: 2.14 us -> 0.31 us  [body(): lax.ppermute(jnp.concatenate([low[:slots], r_own[slots:], high[:slots]]),...]
    ppermute x1, starting transfers between devices: 3.68 us -> 2.01 us  [body(): lax.ppermute(jnp.concatenate([up[2 * slots:], out_mid[slots:], down[2 * s...]
    all_to_all x1, waiting for transfers between devices: 2.7 us -> 4.26 us  [reduced(): lax.all_to_all(jnp.broadcast_to(own[None], (n_near, part, LAT)), near, 0,...]
  transfers between devices with their start and end apart: 13 -> 13, of which waited for: 7 -> 6; matrix products, arithmetic and copies ran while one was open for 1% -> 1% of each run, Pallas kernels for 10% -> 15%
where the time goes in v2:
time: 107 us; the launch traced here: 106 us
  starting transfers between devices  44.1 us (41%)
  Pallas kernels  40 us (37%)
  waiting for transfers between devices  16.5 us (15%)
  local copies, waits for them, and re-layouts  3.76 us (4%)
  between operations  1.6 us (1%)
    pallas_call x1, Pallas kernels, call_forward(): pl.pallas_call(forward_kernel, grid=(edges // step,), out_shape=outs, in_...  11.6 us
    all_to_all x1, starting transfers between devices, reduced(): got = lax.all_to_all(grads.reshape(n_far, part, LAT), far, 0, 0, tiled=True)  10.4 us
    all_to_all x1, starting transfers between devices, reduced(): lax.all_to_all(jnp.broadcast_to(own[None], (n_far, part, LAT)), far, 0, 0...  9.77 us
    pallas_call x1, Pallas kernels, call_backward(): pl.pallas_call(backward_kernel, grid=(edges // step,), out_shape=(shape((...  9.01 us
    ppermute x1, waiting for transfers between devices, body(): lax.ppermute(jnp.concatenate([low[:slots], r_own[slots:], high[:slots]]),...  7.41 us
    pallas_call x2, Pallas kernels, call_own(): pl.pallas_call(own_kernel, grid=(edges // step,), out_shape=shape((edges,...  5.78 us
    all_to_all x1, starting transfers between devices, reduced(): lax.all_to_all(jnp.broadcast_to(own[None], (n_near, part, LAT)), near, 0,...  5.29 us
    pallas_call x1, Pallas kernels, call_local(): pl.pallas_call(local_kernel, grid=(edges // step,), out_shape=shape((owne...  4.91 us
  transfers between devices with their start and end apart: 13, of which 6 were waited for; matrix products, arithmetic and copies ran while one was open for 1% of the time, Pallas kernels for 15%

profile of v2, /device:TPU:1, one launch (start us, length us, event | category | flops | bytes accessed | tf_op | source)
XLA Modules:
  0.0 106.0 jit_solution(15687875494716349307)
XLA Ops:
  0.6 0.0 copy-start.12
  0.7 0.0 copy-start.14
  0.7 0.1 pad_add_fusion.place_ref.refs_0_
  0.7 0.6 copy-done.12
  1.3 0.0 copy-done.14
  1.4 0.9 copy-done.1
  2.3 1.5 %pick.1 = (bf16[768,128]{1,0:T(8,128)(2,1)S(1)}, bf16[768,128]{1,0:T(8,128)(2,1)S(1)}, bf16[512,128]{1,0:T(8,128)(2,1)S(1)}) custom-call(s32[4]{0:T(128)S(1)} %pad_add_fusion.place_ref.refs_0_, s32[1,8]{1,0:T(1,128)S(1)} %copy-done.14, s32[1,8,256]{2,1,0:T(8,128)S(1)} %copy-done.12, bf16[1024,128]{1,0:T(8,128)(2,1)S(1)} %copy-done.1), custom_call_target="tpu_custom_call" | custom-call | flops 536870912 | bytes 1048576 | tf_op jit(solution)/shard_map/pick/pallas_call | solution.py:445
  3.8 2.8 %collective-permute-start = (bf16[768,128]{1,0:T(8,128)(2,1)S(1)}, bf16[768,128]{1,0:T(8,128)(2,1)S(1)}, u32[]{:S(2)}, u32[]{:S(2)}) collective-permute-start(bf16[768,128]{1,0:T(8,128)(2,1)S(1)} %get-tuple-element.42), channel_id=1, source_target_pairs={{0,8},{8,16},{16,24},{24,32},{32,40},{40,48},{48,56},{56,64},{64,7... | collective-permute-start | bytes 589832 | tf_op jit(solution)/shard_map/ppermute | solution.py:631
  6.5 0.6 collective-permute-start.1
  7.8 0.0 copy-start.11
  7.9 0.7 copy-done.11
  8.6 2.9 %own_rows.3.recvs_ref = bf16[4096,128]{1,0:T(8,128)(2,1)S(1)} custom-call(s32[1]{0:T(128)S(6)} %copy.24.count_ref.refs_0_, s32[1,4096]{1,0:T(1,128)S(1)} %copy-done.11, bf16[1024,128]{1,0:T(8,128)(2,1)S(1)} %copy-done.1), custom_call_target="tpu_custom_call" | custom-call | flops 1073741824 | bytes 2097152 | tf_op jit(solution)/shard_map/own_rows/pallas_call | solution.py:467
  11.5 0.0 copy-done
  11.5 0.0 collective-permute-done.up_ref
  11.5 0.1 collective-permute-done.1.down_ref
  11.7 0.0 copy-start.2
  11.7 2.0 %collective-permute-start.2 = (bf16[800,128]{1,0:T(8,128)(2,1)S(1)}, bf16[800,128]{1,0:T(8,128)(2,1)S(1)}, u32[]{:S(2)}, u32[]{:S(2)}) collective-permute-start(bf16[800,128]{1,0:T(8,128)(2,1)S(1)} %pad_maximum_fusion), channel_id=1, source_target_pairs={{0,1},{1,2},{2,3},{3,4},{4,5},{5,6},{6,7},{7,0},{8,9},{9,10},{10,1... | collective-permute-start | bytes 614408 | tf_op jit(solution)/shard_map/ppermute | solution.py:636
  13.7 0.0 copy-start.4
  13.7 0.0 copy-start.5
  13.7 0.0 copy-start.6
  13.8 0.0 copy-start.7
  13.8 0.0 copy-start.13
  13.8 4.0 %collective-permute-start.3 = (bf16[800,128]{1,0:T(8,128)(2,1)S(1)}, bf16[800,128]{1,0:T(8,128)(2,1)S(1)}, u32[]{:S(2)}, u32[]{:S(2)}) collective-permute-start(bf16[800,128]{1,0:T(8,128)(2,1)S(1)} %pad_maximum_fusion.1), channel_id=1, source_target_pairs={{0,7},{1,0},{2,1},{3,2},{4,3},{5,4},{6,5},{7,6},{8,15},{9,8},{10,9... | collective-permute-start | bytes 614408 | tf_op jit(solution)/shard_map/ppermute | solution.py:643
  17.8 0.0 copy-done.2
  17.8 0.0 copy-done.10
  17.8 2.9 %own_rows.2.sown_ref = bf16[4096,128]{1,0:T(8,128)(2,1)S(1)} custom-call(s32[1]{0:T(128)S(6)} %copy.24.count_ref.refs_0_, s32[1,4096]{1,0:T(1,128)S(1)} %copy-done.10, bf16[1024,128]{1,0:T(8,128)(2,1)S(1)} %copy-done.2), custom_call_target="tpu_custom_call" | custom-call | flops 1073741824 | bytes 2097152 | tf_op jit(solution)/shard_map/own_rows/pallas_call | solution.py:467
  20.7 0.0 copy-start.3
  20.7 0.0 collective-permute-done.2.yup_ref
  20.8 0.0 collective-permute-done.3.ydown_ref
  20.8 0.0 copy-done.4
  20.8 0.0 copy-done.5
  20.8 0.0 copy-done.6
  20.8 0.0 copy-done.7
  20.8 0.0 copy-done.13
  20.8 0.0 copy-start.9
  20.8 11.6 %forward.1 = (bf16[4096,128]{1,0:T(8,128)(2,1)S(1)}, bf16[4096,128]{1,0:T(8,128)(2,1)S(1)}, bf16[4096,128]{1,0:T(8,128)(2,1)S(1)}, bf16[1024,128]{1,0:T(8,128)(2...) custom-call(s32[1]{0:T(128)S(6)} %copy.24.count_ref.refs_0_, ...), custom_call_target="tpu_custom_call" | custom-call | flops 4294967296 | bytes 8388608 | tf_op jit(solution)/shard_map/forward/pallas_call | solution.py:486
  32.4 0.0 collective-permute-start.4
  32.4 2.8 %collective-permute-start.5 = (bf16[64,128]{1,0:T(8,128)(2,1)S(1)}, bf16[64,128]{1,0:T(8,128)(2,1)S(1)}, u32[]{:S(2)}, u32[]{:S(2)}) collective-permute-start(bf16[64,128]{1,0:T(8,128)(2,1)S(1)} %get-tuple-element.54), channel_id=1, source_target_pairs={{0,7},{1,0},{2,1},{3,2},{4,3},{5,4},{6,5},{7,6},{8,15},{9,8},{10,9... | collective-permute-start | bytes 49160 | tf_op jit(solution)/shard_map/ppermute | solution.py:670
  35.3 1.1 %collective-permute-done.4.nlow_ref = bf16[64,128]{1,0:T(8,128)(2,1)S(1)} collective-permute-done((bf16[64,128]{1,0:T(8,128)(2,1)S(1)}, bf16[64,128]{1,0:T(8,128)(2,1)S(1)}, u32[]{:S(2)}, u32[]{:S(2)}) %collective-permute-start.4) | collective-permute-done | bytes 16416 | tf_op jit(solution)/shard_map/ppermute | solution.py:669
  36.4 0.0 collective-permute-done.5.nhigh_ref
  36.4 0.0 copy-done.3
  36.4 0.0 copy-done.9
  36.4 0.0 copy-done.8
  36.4 9.0 %backward.1 = (bf16[128,128]{1,0:T(8,128)(2,1)}, f32[1024,128]{1,0:T(8,128)S(1)}, bf16[4096,128]{1,0:T(8,128)(2,1)S(1)}, bf16[1024,128]{1,0:T(8,128)(2,1)}) custom-call(s32[1,4096]{1,0:T(1,128)S(1)} %copy-done.11, s32[1]{0:T(128)S(6)} %copy.24.count_ref.refs_0_, bf16[4096,128]{1,0:T(8,128)(2,1)S(1)} %get-tuple-element.49.senders_ref, ...), custom_call_target="tpu_custom_call" | custom-call | flops 2147483648 | bytes 8388608 | tf_op jit(solution)/shard_map/backward/pallas_call | solution.py:512
  45.4 10.4 %all-to-all-start = ((bf16[32,32,128]{2,1,0:T(8,128)(2,1)}), bf16[32,32,128]{2,1,0:T(8,128)(2,1)S(1)}, u32[]{:S(2)}, u32[]{:S(2)}) async-start(bf16[32,32,128]{2,1,0:T(8,128)(2,1)} %bitcast.2), calls=%async_computation | async-start | bytes 524288 | tf_op jit(solution)/shard_map/all_to_all | solution.py:435
  55.8 4.8 %ghost_grads.1 = (bf16[768,128]{1,0:T(8,128)(2,1)S(1)}, bf16[768,128]{1,0:T(8,128)(2,1)S(1)}, bf16[512,128]{1,0:T(8,128)(2,1)S(1)}) custom-call(s32[1]{0:T(128)S(6)} %copy.24.count_ref.refs_0_, s32[1,4096]{1,0:T(1,128)S(1)} %copy-done.10, bf16[4096,128]{1,0:T(8,128)(2,1)S(1)} %get-tuple-element.59.refs_2_.dedge_ref, bf16[256,128]{1,0:T(8,128)(2,1)S(1)} %copy-done.5), custom_call_target="tpu_custom_call" | custom-call | flops 2147483648 | bytes 3145728 | tf_op jit(solution)/shard_map/ghost_grads/pallas_call | solution.py:550
  60.6 3.0 %collective-permute-start.6 = (bf16[768,128]{1,0:T(8,128)(2,1)S(1)}, bf16[768,128]{1,0:T(8,128)(2,1)S(1)}, u32[]{:S(2)}, u32[]{:S(2)}) collective-permute-start(bf16[768,128]{1,0:T(8,128)(2,1)S(1)} %get-tuple-element.60), channel_id=1, source_target_pairs={{0,7},{1,0},{2,1},{3,2},{4,3},{5,4},{6,5},{7,6},{8,15},{9,8},{10,9... | collective-permute-start | bytes 589832 | tf_op jit(solution)/shard_map/ppermute | solution.py:698
  63.7 0.0 collective-permute-start.7
  63.7 4.9 %local.1.refs_7_ = f32[1024,128]{1,0:T(8,128)S(1)} custom-call(s32[1]{0:T(128)S(6)} %copy.24.count_ref.refs_0_, s32[1,4096]{1,0:T(1,128)S(1)} %copy-done.10, s32[1,4096]{1,0:T(1,128)S(1)} %copy-done.11, bf16[4096,128]{1,0:T(8,128)(2,1)S(1)} %get-tuple-element.59.refs_2_.dedge_ref, f32[1024,128]{1,0:T(8,128)S(1)} %get-tuple-element.62.dnode_ref, ...), custom_call_target="tpu_custom_call" | custom-call | flops 2147483648 | bytes 3145728 | tf_op jit(solution)/shard_map/local/pallas_call | solution.py:565
  68.6 0.0 collective-permute-done.6.refs_6_
  68.6 2.2 %collective-permute-done.7.refs_5_ = bf16[768,128]{1,0:T(8,128)(2,1)S(1)} collective-permute-done((bf16[768,128]{1,0:T(8,128)(2,1)S(1)}, bf16[768,128]{1,0:T(8,128)(2,1)S(1)}, u32[]{:S(2)}, u32[]{:S(2)}) %collective-permute-start.7) | collective-permute-done | bytes 196640 | tf_op jit(solution)/shard_map/ppermute | solution.py:699
  70.9 0.0 all-to-all-done
  70.9 0.1 reduce_sum.24
  70.9 0.6 broadcast_in_dim.4
  71.6 5.3 %all-to-all-start.1 = ((bf16[8,32,128]{2,1,0:T(8,128)(2,1)}), bf16[8,32,128]{2,1,0:T(8,128)(2,1)S(1)}, u32[]{:S(2)}, u32[]{:S(2)}) async-start(bf16[8,32,128]{2,1,0:T(8,128)(2,1)} %broadcast_in_dim.4), calls=%async_computation.1 | async-start | bytes 131072 | tf_op jit(solution)/shard_map/all_to_all | solution.py:437
  76.9 3.0 %collective-permute-start.8 = (bf16[768,128]{1,0:T(8,128)(2,1)S(1)}, bf16[768,128]{1,0:T(8,128)(2,1)S(1)}, u32[]{:S(2)}, u32[]{:S(2)}) collective-permute-start(bf16[768,128]{1,0:T(8,128)(2,1)S(1)} %pad_maximum_fusion.2), channel_id=1, source_target_pairs={{0,8},{8,16},{16,24},{24,32},{32,40},{40,48},{48,56},{56,64},{64,7... | collective-permute-start | bytes 589832 | tf_op jit(solution)/shard_map/ppermute | solution.py:706
  79.9 4.3 %all-to-all-done.1 = bf16[8,32,128]{2,1,0:T(8,128)(2,1)S(1)} async-done(((bf16[8,32,128]{2,1,0:T(8,128)(2,1)}), bf16[8,32,128]{2,1,0:T(8,128)(2,1)S(1)}, u32[]{:S(2)}, u32[]{:S(2)}) %all-to-all-start.1) | async-done | bytes 65568 | tf_op jit(solution)/shard_map/all_to_all | solution.py:437
  84.2 0.7 broadcast_in_dim.5
  84.9 9.8 %all-to-all-start.2 = ((bf16[32,32,128]{2,1,0:T(8,128)(2,1)}), bf16[32,32,128]{2,1,0:T(8,128)(2,1)S(1)}, u32[]{:S(2)}, u32[]{:S(2)}) async-start(bf16[32,32,128]{2,1,0:T(8,128)(2,1)} %broadcast_in_dim.5), calls=%async_computation.2 | async-start | bytes 524288 | tf_op jit(solution)/shard_map/all_to_all | solution.py:439
  94.7 0.3 collective-permute-start.9
  95.0 0.0 collective-permute-done.8.refs_3_
  95.0 7.4 %collective-permute-done.9.refs_4_ = bf16[768,128]{1,0:T(8,128)(2,1)S(1)} collective-permute-done((bf16[768,128]{1,0:T(8,128)(2,1)S(1)}, bf16[768,128]{1,0:T(8,128)(2,1)S(1)}, u32[]{:S(2)}, u32[]{:S(2)}) %collective-permute-start.9) | collective-permute-done | bytes 196640 | tf_op jit(solution)/shard_map/ppermute | solution.py:703
  102.4 1.2 %all-to-all-done.2 = bf16[32,32,128]{2,1,0:T(8,128)(2,1)S(1)} async-done(((bf16[32,32,128]{2,1,0:T(8,128)(2,1)}), bf16[32,32,128]{2,1,0:T(8,128)(2,1)S(1)}, u32[]{:S(2)}, u32[]{:S(2)}) %all-to-all-start.2) | async-done | bytes 262176 | tf_op jit(solution)/shard_map/all_to_all | solution.py:439
  103.7 2.4 %final.1 = (f32[1024,128]{1,0:T(8,128)}, f32[256,128]{1,0:T(8,128)}, f32[128,128]{1,0:T(8,128)}, f32[256,128]{1,0:T(8,128)}, f32[128,128]{1,0:T(8,128)}, /*index=5*/f32[128,128]{1,0:T(8,128)}, f32[128,128]{1,0:T(8,128)}) custom-call(s32[4]{0:T(128)S(1)} %pad_add_fusion.place_ref.refs_0_, s32[1,8]{1,0:T(1,128)S(1)} %copy-done.14, ...), custom_call_target="tpu_custom_call" | custom-call | flops 536870912 | bytes 2097152 | tf_op jit(solution)/shard_map/final/pallas_call | solution.py:588
  (17 shorter events, 0.1 us)
Async XLA Ops:
  0.6 0.7 copy-start.12
  0.7 0.7 copy-start.14
  1.3 1.0 copy-start.1
  3.8 7.7 %collective-permute-start = (bf16[768,128]{1,0:T(8,128)(2,1)S(1)}, bf16[768,128]{1,0:T(8,128)(2,1)S(1)}, u32[]{:S(2)}, u32[]{:S(2)}) collective-permute-start(bf16[768,128]{1,0:T(8,128)(2,1)S(1)} %get-tuple-element.42), channel_id=1, source_target_pairs={{0,8},{8,16},{16,24},{24,32},{32,40},{40,48},{48,56},{56,64},{64,7... | collective-permute-start | bytes 589832 | tf_op jit(solution)/shard_map/ppermute | solution.py:631
  6.5 5.1 %collective-permute-start.1 = (bf16[768,128]{1,0:T(8,128)(2,1)S(1)}, bf16[768,128]{1,0:T(8,128)(2,1)S(1)}, u32[]{:S(2)}, u32[]{:S(2)}) collective-permute-start(bf16[768,128]{1,0:T(8,128)(2,1)S(1)} %get-tuple-element.43), channel_id=1, source_target_pairs={{0,248},{8,0},{16,8},{24,16},{32,24},{40,32},{48,40},{56,48},{64,5... | collective-permute-start | bytes 589832 | tf_op jit(solution)/shard_map/ppermute | solution.py:632
  7.8 0.7 copy-start.11
  8.6 2.9 %copy-start = (bf16[128,128]{1,0:T(8,128)(2,1)S(1)}, bf16[128,128]{1,0:T(8,128)(2,1)}, u32[]{:S(2)}) copy-start(bf16[128,128]{1,0:T(8,128)(2,1)} %dcoarse_ref.1) | copy-start | bytes 98308
  11.7 6.2 %copy-start.2 = (bf16[1024,128]{1,0:T(8,128)(2,1)S(1)}, bf16[1024,128]{1,0:T(8,128)(2,1)}, u32[]{:S(2)}) copy-start(bf16[1024,128]{1,0:T(8,128)(2,1)} %nodes_ref.7) | copy-start | bytes 786436
  11.7 9.1 %collective-permute-start.2 = (bf16[800,128]{1,0:T(8,128)(2,1)S(1)}, bf16[800,128]{1,0:T(8,128)(2,1)S(1)}, u32[]{:S(2)}, u32[]{:S(2)}) collective-permute-start(bf16[800,128]{1,0:T(8,128)(2,1)S(1)} %pad_maximum_fusion), channel_id=1, source_target_pairs={{0,1},{1,2},{2,3},{3,4},{4,5},{5,6},{6,7},{7,0},{8,9},{9,10},{10,1... | collective-permute-start | bytes 614408 | tf_op jit(solution)/shard_map/ppermute | solution.py:636
  13.7 4.1 %copy-start.10 = (s32[1,4096]{1,0:T(1,128)S(1)}, s32[1,4096]{1,0:T(1,128)}, u32[]{:S(2)}) copy-start(s32[1,4096]{1,0:T(1,128)} %send_ref.3) | copy-start | bytes 49156
  13.7 7.1 %copy-start.4 = (bf16[256,128]{1,0:T(8,128)(2,1)S(1)}, bf16[256,128]{1,0:T(8,128)(2,1)}, u32[]{:S(2)}) copy-start(bf16[256,128]{1,0:T(8,128)(2,1)} %wni_ref.3) | copy-start | bytes 196612
  13.7 7.1 %copy-start.5 = (bf16[256,128]{1,0:T(8,128)(2,1)S(1)}, bf16[256,128]{1,0:T(8,128)(2,1)}, u32[]{:S(2)}) copy-start(bf16[256,128]{1,0:T(8,128)(2,1)} %wei_ref.5) | copy-start | bytes 196612
  13.7 7.1 %copy-start.6 = (bf16[128,128]{1,0:T(8,128)(2,1)S(1)}, bf16[128,128]{1,0:T(8,128)(2,1)}, u32[]{:S(2)}) copy-start(bf16[128,128]{1,0:T(8,128)(2,1)} %weo_ref.3) | copy-start | bytes 98308
  13.8 7.1 %copy-start.7 = (bf16[128,128]{1,0:T(8,128)(2,1)S(1)}, bf16[128,128]{1,0:T(8,128)(2,1)}, u32[]{:S(2)}) copy-start(bf16[128,128]{1,0:T(8,128)(2,1)} %wno_ref.3) | copy-start | bytes 98308
  13.8 7.1 %copy-start.13 = (s32[1,1024]{1,0:T(1,128)S(1)}, s32[1,1024]{1,0:T(1,128)}, u32[]{:S(2)}) copy-start(s32[1,1024]{1,0:T(1,128)} %pool_ref.3) | copy-start | bytes 12292
  13.8 7.0 %collective-permute-start.3 = (bf16[800,128]{1,0:T(8,128)(2,1)S(1)}, bf16[800,128]{1,0:T(8,128)(2,1)S(1)}, u32[]{:S(2)}, u32[]{:S(2)}) collective-permute-start(bf16[800,128]{1,0:T(8,128)(2,1)S(1)} %pad_maximum_fusion.1), channel_id=1, source_target_pairs={{0,7},{1,0},{2,1},{3,2},{4,3},{5,4},{6,5},{7,6},{8,15},{9,8},{10,9... | collective-permute-start | bytes 614408 | tf_op jit(solution)/shard_map/ppermute | solution.py:643
  20.7 15.7 %copy-start.3 = (bf16[1024,128]{1,0:T(8,128)(2,1)S(1)}, bf16[1024,128]{1,0:T(8,128)(2,1)}, u32[]{:S(2)}) copy-start(bf16[1024,128]{1,0:T(8,128)(2,1)} %dfine_ref.1) | copy-start | bytes 786436
  20.8 15.6 %copy-start.9 = (bf16[128,128]{1,0:T(8,128)(2,1)S(1)}, bf16[128,128]{1,0:T(8,128)(2,1)}, u32[]{:S(2)}) copy-start(bf16[128,128]{1,0:T(8,128)(2,1)} %wco_ref.1) | copy-start | bytes 98308
  32.4 4.0 %copy-start.8 = (bf16[128,128]{1,0:T(8,128)(2,1)S(1)}, bf16[128,128]{1,0:T(8,128)(2,1)}, u32[]{:S(2)}) copy-start(bf16[128,128]{1,0:T(8,128)(2,1)} %wci_ref.1) | copy-start | bytes 98308
  32.4 4.0 %collective-permute-start.4 = (bf16[64,128]{1,0:T(8,128)(2,1)S(1)}, bf16[64,128]{1,0:T(8,128)(2,1)S(1)}, u32[]{:S(2)}, u32[]{:S(2)}) collective-permute-start(bf16[64,128]{1,0:T(8,128)(2,1)S(1)} %get-tuple-element.53), channel_id=1, source_target_pairs={{0,1},{1,2},{2,3},{3,4},{4,5},{5,6},{6,7},{7,0},{8,9},{9,10},{10,1... | collective-permute-start | bytes 49160 | tf_op jit(solution)/shard_map/ppermute | solution.py:669
  32.4 4.0 %collective-permute-start.5 = (bf16[64,128]{1,0:T(8,128)(2,1)S(1)}, bf16[64,128]{1,0:T(8,128)(2,1)S(1)}, u32[]{:S(2)}, u32[]{:S(2)}) collective-permute-start(bf16[64,128]{1,0:T(8,128)(2,1)S(1)} %get-tuple-element.54), channel_id=1, source_target_pairs={{0,7},{1,0},{2,1},{3,2},{4,3},{5,4},{6,5},{7,6},{8,15},{9,8},{10,9... | collective-permute-start | bytes 49160 | tf_op jit(solution)/shard_map/ppermute | solution.py:670
  45.4 25.4 %all-to-all-start = ((bf16[32,32,128]{2,1,0:T(8,128)(2,1)}), bf16[32,32,128]{2,1,0:T(8,128)(2,1)S(1)}, u32[]{:S(2)}, u32[]{:S(2)}) async-start(bf16[32,32,128]{2,1,0:T(8,128)(2,1)} %bitcast.2), calls=%async_computation | async-start | bytes 524288 | tf_op jit(solution)/shard_map/all_to_all | solution.py:435
  60.6 7.9 %collective-permute-start.6 = (bf16[768,128]{1,0:T(8,128)(2,1)S(1)}, bf16[768,128]{1,0:T(8,128)(2,1)S(1)}, u32[]{:S(2)}, u32[]{:S(2)}) collective-permute-start(bf16[768,128]{1,0:T(8,128)(2,1)S(1)} %get-tuple-element.60), channel_id=1, source_target_pairs={{0,7},{1,0},{2,1},{3,2},{4,3},{5,4},{6,5},{7,6},{8,15},{9,8},{10,9... | collective-permute-start | bytes 589832 | tf_op jit(solution)/shard_map/ppermute | solution.py:698
  63.7 7.2 %collective-permute-start.7 = (bf16[768,128]{1,0:T(8,128)(2,1)S(1)}, bf16[768,128]{1,0:T(8,128)(2,1)S(1)}, u32[]{:S(2)}, u32[]{:S(2)}) collective-permute-start(bf16[768,128]{1,0:T(8,128)(2,1)S(1)} %get-tuple-element.61), channel_id=1, source_target_pairs={{0,1},{1,2},{2,3},{3,4},{4,5},{5,6},{6,7},{7,0},{8,9},{9,10},{10,1... | collective-permute-start | bytes 589832 | tf_op jit(solution)/shard_map/ppermute | solution.py:699
  71.6 12.6 %all-to-all-start.1 = ((bf16[8,32,128]{2,1,0:T(8,128)(2,1)}), bf16[8,32,128]{2,1,0:T(8,128)(2,1)S(1)}, u32[]{:S(2)}, u32[]{:S(2)}) async-start(bf16[8,32,128]{2,1,0:T(8,128)(2,1)} %broadcast_in_dim.4), calls=%async_computation.1 | async-start | bytes 131072 | tf_op jit(solution)/shard_map/all_to_all | solution.py:437
  76.9 18.1 %collective-permute-start.8 = (bf16[768,128]{1,0:T(8,128)(2,1)S(1)}, bf16[768,128]{1,0:T(8,128)(2,1)S(1)}, u32[]{:S(2)}, u32[]{:S(2)}) collective-permute-start(bf16[768,128]{1,0:T(8,128)(2,1)S(1)} %pad_maximum_fusion.2), channel_id=1, source_target_pairs={{0,8},{8,16},{16,24},{24,32},{32,40},{40,48},{48,56},{56,64},{64,7... | collective-permute-start | bytes 589832 | tf_op jit(solution)/shard_map/ppermute | solution.py:706
  84.9 18.8 %all-to-all-start.2 = ((bf16[32,32,128]{2,1,0:T(8,128)(2,1)}), bf16[32,32,128]{2,1,0:T(8,128)(2,1)S(1)}, u32[]{:S(2)}, u32[]{:S(2)}) async-start(bf16[32,32,128]{2,1,0:T(8,128)(2,1)} %broadcast_in_dim.5), calls=%async_computation.2 | async-start | bytes 524288 | tf_op jit(solution)/shard_map/all_to_all | solution.py:439
  94.7 7.7 %collective-permute-start.9 = (bf16[768,128]{1,0:T(8,128)(2,1)S(1)}, bf16[768,128]{1,0:T(8,128)(2,1)S(1)}, u32[]{:S(2)}, u32[]{:S(2)}) collective-permute-start(bf16[768,128]{1,0:T(8,128)(2,1)S(1)} %pad_maximum_fusion.3), channel_id=1, source_target_pairs={{0,248},{8,0},{16,8},{24,16},{32,24},{40,32},{48,40},{56,48},{64,5... | collective-permute-start | bytes 589832 | tf_op jit(solution)/shard_map/ppermute | solution.py:703

commit v3 on v2

--- a/solution.py
+++ b/solution.py
@@ -10,7 +10,7 @@
 LAT = 128
 LOW = 512
 BITS = 9
-OWN_STEP = FWD_STEP = BWD_STEP = GHOST_STEP = LOCAL_STEP = 512
+OWN_STEP = FWD_STEP = BWD_STEP = GHOST_STEP = LOCAL_STEP = 4096
 GX_GY = ("gx_0", "gx_1", "gx_2", "gy")
 GX = ("gx_0", "gx_1", "gx_2")
 ACROSS = (-1, -1, -1, 0, 0, 1, 1, 1)
@@ -47,25 +47,28 @@
     parts = []
     for j in range(row.shape[1] // LAT):
         parts.append(jnp.broadcast_to(row[:, j * LAT : (j + 1) * LAT], (LAT, LAT)).T)
-    return jnp.concatenate(parts, axis=0)
+    return jnp.concatenate(parts, axis=0).astype(jnp.int16)
 
 
 def one_hot(col, rows):
-    lanes = lax.broadcasted_iota(jnp.int32, col.shape, 1)
+    lanes = lax.broadcasted_iota(jnp.int16, col.shape, 1)
+    one, zero = jnp.ones((), bf16), jnp.zeros((), bf16)
     return jnp.concatenate(
-        [(col == lanes + j * LAT).astype(f32).astype(bf16) for j in range(rows // LAT)], axis=1
+        [jnp.where(col == lanes + j * LAT, one, zero) for j in range(rows // LAT)], axis=1
     )
 
 
 def one_hot_t(row, rows):
-    ids = lax.broadcasted_iota(jnp.int32, (rows, row.shape[1]), 0)
-    return (ids == row).astype(f32).astype(bf16)
+    ids = lax.broadcasted_iota(jnp.int16, (rows, row.shape[1]), 0)
+    col = jnp.broadcast_to(row, (16, row.shape[1])).astype(jnp.int16)
+    col = jnp.concatenate([col] * (rows // 16), axis=0)
+    return jnp.where(ids == col, jnp.ones((), bf16), jnp.zeros((), bf16))
 
 
 def take(col, table):
-    got = mm(one_hot(col & (LOW - 1), LOW), table)
+    got = mm(one_hot(col & (LOW - 1), LOW), table).astype(bf16)
     group = col >> BITS
-    total = jnp.zeros((col.shape[0], LAT), f32)
+    total = jnp.zeros((col.shape[0], LAT), bf16)
     for i in range(table.shape[1] // LAT):
         total = jnp.where(group == i, got[:, i * LAT : (i + 1) * LAT], total)
     return total
@@ -73,14 +76,13 @@
 
 def put(row, col, values, groups):
     group = col >> BITS
-    spread = jnp.concatenate(
-        [jnp.where(group == i, values, 0.0).astype(bf16) for i in range(groups)], axis=1
-    )
+    zero = jnp.zeros((), bf16)
+    spread = jnp.concatenate([jnp.where(group == i, values, zero) for i in range(groups)], axis=1)
     return mm(one_hot_t(row & (LOW - 1), LOW), spread)
 
 
 def sigmoid(v):
-    return 1.0 / (1.0 + jnp.exp(-v))
+    return 0.5 + 0.5 * jnp.tanh(0.5 * v)
 
 
 def act_and_slope(v):
@@ -100,7 +102,7 @@
     return jnp.where(inside, count_ref[0, k], 0)
 
 
-def pick_kernel(place_ref, count_ref, rows_hbm, nodes_hbm, up_ref, down_ref, mid_ref, rows, nodes, sems):
+def pick_kernel(place_ref, count_ref, rows_hbm, nodes_hbm, up_ref, down_ref, mid_ref, cols_ref, rows, nodes, sems):
     copies = (
         pltpu.make_async_copy(nodes_hbm, nodes, sems.at[0]),
         pltpu.make_async_copy(rows_hbm, rows, sems.at[1]),
@@ -113,7 +115,9 @@
     slots = rows.shape[2]
     for k in range(8):
         row = live_row(rows[0, k : k + 1, :], 0, live_slots(place_ref, count_ref, k))
-        got = take(in_columns(row), table).astype(bf16)
+        col = in_columns(row)
+        cols_ref[k * slots : (k + 1) * slots, :] = col
+        got = take(col, table)
         if k < 3:
             down_ref[k * slots : (k + 1) * slots, :] = got
         elif k < 5:
@@ -122,17 +126,19 @@
             up_ref[(k - 5) * slots : (k - 4) * slots, :] = got
 
 
-def own_kernel(count_ref, index_ref, nodes_ref, out_ref):
+def own_kernel(count_ref, index_ref, nodes_ref, out_ref, cols_ref):
     table = wide(nodes_ref[...])
     first = pl.program_id(0) * index_ref.shape[1]
-    row = live_row(index_ref[...], first, count_ref[0])
-    out_ref[...] = take(in_columns(row), table).astype(bf16)
+    col = in_columns(live_row(index_ref[...], first, count_ref[0]))
+    cols_ref[...] = col
+    out_ref[...] = take(col, table)
 
 
 def forward_kernel(
     count_ref,
-    send_ref,
     recv_ref,
+    scol_ref,
+    rcol_ref,
     sown_ref,
     recvs_ref,
     up_ref,
@@ -180,20 +186,17 @@
             table[(k % 2) * slots : (k % 2 + 1) * slots, (k // 2) * LAT : (k // 2 + 1) * LAT] = blocks[k]
         acc[...] = jnp.zeros_like(acc)
 
-    first = step * send_ref.shape[1]
-    count = count_ref[0]
     owned = nodes_ref.shape[0]
-    send = in_columns(live_row(send_ref[...], first, count)) - owned
-    senders = (take(send, table[...]) + sown_ref[...].astype(f32)).astype(bf16)
+    senders = take(scol_ref[...] - owned, table[...]) + sown_ref[...]
     senders_ref[...] = senders
     pre = mm(jnp.concatenate([senders, recvs_ref[...]], axis=1), wei_ref[...])
     act, slope = act_and_slope(pre)
     act = act.astype(bf16)
     act_ref[...] = act
     slope_ref[...] = slope.astype(bf16)
-    message = mm(act, weo_ref[...]).astype(bf16).astype(f32)
-    recv = live_row(recv_ref[...], first, count)
-    acc[...] += put(recv, in_columns(recv), message, owned // LOW)
+    message = mm(act, weo_ref[...]).astype(bf16)
+    recv = live_row(recv_ref[...], step * recv_ref.shape[1], count_ref[0])
+    acc[...] += put(recv, rcol_ref[...], message, owned // LOW)
 
     @pl.when(step == pl.num_programs(0) - 1)
     def _():
@@ -215,8 +218,7 @@
 
 
 def backward_kernel(
-    recv_ref,
-    count_ref,
+    rcol_ref,
     senders_ref,
     recvs_ref,
     act_ref,
@@ -287,10 +289,7 @@
         grads_ref[6 * LAT : 7 * LAT, :] = g_ci.astype(bf16)
         grads_ref[7 * LAT :, :] = g_co.astype(bf16)
 
-    first = step * recv_ref.shape[1]
-    count = count_ref[0]
-    recv = in_columns(live_row(recv_ref[...], first, count))
-    d_message = take(recv, table[...]).astype(bf16)
+    d_message = take(rcol_ref[...], table[...])
     d_pre = (mm_nt(d_message, weo_ref[...]) * slope_ref[...].astype(f32)).astype(bf16)
     dedge_ref[...] = d_pre
     gacc[: 2 * LAT, :] += mm_tn(jnp.concatenate([senders_ref[...], recvs_ref[...]], axis=1), d_pre)
@@ -302,7 +301,7 @@
 
 
 def ghost_kernel(
-    count_ref, send_ref, dedge_ref, wei_ref, rdown_ref, rup_ref, rown_ref, acc, *, owned
+    count_ref, send_ref, scol_ref, dedge_ref, wei_ref, rdown_ref, rup_ref, rown_ref, acc, *, owned
 ):
     step = pl.program_id(0)
 
@@ -312,7 +311,7 @@
 
     first = step * send_ref.shape[1]
     send = live_row(send_ref[...], first, count_ref[0]) - owned
-    acc[...] += put(send, in_columns(send), dedge_ref[...].astype(f32), 4)
+    acc[...] += put(send, scol_ref[...] - owned, dedge_ref[...], 4)
 
     @pl.when(step == pl.num_programs(0) - 1)
     def _():
@@ -333,7 +332,7 @@
             ref[i * slots : (i + 1) * slots, :] = ghosts[place * slots : (place + 1) * slots]
 
 
-def local_kernel(count_ref, send_ref, recv_ref, dedge_ref, dnode_ref, wei_ref, out_ref, acc_s, acc_r):
+def local_kernel(count_ref, send_ref, recv_ref, scol_ref, rcol_ref, dedge_ref, dnode_ref, wei_ref, out_ref, acc_s, acc_r):
     step = pl.program_id(0)
 
     @pl.when(step == 0)
@@ -344,11 +343,11 @@
     first = step * send_ref.shape[1]
     count = count_ref[0]
     groups = out_ref.shape[0] // LOW
-    d_pre = dedge_ref[...].astype(f32)
+    d_pre = dedge_ref[...]
     send = live_row(send_ref[...], first, count)
     recv = live_row(recv_ref[...], first, count)
-    acc_s[...] += put(send, in_columns(send), d_pre, groups)
-    acc_r[...] += put(recv, in_columns(recv), d_pre, groups)
+    acc_s[...] += put(send, scol_ref[...], d_pre, groups)
+    acc_r[...] += put(recv, rcol_ref[...], d_pre, groups)
 
     @pl.when(step == pl.num_programs(0) - 1)
     def _():
@@ -364,6 +363,7 @@
     place_ref,
     count_ref,
     rows_ref,
+    cols_ref,
     down_ref,
     up_ref,
     mid_low_ref,
@@ -378,6 +378,7 @@
     total = jnp.zeros((LOW, groups * LAT), f32)
     for k in range(8):
         row = live_row(rows_ref[0, k : k + 1, :], 0, live_slots(place_ref, count_ref, k))
+        col = cols_ref[k * slots : (k + 1) * slots, :]
         if k < 3:
             got = down_ref[k * slots : (k + 1) * slots, :]
         elif k == 3:
@@ -386,7 +387,7 @@
             got = mid_high_ref[slots : 2 * slots, :]
         else:
             got = up_ref[(k - 5) * slots : (k - 4) * slots, :]
-        total = total + put(row, in_columns(row), got.astype(f32), groups)
+        total = total + put(row, col, got, groups)
     out_ref[...] = part_ref[...] + tall(total)
     first = 0
     for ref in grad_refs:
@@ -448,6 +449,7 @@
             shape((3 * slots, LAT), bf16),
             shape((3 * slots, LAT), bf16),
             shape((2 * slots, LAT), bf16),
+            shape((8 * slots, LAT), jnp.int16),
         ),
         in_specs=[scalars(), scalars(), hbm(), hbm()],
         scratch_shapes=[
@@ -467,17 +469,17 @@
     return pl.pallas_call(
         own_kernel,
         grid=(edges // step,),
-        out_shape=shape((edges, LAT), bf16),
+        out_shape=(shape((edges, LAT), bf16), shape((edges, LAT), jnp.int16)),
         in_specs=[scalars(), edge_row(step), whole(nodes.shape)],
-        out_specs=edge_block(step),
+        out_specs=(edge_block(step), edge_block(step)),
         compiler_params=params(32),
         cost_estimate=cost(2 * 4096 * 512 * 256, 2 * MIB),
         name="own_rows",
     )(edge_count, index, nodes)
 
 
-def call_forward(edge_count, send, recv, sown, recvs, up, down, yup, ydown, nodes, pool, rows, *weights):
-    edges, owned, step = send.shape[1], nodes.shape[0], FWD_STEP
+def call_forward(edge_count, recv, scol, rcol, sown, recvs, up, down, yup, ydown, nodes, pool, rows, *weights):
+    edges, owned, step = recv.shape[1], nodes.shape[0], FWD_STEP
     edge16 = shape((edges, LAT), bf16)
     node16 = shape((owned, LAT), bf16)
     band = shape((2 * BAND, LAT), bf16)
@@ -490,7 +492,8 @@
         in_specs=[
             scalars(),
             edge_row(step),
-            edge_row(step),
+            edge_block(step),
+            edge_block(step),
             edge_block(step),
             edge_block(step),
             *(whole(x.shape) for x in plain),
@@ -503,11 +506,11 @@
         compiler_params=params(40),
         cost_estimate=cost(2 * 4096 * 512 * 1024, 8 * MIB),
         name="forward",
-    )(edge_count, send, recv, sown, recvs, *plain)
-
-
-def call_backward(recv, edge_count, edge_arrays, plain):
-    edges, step = recv.shape[1], BWD_STEP
+    )(edge_count, recv, scol, rcol, sown, recvs, *plain)
+
+
+def call_backward(edge_arrays, plain):
+    edges, step = edge_arrays[0].shape[0], BWD_STEP
     owned, coarse = plain[8].shape[0], plain[5].shape[0]
     return pl.pallas_call(
         backward_kernel,
@@ -519,8 +522,6 @@
             shape((8 * LAT, LAT), bf16),
         ),
         in_specs=[
-            edge_row(step),
-            scalars(),
             *(edge_block(step) for _ in edge_arrays),
             *(whole(x.shape) for x in plain),
         ],
@@ -537,10 +538,10 @@
         compiler_params=params(40),
         cost_estimate=cost(2 * 4096 * 512 * 512, 8 * MIB),
         name="backward",
-    )(recv, edge_count, *edge_arrays, *plain)
-
-
-def call_ghost(edge_count, send, d_edge, w_edge_in, owned, slots):
+    )(*edge_arrays, *plain)
+
+
+def call_ghost(edge_count, send, scol, d_edge, w_edge_in, owned, slots):
     edges, step = send.shape[1], GHOST_STEP
     outs = (
         shape((3 * slots, LAT), bf16),
@@ -551,16 +552,22 @@
         lambda *refs: ghost_kernel(*refs, owned=owned),
         grid=(edges // step,),
         out_shape=outs,
-        in_specs=[scalars(), edge_row(step), edge_block(step), whole(w_edge_in.shape)],
+        in_specs=[
+            scalars(),
+            edge_row(step),
+            edge_block(step),
+            edge_block(step),
+            whole(w_edge_in.shape),
+        ],
         out_specs=tuple(whole(x.shape) for x in outs),
         scratch_shapes=[pltpu.VMEM((LOW, 4 * LAT), f32)],
         compiler_params=params(32),
         cost_estimate=cost(2 * 4096 * 512 * 512, 3 * MIB),
         name="ghost_grads",
-    )(edge_count, send, d_edge, w_edge_in)
-
-
-def call_local(edge_count, send, recv, d_edge, d_node, w_edge_in):
+    )(edge_count, send, scol, d_edge, w_edge_in)
+
+
+def call_local(edge_count, send, recv, scol, rcol, d_edge, d_node, w_edge_in):
     edges, step, owned = send.shape[1], LOCAL_STEP, d_node.shape[0]
     return pl.pallas_call(
         local_kernel,
@@ -571,6 +578,8 @@
             edge_row(step),
             edge_row(step),
             edge_block(step),
+            edge_block(step),
+            edge_block(step),
             whole((owned, LAT)),
             whole(w_edge_in.shape),
         ],
@@ -579,11 +588,11 @@
         compiler_params=params(32),
         cost_estimate=cost(2 * 2 * 4096 * 512 * 256, 3 * MIB),
         name="local",
-    )(edge_count, send, recv, d_edge, d_node, w_edge_in)
+    )(edge_count, send, recv, scol, rcol, d_edge, d_node, w_edge_in)
 
 
 def call_final(scale, place, ghost_count, ghost_rows, *arrays):
-    owned = arrays[4].shape[0]
+    owned = arrays[5].shape[0]
     heights = (2 * LAT, LAT, 2 * LAT, LAT, LAT, LAT)
     return pl.pallas_call(
         lambda *refs: final_kernel(scale, *refs),
@@ -627,10 +636,10 @@
     n_gx, n_gy = lax.axis_size(GX), lax.axis_size("gy")
     place = jnp.stack([lax.axis_index(GX), lax.axis_index("gy"), n_gx, n_gy]).astype(jnp.int32)
 
-    out_up, out_down, out_mid = call_pick(place, ghost_count, ghost_rows, nodes)
+    out_up, out_down, out_mid, gcol = call_pick(place, ghost_count, ghost_rows, nodes)
     up = lax.ppermute(out_up, GX, ring(n_gx, 1))
     down = lax.ppermute(out_down, GX, ring(n_gx, -1))
-    recvs = call_own(edge_count, edge_recv, nodes)
+    recvs, rcol = call_own(edge_count, edge_recv, nodes)
     up, down, recvs = lax.optimization_barrier((up, down, recvs))
 
     yup = lax.ppermute(
@@ -645,12 +654,13 @@
         "gy",
         ring(n_gy, -1),
     )
-    sown = call_own(edge_count, edge_send, nodes)
+    sown, scol = call_own(edge_count, edge_send, nodes)
 
     (senders, act, slope, fine_out, summed, nact, nslope, window, wlow, whigh) = call_forward(
         edge_count,
-        edge_send,
         edge_recv,
+        scol,
+        rcol,
         sown,
         recvs,
         up,
@@ -670,9 +680,7 @@
     nhigh = lax.ppermute(wlow, "gy", ring(n_gy, -1))
 
     coarse_out, d_node, d_edge, grads = call_backward(
-        edge_recv,
-        edge_count,
-        (senders, recvs, act, slope),
+        (rcol, senders, recvs, act, slope),
         (
             window,
             nlow,
@@ -694,10 +702,12 @@
             w_coarse_out,
         ),
     )
-    r_down, r_up, r_own = call_ghost(edge_count, edge_send, d_edge, w_edge_in, owned, slots)
+    r_down, r_up, r_own = call_ghost(edge_count, edge_send, scol, d_edge, w_edge_in, owned, slots)
     high = lax.ppermute(r_down, "gy", ring(n_gy, -1))
     low = lax.ppermute(r_up, "gy", ring(n_gy, 1))
-    d_own = call_local(edge_count, edge_send, edge_recv, d_edge, d_node, w_edge_in)
+    d_own = call_local(
+        edge_count, edge_send, edge_recv, scol, rcol, d_edge, d_node, w_edge_in
+    )
     high, low, d_own = lax.optimization_barrier((high, low, d_own))
 
     ret_up = lax.ppermute(
@@ -710,7 +720,7 @@
     sums = reduced(grads)
     grad_scale = 1.0 / (owned * n_gx * n_gy) ** 0.5
     grad_nodes, *scaled = call_final(
-        grad_scale, place, ghost_count, ghost_rows, ret_down, ret_up, low, high, d_own, sums
+        grad_scale, place, ghost_count, ghost_rows, gcol, ret_down, ret_up, low, high, d_own, sums
     )
     return (fine_out, coarse_out, grad_nodes, *scaled)
 

time: 107 us -> 97.7 us (0.913)
  Pallas kernels: 40 us -> 25.6 us
  local copies, waits for them, and re-layouts: 3.76 us -> 7.26 us
  waiting for transfers between devices: 16.5 us -> 18.5 us
    pallas_call x1, Pallas kernels: 11.6 us -> 7.91 us  [call_forward(): pl.pallas_call(forward_kernel, grid=(edges // step,), out_shape=outs, in_...]
    unnamed x30 -> x42, local copies, waits for them, and re-layouts: 2.31 us -> 5.81 us
    pallas_call x2, Pallas kernels: 5.78 us -> 2.63 us  [call_own(): pl.pallas_call(own_kernel, grid=(edges // step,), out_shape=(shape((edges...]
    pallas_call x1, Pallas kernels: 9.01 us -> 6 us  [call_backward(): pl.pallas_call(backward_kernel, grid=(edges // step,), out_shape=(shape((...]
    pallas_call x1, Pallas kernels: 4.91 us -> 2.7 us  [call_local(): pl.pallas_call(local_kernel, grid=(edges // step,), out_shape=shape((owne...]
    pallas_call x1, Pallas kernels: 4.83 us -> 2.75 us  [call_ghost(): pl.pallas_call(lambda *refs: ghost_kernel(*refs, owned=owned), grid=(edge...]
    ppermute x1, waiting for transfers between devices: 0.04 us -> 1.84 us  [body(): lax.ppermute(jnp.concatenate([up[2 * slots:], out_mid[slots:], down[2 * s...]
    ppermute x1, waiting for transfers between devices: 0.14 us -> 1.72 us  [body(): down = lax.ppermute(out_down, GX, ring(n_gx, -1))]
  transfers between devices with their start and end apart: 13 -> 13, of which waited for: 6 -> 7; matrix products, arithmetic and copies ran while one was open for 1% -> 1% of each run, Pallas kernels for 15% -> 5%
where the time goes in v3:
time: 97.7 us; the launch traced here: 97.1 us
  starting transfers between devices  43.9 us (45%)
  Pallas kernels  25.6 us (26%)
  waiting for transfers between devices  18.5 us (19%)
  local copies, waits for them, and re-layouts  7.26 us (7%)
  between operations  1.63 us (2%)
    all_to_all x1, starting transfers between devices, reduced(): lax.all_to_all(jnp.broadcast_to(own[None], (n_far, part, LAT)), far, 0, 0...  9.77 us
    all_to_all x1, starting transfers between devices, reduced(): got = lax.all_to_all(grads.reshape(n_far, part, LAT), far, 0, 0, tiled=True)  9.43 us
    pallas_call x1, Pallas kernels, call_forward(): pl.pallas_call(forward_kernel, grid=(edges // step,), out_shape=outs, in_...  7.91 us
    ppermute x1, waiting for transfers between devices, body(): lax.ppermute(jnp.concatenate([low[:slots], r_own[slots:], high[:slots]]),...  7.41 us
    pallas_call x1, Pallas kernels, call_backward(): pl.pallas_call(backward_kernel, grid=(edges // step,), out_shape=(shape((...  6 us
    all_to_all x1, starting transfers between devices, reduced(): lax.all_to_all(jnp.broadcast_to(own[None], (n_near, part, LAT)), near, 0,...  5.99 us
    unnamed x42, local copies, waits for them, and re-layouts  5.81 us
    all_to_all x1, waiting for transfers between devices, reduced(): lax.all_to_all(jnp.broadcast_to(own[None], (n_near, part, LAT)), near, 0,...  4.26 us
  transfers between devices with their start and end apart: 13, of which 7 were waited for; matrix products, arithmetic and copies ran while one was open for 1% of the time, Pallas kernels for 5%

profile of v3, /device:TPU:1, one launch (start us, length us, event | category | flops | bytes accessed | tf_op | source)
XLA Modules:
  0.0 97.1 jit_solution(1607873273683735151)
XLA Ops:
  0.6 0.0 copy-start
  0.7 0.0 copy-start.2
  0.7 0.1 pad_add_fusion.place_ref.refs_0_
  0.7 0.6 copy-done
  1.3 0.0 copy-done.2
  1.4 0.9 copy-done.3
  2.3 1.4 %pick.1 = (bf16[768,128]{1,0:T(8,128)(2,1)S(1)}, bf16[768,128]{1,0:T(8,128)(2,1)S(1)}, bf16[512,128]{1,0:T(8,128)(2,1)S(1)}, s16[2048,128]{1,0:T(8,128)(2,1)S(1)}) custom-call(s32[4]{0:T(128)S(1)} %pad_add_fusion.place_ref.refs_0_, s32[1,8]{1,0:T(1,128)S(1)} %copy-done.2, s32[1,8,256]{2,1,0:T(8,128)S(1)} %copy-done, bf16[1024,128]{1,0:T(8,128)(2,1)S(1)} %copy-done.3), custom_call_target="tpu_custom_call" | custom-call | flops 536870912 | bytes 1048576 | tf_op jit(solution)/shard_map/pick/pallas_call | solution.py:446
  3.7 2.8 %collective-permute-start = (bf16[768,128]{1,0:T(8,128)(2,1)S(1)}, bf16[768,128]{1,0:T(8,128)(2,1)S(1)}, u32[]{:S(2)}, u32[]{:S(2)}) collective-permute-start(bf16[768,128]{1,0:T(8,128)(2,1)S(1)} %get-tuple-element.50), channel_id=1, source_target_pairs={{0,8},{8,16},{16,24},{24,32},{32,40},{40,48},{48,56},{56,64},{64,7... | collective-permute-start | bytes 589832 | tf_op jit(solution)/shard_map/ppermute | solution.py:640
  6.4 0.7 collective-permute-start.1
  7.8 0.0 copy-start.12
  7.8 0.7 copy-done.12
  8.5 1.3 %own_rows.3 = (bf16[4096,128]{1,0:T(8,128)(2,1)S(1)}, s16[4096,128]{1,0:T(8,128)(2,1)S(1)}) custom-call(s32[1]{0:T(128)S(6)} %copy.24.count_ref.refs_0_, s32[1,4096]{1,0:T(1,128)S(1)} %copy-done.12, bf16[1024,128]{1,0:T(8,128)(2,1)S(1)} %copy-done.3), custom_call_target="tpu_custom_call" | custom-call | flops 1073741824 | bytes 2097152 | tf_op jit(solution)/shard_map/own_rows/pallas_call | solution.py:469
  9.8 0.0 copy-done.1
  9.8 0.0 collective-permute-done.up_ref
  9.8 1.7 %collective-permute-done.1.down_ref = bf16[768,128]{1,0:T(8,128)(2,1)S(1)} collective-permute-done((bf16[768,128]{1,0:T(8,128)(2,1)S(1)}, bf16[768,128]{1,0:T(8,128)(2,1)S(1)}, u32[]{:S(2)}, u32[]{:S(2)}) %collective-permute-start.1) | collective-permute-done | bytes 196640 | tf_op jit(solution)/shard_map/ppermute | solution.py:641
  11.6 0.0 copy-start.4
  11.6 2.0 %collective-permute-start.2 = (bf16[800,128]{1,0:T(8,128)(2,1)S(1)}, bf16[800,128]{1,0:T(8,128)(2,1)S(1)}, u32[]{:S(2)}, u32[]{:S(2)}) collective-permute-start(bf16[800,128]{1,0:T(8,128)(2,1)S(1)} %pad_maximum_fusion), channel_id=1, source_target_pairs={{0,1},{1,2},{2,3},{3,4},{4,5},{5,6},{6,7},{7,0},{8,9},{9,10},{10,1... | collective-permute-start | bytes 614408 | tf_op jit(solution)/shard_map/ppermute | solution.py:645
  13.6 0.0 copy-start.6
  13.6 0.0 copy-start.7
  13.7 0.0 copy-start.8
  13.7 0.0 copy-start.9
  13.7 4.2 %collective-permute-start.3 = (bf16[800,128]{1,0:T(8,128)(2,1)S(1)}, bf16[800,128]{1,0:T(8,128)(2,1)S(1)}, u32[]{:S(2)}, u32[]{:S(2)}) collective-permute-start(bf16[800,128]{1,0:T(8,128)(2,1)S(1)} %pad_maximum_fusion.1), channel_id=1, source_target_pairs={{0,7},{1,0},{2,1},{3,2},{4,3},{5,4},{6,5},{7,6},{8,15},{9,8},{10,9... | collective-permute-start | bytes 614408 | tf_op jit(solution)/shard_map/ppermute | solution.py:652
  17.9 0.0 copy-done.4
  17.9 0.0 copy-done.13
  17.9 1.3 %own_rows.2 = (bf16[4096,128]{1,0:T(8,128)(2,1)S(1)}, s16[4096,128]{1,0:T(8,128)(2,1)S(1)}) custom-call(s32[1]{0:T(128)S(6)} %copy.24.count_ref.refs_0_, s32[1,4096]{1,0:T(1,128)S(1)} %copy-done.13, bf16[1024,128]{1,0:T(8,128)(2,1)S(1)} %copy-done.4), custom_call_target="tpu_custom_call" | custom-call | flops 1073741824 | bytes 2097152 | tf_op jit(solution)/shard_map/own_rows/pallas_call | solution.py:469
  19.2 0.0 copy-start.19
  19.2 0.0 copy-start.14
  19.3 1.8 %collective-permute-done.2.yup_ref = bf16[800,128]{1,0:T(8,128)(2,1)S(1)} collective-permute-done((bf16[800,128]{1,0:T(8,128)(2,1)S(1)}, bf16[800,128]{1,0:T(8,128)(2,1)S(1)}, u32[]{:S(2)}, u32[]{:S(2)}) %collective-permute-start.2) | collective-permute-done | bytes 204832 | tf_op jit(solution)/shard_map/ppermute | solution.py:645
  21.1 0.0 collective-permute-done.3.ydown_ref
  21.1 0.0 copy-done.6
  21.1 0.0 copy-done.8
  21.1 0.0 copy-done.9
  21.1 0.0 copy-done.14
  21.1 0.0 copy-start.5
  21.2 0.0 copy-start.11
  21.2 7.9 %forward.1 = (bf16[4096,128]{1,0:T(8,128)(2,1)S(1)}, bf16[4096,128]{1,0:T(8,128)(2,1)S(1)}, bf16[4096,128]{1,0:T(8,128)(2,1)S(1)}, bf16[1024,128]{1,0:T(8,128)(2...) custom-call(s32[1]{0:T(128)S(6)} %copy.24.count_ref.refs_0_, ...), custom_call_target="tpu_custom_call" | custom-call | flops 4294967296 | bytes 8388608 | tf_op jit(solution)/shard_map/forward/pallas_call | solution.py:488
  29.1 0.0 collective-permute-start.4
  29.1 2.7 %collective-permute-start.5 = (bf16[64,128]{1,0:T(8,128)(2,1)S(1)}, bf16[64,128]{1,0:T(8,128)(2,1)S(1)}, u32[]{:S(2)}, u32[]{:S(2)}) collective-permute-start(bf16[64,128]{1,0:T(8,128)(2,1)S(1)} %get-tuple-element.63), channel_id=1, source_target_pairs={{0,7},{1,0},{2,1},{3,2},{4,3},{5,4},{6,5},{7,6},{8,15},{9,8},{10,9... | collective-permute-start | bytes 49160 | tf_op jit(solution)/shard_map/ppermute | solution.py:680
  31.8 1.1 %collective-permute-done.4.nlow_ref = bf16[64,128]{1,0:T(8,128)(2,1)S(1)} collective-permute-done((bf16[64,128]{1,0:T(8,128)(2,1)S(1)}, bf16[64,128]{1,0:T(8,128)(2,1)S(1)}, u32[]{:S(2)}, u32[]{:S(2)}) %collective-permute-start.4) | collective-permute-done | bytes 16416 | tf_op jit(solution)/shard_map/ppermute | solution.py:679
  32.9 0.0 collective-permute-done.5.nhigh_ref
  32.9 6.0 %backward.1 = (bf16[128,128]{1,0:T(8,128)(2,1)}, f32[1024,128]{1,0:T(8,128)S(1)}, bf16[4096,128]{1,0:T(8,128)(2,1)S(1)}, bf16[1024,128]{1,0:T(8,128)(2,1)}) custom-call(s16[4096,128]{1,0:T(8,128)(2,1)S(1)} %get-tuple-element.48.rcol_ref, bf16[4096,128]{1,0:T(8,128)(2,1)S(1)} %get-tuple-element.58.senders_ref, ...), custom_call_target="tpu_custom_call" | custom-call | flops 2147483648 | bytes 8388608 | tf_op jit(solution)/shard_map/backward/pallas_call | solution.py:515
  38.9 2.8 %ghost_grads.1 = (bf16[768,128]{1,0:T(8,128)(2,1)S(1)}, bf16[768,128]{1,0:T(8,128)(2,1)S(1)}, bf16[512,128]{1,0:T(8,128)(2,1)S(1)}) custom-call(s32[1]{0:T(128)S(6)} %copy.24.count_ref.refs_0_, s32[1,4096]{1,0:T(1,128)S(1)} %copy-done.13, s16[4096,128]{1,0:T(8,128)(2,1)S(1)} %get-tuple-element.47.scol_ref.refs_2_, ...), custom_call_target="tpu_custom_call" | custom-call | flops 2147483648 | bytes 3145728 | tf_op jit(solution)/shard_map/ghost_grads/pallas_call | solution.py:551
  41.7 9.4 %all-to-all-start = ((bf16[32,32,128]{2,1,0:T(8,128)(2,1)}), bf16[32,32,128]{2,1,0:T(8,128)(2,1)S(1)}, u32[]{:S(2)}, u32[]{:S(2)}) async-start(bf16[32,32,128]{2,1,0:T(8,128)(2,1)} %bitcast.2), calls=%async_computation | async-start | bytes 524288 | tf_op jit(solution)/shard_map/all_to_all | solution.py:436
  51.1 3.0 %collective-permute-start.6 = (bf16[768,128]{1,0:T(8,128)(2,1)S(1)}, bf16[768,128]{1,0:T(8,128)(2,1)S(1)}, u32[]{:S(2)}, u32[]{:S(2)}) collective-permute-start(bf16[768,128]{1,0:T(8,128)(2,1)S(1)} %get-tuple-element.70), channel_id=1, source_target_pairs={{0,7},{1,0},{2,1},{3,2},{4,3},{5,4},{6,5},{7,6},{8,15},{9,8},{10,9... | collective-permute-start | bytes 589832 | tf_op jit(solution)/shard_map/ppermute | solution.py:706
  54.2 0.0 collective-permute-start.7
  54.2 1.2 %copy-done.16 = bf16[4096,128]{1,0:T(8,128)(2,1)S(1)} copy-done((bf16[4096,128]{1,0:T(8,128)(2,1)S(1)}, bf16[4096,128]{1,0:T(8,128)(2,1)}, u32[]{:S(2)}) %copy-start.16) | copy-done | bytes 1048600
  55.4 1.0 %copy-done.18 = f32[1024,128]{1,0:T(8,128)S(1)} copy-done((f32[1024,128]{1,0:T(8,128)S(1)}, f32[1024,128]{1,0:T(8,128)}, u32[]{:S(2)}) %copy-start.18) | copy-done | bytes 524312
  56.5 1.2 %copy-done.20 = s16[4096,128]{1,0:T(8,128)(2,1)S(1)} copy-done((s16[4096,128]{1,0:T(8,128)(2,1)S(1)}, s16[4096,128]{1,0:T(8,128)(2,1)}, u32[]{:S(2)}) %copy-start.20) | copy-done | bytes 1048600
  57.7 2.7 %local.1.refs_8_ = f32[1024,128]{1,0:T(8,128)S(1)} custom-call(s32[1]{0:T(128)S(6)} %copy.24.count_ref.refs_0_, s32[1,4096]{1,0:T(1,128)S(1)} %copy-done.13, s32[1,4096]{1,0:T(1,128)S(1)} %copy-done.12, s16[4096,128]{1,0:T(8,128)(2,1)S(1)} %copy-done.20, s16[4096,128]{1,0:T(8,128)(2,1)S(1)} %get-tuple-element.48.rcol_ref, bf16[4096,128]{1,0:T(8,128)(2,1)S(1)} %copy-done.16, ...), custom_call_target="tpu_custom_call" | custom-call | flops 2147483648 | bytes 3145728 | tf_op jit(solution)/shard_map/local/pallas_call | solution.py:572
  60.4 0.0 collective-permute-done.6.refs_7_
  60.4 0.9 collective-permute-done.7.refs_6_
  61.4 0.0 all-to-all-done
  61.4 0.1 reduce_sum.24
  61.4 0.6 broadcast_in_dim.4
  62.1 6.0 %all-to-all-start.1 = ((bf16[8,32,128]{2,1,0:T(8,128)(2,1)}), bf16[8,32,128]{2,1,0:T(8,128)(2,1)S(1)}, u32[]{:S(2)}, u32[]{:S(2)}) async-start(bf16[8,32,128]{2,1,0:T(8,128)(2,1)} %broadcast_in_dim.4), calls=%async_computation.1 | async-start | bytes 131072 | tf_op jit(solution)/shard_map/all_to_all | solution.py:438
  68.1 3.0 %collective-permute-start.8 = (bf16[768,128]{1,0:T(8,128)(2,1)S(1)}, bf16[768,128]{1,0:T(8,128)(2,1)S(1)}, u32[]{:S(2)}, u32[]{:S(2)}) collective-permute-start(bf16[768,128]{1,0:T(8,128)(2,1)S(1)} %pad_maximum_fusion.2), channel_id=1, source_target_pairs={{0,8},{8,16},{16,24},{24,32},{32,40},{40,48},{48,56},{56,64},{64,7... | collective-permute-start | bytes 589832 | tf_op jit(solution)/shard_map/ppermute | solution.py:716
  71.1 4.3 %all-to-all-done.1 = bf16[8,32,128]{2,1,0:T(8,128)(2,1)S(1)} async-done(((bf16[8,32,128]{2,1,0:T(8,128)(2,1)}), bf16[8,32,128]{2,1,0:T(8,128)(2,1)S(1)}, u32[]{:S(2)}, u32[]{:S(2)}) %all-to-all-start.1) | async-done | bytes 65568 | tf_op jit(solution)/shard_map/all_to_all | solution.py:438
  75.4 0.7 broadcast_in_dim.5
  76.1 9.8 %all-to-all-start.2 = ((bf16[32,32,128]{2,1,0:T(8,128)(2,1)}), bf16[32,32,128]{2,1,0:T(8,128)(2,1)S(1)}, u32[]{:S(2)}, u32[]{:S(2)}) async-start(bf16[32,32,128]{2,1,0:T(8,128)(2,1)} %broadcast_in_dim.5), calls=%async_computation.2 | async-start | bytes 524288 | tf_op jit(solution)/shard_map/all_to_all | solution.py:440
  85.9 0.3 collective-permute-start.9
  86.2 0.0 collective-permute-done.8.refs_4_
  86.2 7.4 %collective-permute-done.9.refs_5_ = bf16[768,128]{1,0:T(8,128)(2,1)S(1)} collective-permute-done((bf16[768,128]{1,0:T(8,128)(2,1)S(1)}, bf16[768,128]{1,0:T(8,128)(2,1)S(1)}, u32[]{:S(2)}, u32[]{:S(2)}) %collective-permute-start.9) | collective-permute-done | bytes 196640 | tf_op jit(solution)/shard_map/ppermute | solution.py:713
  93.6 1.2 %all-to-all-done.2 = bf16[32,32,128]{2,1,0:T(8,128)(2,1)S(1)} async-done(((bf16[32,32,128]{2,1,0:T(8,128)(2,1)}), bf16[32,32,128]{2,1,0:T(8,128)(2,1)S(1)}, u32[]{:S(2)}, u32[]{:S(2)}) %all-to-all-start.2) | async-done | bytes 262176 | tf_op jit(solution)/shard_map/all_to_all | solution.py:440
  94.9 2.2 %final.1 = (f32[1024,128]{1,0:T(8,128)}, f32[256,128]{1,0:T(8,128)}, f32[128,128]{1,0:T(8,128)}, f32[256,128]{1,0:T(8,128)}, f32[128,128]{1,0:T(8,128)}, /*index=5*/f32[128,128]{1,0:T(8,128)}, f32[128,128]{1,0:T(8,128)}) custom-call(s32[4]{0:T(128)S(1)} %pad_add_fusion.place_ref.refs_0_, s32[1,8]{1,0:T(1,128)S(1)} %copy-done.2, s32[1,8,256]{2,1,0:T(8,128)S(1)} %copy-done, ...), custom_call_target="tpu_custom_call" | custom-call | flops 536870912 | bytes 2097152 | tf_op jit(solution)/shard_map/final/pallas_call | solution.py:597
  (29 shorter events, 0.2 us)
Async XLA Ops:
  0.6 0.7 copy-start
  0.7 0.7 copy-start.2
  1.3 1.0 copy-start.3
  3.7 6.1 %collective-permute-start = (bf16[768,128]{1,0:T(8,128)(2,1)S(1)}, bf16[768,128]{1,0:T(8,128)(2,1)S(1)}, u32[]{:S(2)}, u32[]{:S(2)}) collective-permute-start(bf16[768,128]{1,0:T(8,128)(2,1)S(1)} %get-tuple-element.50), channel_id=1, source_target_pairs={{0,8},{8,16},{16,24},{24,32},{32,40},{40,48},{48,56},{56,64},{64,7... | collective-permute-start | bytes 589832 | tf_op jit(solution)/shard_map/ppermute | solution.py:640
  6.4 5.1 %collective-permute-start.1 = (bf16[768,128]{1,0:T(8,128)(2,1)S(1)}, bf16[768,128]{1,0:T(8,128)(2,1)S(1)}, u32[]{:S(2)}, u32[]{:S(2)}) collective-permute-start(bf16[768,128]{1,0:T(8,128)(2,1)S(1)} %get-tuple-element.51), channel_id=1, source_target_pairs={{0,248},{8,0},{16,8},{24,16},{32,24},{40,32},{48,40},{56,48},{64,5... | collective-permute-start | bytes 589832 | tf_op jit(solution)/shard_map/ppermute | solution.py:641
  7.8 0.7 copy-start.12
  8.5 1.3 %copy-start.1 = (bf16[128,128]{1,0:T(8,128)(2,1)S(1)}, bf16[128,128]{1,0:T(8,128)(2,1)}, u32[]{:S(2)}) copy-start(bf16[128,128]{1,0:T(8,128)(2,1)} %dcoarse_ref.1) | copy-start | bytes 98308
  11.6 6.3 %copy-start.4 = (bf16[1024,128]{1,0:T(8,128)(2,1)S(1)}, bf16[1024,128]{1,0:T(8,128)(2,1)}, u32[]{:S(2)}) copy-start(bf16[1024,128]{1,0:T(8,128)(2,1)} %nodes_ref.7) | copy-start | bytes 786436
  11.6 9.5 %collective-permute-start.2 = (bf16[800,128]{1,0:T(8,128)(2,1)S(1)}, bf16[800,128]{1,0:T(8,128)(2,1)S(1)}, u32[]{:S(2)}, u32[]{:S(2)}) collective-permute-start(bf16[800,128]{1,0:T(8,128)(2,1)S(1)} %pad_maximum_fusion), channel_id=1, source_target_pairs={{0,1},{1,2},{2,3},{3,4},{4,5},{5,6},{6,7},{7,0},{8,9},{9,10},{10,1... | collective-permute-start | bytes 614408 | tf_op jit(solution)/shard_map/ppermute | solution.py:645
  13.6 4.3 %copy-start.13 = (s32[1,4096]{1,0:T(1,128)S(1)}, s32[1,4096]{1,0:T(1,128)}, u32[]{:S(2)}) copy-start(s32[1,4096]{1,0:T(1,128)} %send_ref.1) | copy-start | bytes 49156
  13.6 7.5 %copy-start.6 = (bf16[256,128]{1,0:T(8,128)(2,1)S(1)}, bf16[256,128]{1,0:T(8,128)(2,1)}, u32[]{:S(2)}) copy-start(bf16[256,128]{1,0:T(8,128)(2,1)} %wni_ref.3) | copy-start | bytes 196612
  13.6 7.5 %copy-start.7 = (bf16[256,128]{1,0:T(8,128)(2,1)S(1)}, bf16[256,128]{1,0:T(8,128)(2,1)}, u32[]{:S(2)}) copy-start(bf16[256,128]{1,0:T(8,128)(2,1)} %wei_ref.5) | copy-start | bytes 196612
  13.7 7.5 %copy-start.8 = (bf16[128,128]{1,0:T(8,128)(2,1)S(1)}, bf16[128,128]{1,0:T(8,128)(2,1)}, u32[]{:S(2)}) copy-start(bf16[128,128]{1,0:T(8,128)(2,1)} %weo_ref.3) | copy-start | bytes 98308
  13.7 7.5 %copy-start.9 = (bf16[128,128]{1,0:T(8,128)(2,1)S(1)}, bf16[128,128]{1,0:T(8,128)(2,1)}, u32[]{:S(2)}) copy-start(bf16[128,128]{1,0:T(8,128)(2,1)} %wno_ref.3) | copy-start | bytes 98308
  13.7 7.4 %collective-permute-start.3 = (bf16[800,128]{1,0:T(8,128)(2,1)S(1)}, bf16[800,128]{1,0:T(8,128)(2,1)S(1)}, u32[]{:S(2)}, u32[]{:S(2)}) collective-permute-start(bf16[800,128]{1,0:T(8,128)(2,1)S(1)} %pad_maximum_fusion.1), channel_id=1, source_target_pairs={{0,7},{1,0},{2,1},{3,2},{4,3},{5,4},{6,5},{7,6},{8,15},{9,8},{10,9... | collective-permute-start | bytes 614408 | tf_op jit(solution)/shard_map/ppermute | solution.py:652
  19.2 19.7 %copy-start.19 = (s16[4096,128]{1,0:T(8,128)(2,1)}, s16[4096,128]{1,0:T(8,128)(2,1)S(1)}, u32[]{:S(2)}) copy-start(s16[4096,128]{1,0:T(8,128)(2,1)S(1)} %get-tuple-element.47.scol_ref.refs_2_) | copy-start | bytes 3145732
  19.2 1.9 %copy-start.14 = (s32[1,1024]{1,0:T(1,128)S(1)}, s32[1,1024]{1,0:T(1,128)}, u32[]{:S(2)}) copy-start(s32[1,1024]{1,0:T(1,128)} %pool_ref.3) | copy-start | bytes 12292
  21.1 11.7 %copy-start.5 = (bf16[1024,128]{1,0:T(8,128)(2,1)S(1)}, bf16[1024,128]{1,0:T(8,128)(2,1)}, u32[]{:S(2)}) copy-start(bf16[1024,128]{1,0:T(8,128)(2,1)} %dfine_ref.1) | copy-start | bytes 786436
  21.2 11.7 %copy-start.11 = (bf16[128,128]{1,0:T(8,128)(2,1)S(1)}, bf16[128,128]{1,0:T(8,128)(2,1)}, u32[]{:S(2)}) copy-start(bf16[128,128]{1,0:T(8,128)(2,1)} %wco_ref.1) | copy-start | bytes 98308
  29.1 3.8 %copy-start.10 = (bf16[128,128]{1,0:T(8,128)(2,1)S(1)}, bf16[128,128]{1,0:T(8,128)(2,1)}, u32[]{:S(2)}) copy-start(bf16[128,128]{1,0:T(8,128)(2,1)} %wci_ref.1) | copy-start | bytes 98308
  29.1 3.8 %collective-permute-start.4 = (bf16[64,128]{1,0:T(8,128)(2,1)S(1)}, bf16[64,128]{1,0:T(8,128)(2,1)S(1)}, u32[]{:S(2)}, u32[]{:S(2)}) collective-permute-start(bf16[64,128]{1,0:T(8,128)(2,1)S(1)} %get-tuple-element.62), channel_id=1, source_target_pairs={{0,1},{1,2},{2,3},{3,4},{4,5},{5,6},{6,7},{7,0},{8,9},{9,10},{10,1... | collective-permute-start | bytes 49160 | tf_op jit(solution)/shard_map/ppermute | solution.py:679
  29.1 3.8 %collective-permute-start.5 = (bf16[64,128]{1,0:T(8,128)(2,1)S(1)}, bf16[64,128]{1,0:T(8,128)(2,1)S(1)}, u32[]{:S(2)}, u32[]{:S(2)}) collective-permute-start(bf16[64,128]{1,0:T(8,128)(2,1)S(1)} %get-tuple-element.63), channel_id=1, source_target_pairs={{0,7},{1,0},{2,1},{3,2},{4,3},{5,4},{6,5},{7,6},{8,15},{9,8},{10,9... | collective-permute-start | bytes 49160 | tf_op jit(solution)/shard_map/ppermute | solution.py:680
  38.9 2.8 %copy-start.15 = (bf16[4096,128]{1,0:T(8,128)(2,1)}, bf16[4096,128]{1,0:T(8,128)(2,1)S(1)}, u32[]{:S(2)}) copy-start(bf16[4096,128]{1,0:T(8,128)(2,1)S(1)} %get-tuple-element.69.refs_3_.dedge_ref) | copy-start | bytes 3145732
  38.9 2.8 %copy-start.17 = (f32[1024,128]{1,0:T(8,128)}, f32[1024,128]{1,0:T(8,128)S(1)}, u32[]{:S(2)}) copy-start(f32[1024,128]{1,0:T(8,128)S(1)} %get-tuple-element.72.dnode_ref) | copy-start | bytes 1572868
  41.7 19.7 %all-to-all-start = ((bf16[32,32,128]{2,1,0:T(8,128)(2,1)}), bf16[32,32,128]{2,1,0:T(8,128)(2,1)S(1)}, u32[]{:S(2)}, u32[]{:S(2)}) async-start(bf16[32,32,128]{2,1,0:T(8,128)(2,1)} %bitcast.2), calls=%async_computation | async-start | bytes 524288 | tf_op jit(solution)/shard_map/all_to_all | solution.py:436
  51.1 9.3 %collective-permute-start.6 = (bf16[768,128]{1,0:T(8,128)(2,1)S(1)}, bf16[768,128]{1,0:T(8,128)(2,1)S(1)}, u32[]{:S(2)}, u32[]{:S(2)}) collective-permute-start(bf16[768,128]{1,0:T(8,128)(2,1)S(1)} %get-tuple-element.70), channel_id=1, source_target_pairs={{0,7},{1,0},{2,1},{3,2},{4,3},{5,4},{6,5},{7,6},{8,15},{9,8},{10,9... | collective-permute-start | bytes 589832 | tf_op jit(solution)/shard_map/ppermute | solution.py:706
  54.2 7.2 %collective-permute-start.7 = (bf16[768,128]{1,0:T(8,128)(2,1)S(1)}, bf16[768,128]{1,0:T(8,128)(2,1)S(1)}, u32[]{:S(2)}, u32[]{:S(2)}) collective-permute-start(bf16[768,128]{1,0:T(8,128)(2,1)S(1)} %get-tuple-element.71), channel_id=1, source_target_pairs={{0,1},{1,2},{2,3},{3,4},{4,5},{5,6},{6,7},{7,0},{8,9},{9,10},{10,1... | collective-permute-start | bytes 589832 | tf_op jit(solution)/shard_map/ppermute | solution.py:707
  54.2 1.2 %copy-start.16 = (bf16[4096,128]{1,0:T(8,128)(2,1)S(1)}, bf16[4096,128]{1,0:T(8,128)(2,1)}, u32[]{:S(2)}) copy-start(bf16[4096,128]{1,0:T(8,128)(2,1)} %copy-done.15) | copy-start | bytes 3145732
  55.4 1.0 %copy-start.18 = (f32[1024,128]{1,0:T(8,128)S(1)}, f32[1024,128]{1,0:T(8,128)}, u32[]{:S(2)}) copy-start(f32[1024,128]{1,0:T(8,128)} %copy-done.17) | copy-start | bytes 1572868
  56.5 1.2 %copy-start.20 = (s16[4096,128]{1,0:T(8,128)(2,1)S(1)}, s16[4096,128]{1,0:T(8,128)(2,1)}, u32[]{:S(2)}) copy-start(s16[4096,128]{1,0:T(8,128)(2,1)} %copy-done.19) | copy-start | bytes 3145732
  62.1 13.3 %all-to-all-start.1 = ((bf16[8,32,128]{2,1,0:T(8,128)(2,1)}), bf16[8,32,128]{2,1,0:T(8,128)(2,1)S(1)}, u32[]{:S(2)}, u32[]{:S(2)}) async-start(bf16[8,32,128]{2,1,0:T(8,128)(2,1)} %broadcast_in_dim.4), calls=%async_computation.1 | async-start | bytes 131072 | tf_op jit(solution)/shard_map/all_to_all | solution.py:438
  68.1 18.1 %collective-permute-start.8 = (bf16[768,128]{1,0:T(8,128)(2,1)S(1)}, bf16[768,128]{1,0:T(8,128)(2,1)S(1)}, u32[]{:S(2)}, u32[]{:S(2)}) collective-permute-start(bf16[768,128]{1,0:T(8,128)(2,1)S(1)} %pad_maximum_fusion.2), channel_id=1, source_target_pairs={{0,8},{8,16},{16,24},{24,32},{32,40},{40,48},{48,56},{56,64},{64,7... | collective-permute-start | bytes 589832 | tf_op jit(solution)/shard_map/ppermute | solution.py:716
  76.1 18.8 %all-to-all-start.2 = ((bf16[32,32,128]{2,1,0:T(8,128)(2,1)}), bf16[32,32,128]{2,1,0:T(8,128)(2,1)S(1)}, u32[]{:S(2)}, u32[]{:S(2)}) async-start(bf16[32,32,128]{2,1,0:T(8,128)(2,1)} %broadcast_in_dim.5), calls=%async_computation.2 | async-start | bytes 524288 | tf_op jit(solution)/shard_map/all_to_all | solution.py:440
  85.9 7.7 %collective-permute-start.9 = (bf16[768,128]{1,0:T(8,128)(2,1)S(1)}, bf16[768,128]{1,0:T(8,128)(2,1)S(1)}, u32[]{:S(2)}, u32[]{:S(2)}) collective-permute-start(bf16[768,128]{1,0:T(8,128)(2,1)S(1)} %pad_maximum_fusion.3), channel_id=1, source_target_pairs={{0,248},{8,0},{16,8},{24,16},{32,24},{40,32},{48,40},{56,48},{64,5... | collective-permute-start | bytes 589832 | tf_op jit(solution)/shard_map/ppermute | solution.py:713

commit v4 on v3

v4 whole, which is shorter than its diff:
```python
import jax
import jax.numpy as jnp
from jax import lax
from jax.experimental import pallas as pl
from jax.experimental.pallas import tpu as pltpu
from jax.sharding import Mesh
from jax.sharding import PartitionSpec as P

BAND = 32
LAT = 128
LOW = 512
BITS = 9
CHUNK = 1024
FWD_CHUNK = 4096
FWD_MIB = BWD_MIB = 24
GX_GY = ("gx_0", "gx_1", "gx_2", "gy")
GX = ("gx_0", "gx_1", "gx_2")
ACROSS = (-1, -1, -1, 0, 0, 1, 1, 1)
ALONG = (-1, 0, 1, -1, 1, -1, 0, 1)
MIB = 1024 * 1024

f32 = jnp.float32
bf16 = jnp.bfloat16


def mm(left, right):
    return jnp.dot(left, right, preferred_element_type=f32)


def mm_nt(left, right):
    return lax.dot_general(left, right, (((1,), (1,)), ((), ())), preferred_element_type=f32)


def mm_tn(left, right):
    return lax.dot_general(left, right, (((0,), (0,)), ((), ())), preferred_element_type=f32)


def wide(table):
    groups = table.shape[0] // LOW
    return jnp.concatenate([table[i * LOW : (i + 1) * LOW] for i in range(groups)], axis=1)


def tall(table):
    groups = table.shape[1] // LAT
    return jnp.concatenate([table[:, i * LAT : (i + 1) * LAT] for i in range(groups)], axis=0)


def in_columns(row):
    parts = []
    for j in range(row.shape[1] // LAT):
        parts.append(jnp.broadcast_to(row[:, j * LAT : (j + 1) * LAT], (LAT, LAT)).T)
    return jnp.concatenate(parts, axis=0).astype(jnp.int16)


def one_hot(col, rows):
    lanes = lax.broadcasted_iota(jnp.int16, col.shape, 1)
    one, zero = jnp.ones((), bf16), jnp.zeros((), bf16)
    return jnp.concatenate(
        [jnp.where(col == lanes + j * LAT, one, zero) for j in range(rows // LAT)], axis=1
    )


def one_hot_t(row, rows):
    ids = lax.broadcasted_iota(jnp.int16, (rows, row.shape[1]), 0)
    col = jnp.broadcast_to(row, (16, row.shape[1])).astype(jnp.int16)
    col = jnp.concatenate([col] * (rows // 16), axis=0)
    return jnp.where(ids == col, jnp.ones((), bf16), jnp.zeros((), bf16))


def take(col, table):
    got = mm(one_hot(col & (LOW - 1), LOW), table).astype(bf16)
    group = col >> BITS
    total = jnp.zeros((col.shape[0], LAT), bf16)
    for i in range(table.shape[1] // LAT):
        total = jnp.where(group == i, got[:, i * LAT : (i + 1) * LAT], total)
    return total


def put(row, col, values, groups):
    group = col >> BITS
    zero = jnp.zeros((), bf16)
    spread = jnp.concatenate([jnp.where(group == i, values, zero) for i in range(groups)], axis=1)
    return mm(one_hot_t(row & (LOW - 1), LOW), spread)


def sigmoid(v):
    return 0.5 + 0.5 * jnp.tanh(0.5 * v)


def act_and_slope(v):
    s = sigmoid(v)
    return v * s, s * (1.0 + v * (1.0 - s))


def live_row(row, first, count):
    ids = lax.broadcasted_iota(jnp.int32, row.shape, 1) + first
    return jnp.where(ids < count, row, -1)


def live_slots(place_ref, count_ref, k):
    a = place_ref[0] + ACROSS[k]
    b = place_ref[1] + ALONG[k]
    inside = (a >= 0) & (a < place_ref[2]) & (b >= 0) & (b < place_ref[3])
    return jnp.where(inside, count_ref[0, k], 0)


def pick_kernel(place_ref, count_ref, rows_hbm, nodes_hbm, up_ref, down_ref, mid_ref, cols_ref, rows, nodes, sems):
    copies = (
        pltpu.make_async_copy(nodes_hbm, nodes, sems.at[0]),
        pltpu.make_async_copy(rows_hbm, rows, sems.at[1]),
    )
    for copy in copies:
        copy.start()
    for copy in copies:
        copy.wait()
    table = wide(nodes[...])
    slots = rows.shape[2]
    for k in range(8):
        row = live_row(rows[0, k : k + 1, :], 0, live_slots(place_ref, count_ref, k))
        col = in_columns(row)
        cols_ref[k * slots : (k + 1) * slots, :] = col
        got = take(col, table)
        if k < 3:
            down_ref[k * slots : (k + 1) * slots, :] = got
        elif k < 5:
            mid_ref[(k - 3) * slots : (k - 2) * slots, :] = got
        else:
            up_ref[(k - 5) * slots : (k - 4) * slots, :] = got


def own_kernel(count_ref, index_ref, nodes_ref, out_ref, cols_ref):
    table = wide(nodes_ref[...])
    col = in_columns(live_row(index_ref[...], 0, count_ref[0]))
    cols_ref[...] = col
    out_ref[...] = take(col, table)


def forward_kernel(
    count_ref,
    recv_ref,
    scol_ref,
    rcol_ref,
    sown_ref,
    recvs_ref,
    up_ref,
    down_ref,
    yup_ref,
    ydown_ref,
    nodes_ref,
    pool_ref,
    wei_ref,
    weo_ref,
    wni_ref,
    wno_ref,
    senders_ref,
    act_ref,
    slope_ref,
    fine_ref,
    summed_ref,
    nact_ref,
    nslope_ref,
    window_ref,
    wlow_ref,
    whigh_ref,
    table,
    message,
):
    slots = up_ref.shape[0] // 3

    def block(ref, i):
        return ref[i * slots : (i + 1) * slots, :]

    blocks = (
        block(ydown_ref, 2),
        block(down_ref, 1),
        block(yup_ref, 2),
        block(ydown_ref, 1),
        block(yup_ref, 1),
        block(ydown_ref, 0),
        block(up_ref, 1),
        block(yup_ref, 0),
    )
    for k in range(8):
        table[(k % 2) * slots : (k % 2 + 1) * slots, (k // 2) * LAT : (k // 2 + 1) * LAT] = blocks[k]

    owned = nodes_ref.shape[0]
    edges = recv_ref.shape[1]
    for first in range(0, edges, FWD_CHUNK):
        here = slice(first, first + FWD_CHUNK)
        senders = take(scol_ref[here, :] - owned, table[...]) + sown_ref[here, :]
        senders_ref[here, :] = senders
        pre = mm(jnp.concatenate([senders, recvs_ref[here, :]], axis=1), wei_ref[...])
        act, slope = act_and_slope(pre)
        act = act.astype(bf16)
        act_ref[here, :] = act
        slope_ref[here, :] = slope.astype(bf16)
        message[here, :] = mm(act, weo_ref[...]).astype(bf16)
    recv = live_row(recv_ref[...], 0, count_ref[0])
    summed = tall(put(recv, rcol_ref[...], message[...], owned // LOW)).astype(bf16)
    summed_ref[...] = summed
    nodes = nodes_ref[...]
    pre = mm(jnp.concatenate([nodes, summed], axis=1), wni_ref[...])
    act, slope = act_and_slope(pre)
    act = act.astype(bf16)
    nact_ref[...] = act
    nslope_ref[...] = slope.astype(bf16)
    fine = (nodes.astype(f32) + mm(act, wno_ref[...])).astype(bf16)
    fine_ref[...] = fine
    rows = window_ref.shape[0]
    window = mm(one_hot_t(pool_ref[...], rows), fine)
    window_ref[...] = window
    wlow_ref[...] = window[: 2 * BAND].astype(bf16)
    whigh_ref[...] = window[rows - 2 * BAND :].astype(bf16)


def backward_kernel(
    rcol_ref,
    senders_ref,
    recvs_ref,
    act_ref,
    slope_ref,
    window_ref,
    nlow_ref,
    nhigh_ref,
    dcl_ref,
    dch_ref,
    dcoarse_ref,
    dfine_ref,
    pool_ref,
    nodes_ref,
    summed_ref,
    nact_ref,
    nslope_ref,
    wei_ref,
    weo_ref,
    wni_ref,
    wno_ref,
    wci_ref,
    wco_ref,
    coarse_ref,
    dnode_ref,
    dedge_ref,
    grads_ref,
    table,
):
    window = window_ref[...]
    rows = window.shape[0]
    total = jnp.concatenate(
        [
            window[: 2 * BAND] + nlow_ref[...].astype(f32),
            window[2 * BAND : rows - 2 * BAND],
            window[rows - 2 * BAND :] + nhigh_ref[...].astype(f32),
        ],
        axis=0,
    )
    coarse_in = (0.125 * total).astype(bf16)
    d_coarse = jnp.concatenate([dcl_ref[...], dcoarse_ref[...], dch_ref[...]], axis=0)
    act, slope = act_and_slope(mm(coarse_in, wci_ref[...]))
    act = act.astype(bf16)
    coarse_out = (coarse_in.astype(f32) + mm(act, wco_ref[...])).astype(bf16)
    coarse_ref[...] = coarse_out[BAND : rows - BAND]
    d_pre = (mm_nt(d_coarse, wco_ref[...]) * slope).astype(bf16)
    d_in = (d_coarse.astype(f32) + mm_nt(d_pre, wci_ref[...])).astype(bf16)
    inner = slice(BAND, rows - BAND)
    g_ci = mm_tn(coarse_in[inner], d_pre[inner])
    g_co = mm_tn(act[inner], d_coarse[inner])
    reach = jnp.concatenate([d_in, jnp.zeros((2 * LAT - rows, LAT), bf16)], axis=0)
    parent = mm(one_hot(in_columns(pool_ref[...]), 2 * LAT), reach)
    d_total = dfine_ref[...].astype(f32) + 0.125 * parent
    d_out = d_total.astype(bf16)
    d_node = (mm_nt(d_out, wno_ref[...]) * nslope_ref[...].astype(f32)).astype(bf16)
    back = mm_nt(d_node, wni_ref[...])
    dnode_ref[...] = d_total + back[:, :LAT]
    table[...] = wide(back[:, LAT:].astype(bf16))
    g_ni = mm_tn(jnp.concatenate([nodes_ref[...], summed_ref[...]], axis=1), d_node)
    g_no = mm_tn(nact_ref[...], d_out)
    grads_ref[3 * LAT : 5 * LAT, :] = g_ni.astype(bf16)
    grads_ref[5 * LAT : 6 * LAT, :] = g_no.astype(bf16)
    grads_ref[6 * LAT : 7 * LAT, :] = g_ci.astype(bf16)
    grads_ref[7 * LAT :, :] = g_co.astype(bf16)

    edges = rcol_ref.shape[0]
    g_ei = jnp.zeros((2 * LAT, LAT), f32)
    g_eo = jnp.zeros((LAT, LAT), f32)
    for first in range(0, edges, CHUNK):
        here = slice(first, first + CHUNK)
        d_message = take(rcol_ref[here, :], table[...])
        d_pre = (mm_nt(d_message, weo_ref[...]) * slope_ref[here, :].astype(f32)).astype(bf16)
        dedge_ref[here, :] = d_pre
        ends = jnp.concatenate([senders_ref[here, :], recvs_ref[here, :]], axis=1)
        g_ei = g_ei + mm_tn(ends, d_pre)
        g_eo = g_eo + mm_tn(act_ref[here, :], d_message)
    grads_ref[: 2 * LAT, :] = g_ei.astype(bf16)
    grads_ref[2 * LAT : 3 * LAT, :] = g_eo.astype(bf16)


def ghost_kernel(count_ref, send_ref, dedge_ref, wei_ref, rdown_ref, rup_ref, rown_ref, *, owned):
    send = live_row(send_ref[...], 0, count_ref[0]) - owned
    total = put(send, in_columns(send), dedge_ref[...], 4)
    ghosts = mm_nt(tall(total).astype(bf16), wei_ref[:LAT, :]).astype(bf16)
    slots = ghosts.shape[0] // 8
    for place, (ref, i) in enumerate(
        (
            (rup_ref, 2),
            (rown_ref, 0),
            (rdown_ref, 2),
            (rup_ref, 1),
            (rdown_ref, 1),
            (rup_ref, 0),
            (rown_ref, 1),
            (rdown_ref, 0),
        )
    ):
        ref[i * slots : (i + 1) * slots, :] = ghosts[place * slots : (place + 1) * slots]


def local_kernel(count_ref, send_ref, recv_ref, dedge_ref, dnode_ref, wei_ref, out_ref):
    groups = out_ref.shape[0] // LOW
    d_pre = dedge_ref[...]
    send = live_row(send_ref[...], 0, count_ref[0])
    recv = live_row(recv_ref[...], 0, count_ref[0])
    by_send = tall(put(send, in_columns(send), d_pre, groups)).astype(bf16)
    by_recv = tall(put(recv, in_columns(recv), d_pre, groups)).astype(bf16)
    out_ref[...] = dnode_ref[...] + mm_nt(
        jnp.concatenate([by_send, by_recv], axis=1),
        jnp.concatenate([wei_ref[:LAT, :], wei_ref[LAT:, :]], axis=1),
    )


def return_kernel(
    place_ref,
    count_ref,
    rows_ref,
    cols_ref,
    down_ref,
    up_ref,
    mid_low_ref,
    mid_high_ref,
    part_ref,
    out_ref,
):
    slots = rows_ref.shape[2]
    groups = out_ref.shape[0] // LOW
    total = jnp.zeros((LOW, groups * LAT), f32)
    for k in range(8):
        row = live_row(rows_ref[0, k : k + 1, :], 0, live_slots(place_ref, count_ref, k))
        col = cols_ref[k * slots : (k + 1) * slots, :]
        if k < 3:
            got = down_ref[k * slots : (k + 1) * slots, :]
        elif k == 3:
            got = mid_low_ref[slots : 2 * slots, :]
        elif k == 4:
            got = mid_high_ref[slots : 2 * slots, :]
        else:
            got = up_ref[(k - 5) * slots : (k - 4) * slots, :]
        total = total + put(row, col, got, groups)
    out_ref[...] = part_ref[...] + tall(total)


def scale_kernel(scale, sums_ref, *grad_refs):
    first = 0
    for ref in grad_refs:
        rows = ref.shape[0]
        ref[...] = sums_ref[first : first + rows, :].astype(f32) * scale
        first += rows


def scalars():
    return pl.BlockSpec(memory_space=pltpu.SMEM)


def inside(count):
    return [pl.BlockSpec(memory_space=pltpu.VMEM)] * count


def hbm():
    return pl.BlockSpec(memory_space=pltpu.HBM)


def shape(dims, dtype):
    return jax.ShapeDtypeStruct(dims, dtype)


def params(mib):
    return pltpu.CompilerParams(vmem_limit_bytes=mib * MIB)


def cost(flops, moved):
    return pl.CostEstimate(flops=flops, bytes_accessed=moved, transcendentals=0)


def scattered(grads):
    n_far = lax.axis_size(GX)
    got = lax.all_to_all(grads.reshape(n_far, -1, LAT), GX, 0, 0, tiled=True)
    return got.astype(f32).sum(axis=0).astype(bf16)


def to_all(own, axis):
    pieces = jnp.broadcast_to(own[None], (lax.axis_size(axis), *own.shape))
    return lax.all_to_all(pieces, axis, 0, 0, tiled=True)


def call_pick(place, ghost_count, ghost_rows, nodes):
    slots = ghost_rows.shape[2]
    return pl.pallas_call(
        pick_kernel,
        out_shape=(
            shape((3 * slots, LAT), bf16),
            shape((3 * slots, LAT), bf16),
            shape((2 * slots, LAT), bf16),
            shape((8 * slots, LAT), jnp.int16),
        ),
        in_specs=[scalars(), scalars(), hbm(), hbm()],
        out_specs=tuple(inside(4)),
        scratch_shapes=[
            pltpu.VMEM(ghost_rows.shape, jnp.int32),
            pltpu.VMEM(nodes.shape, bf16),
            pltpu.SemaphoreType.DMA((2,)),
        ],
        compiler_params=params(32),
        cost_estimate=cost(2 * 2048 * 512 * 256, MIB),
        name="pick",
    )(place, ghost_count, ghost_rows, nodes)


def call_own(edge_count, index, nodes):
    edges = index.shape[1]
    return pl.pallas_call(
        own_kernel,
        out_shape=(shape((edges, LAT), bf16), shape((edges, LAT), jnp.int16)),
        in_specs=[scalars(), *inside(2)],
        out_specs=tuple(inside(2)),
        compiler_params=params(24),
        cost_estimate=cost(2 * 4096 * 512 * 256, 2 * MIB),
        name="own_rows",
    )(edge_count, index, nodes)


def call_forward(edge_count, recv, rows, *plain):
    edges, owned = recv.shape[1], plain[8].shape[0]
    edge16 = shape((edges, LAT), bf16)
    node16 = shape((owned, LAT), bf16)
    band = shape((2 * BAND, LAT), bf16)
    outs = (edge16,) * 3 + (node16,) * 4 + (shape((rows, LAT), f32), band, band)
    return pl.pallas_call(
        forward_kernel,
        out_shape=outs,
        in_specs=[scalars(), *inside(1 + len(plain))],
        out_specs=tuple(inside(len(outs))),
        scratch_shapes=[pltpu.VMEM((LOW, 4 * LAT), bf16), pltpu.VMEM((edges, LAT), bf16)],
        compiler_params=params(FWD_MIB),
        cost_estimate=cost(2 * 4096 * 512 * 1024, 8 * MIB),
        name="forward",
    )(edge_count, recv, *plain)


def call_backward(edge_arrays, plain):
    edges = edge_arrays[0].shape[0]
    owned, coarse = plain[8].shape[0], plain[5].shape[0]
    return pl.pallas_call(
        backward_kernel,
        out_shape=(
            shape((coarse, LAT), bf16),
            shape((owned, LAT), f32),
            shape((edges, LAT), bf16),
            shape((8 * LAT, LAT), bf16),
        ),
        in_specs=inside(len(edge_arrays) + len(plain)),
        out_specs=tuple(inside(4)),
        scratch_shapes=[pltpu.VMEM((LOW, owned // LOW * LAT), bf16)],
        compiler_params=params(BWD_MIB),
        cost_estimate=cost(2 * 4096 * 512 * 512, 8 * MIB),
        name="backward",
    )(*edge_arrays, *plain)


def call_ghost(edge_count, send, d_edge, w_edge_in, owned, slots):
    return pl.pallas_call(
        lambda *refs: ghost_kernel(*refs, owned=owned),
        out_shape=(
            shape((3 * slots, LAT), bf16),
            shape((3 * slots, LAT), bf16),
            shape((2 * slots, LAT), bf16),
        ),
        in_specs=[scalars(), *inside(3)],
        out_specs=tuple(inside(3)),
        compiler_params=params(24),
        cost_estimate=cost(2 * 4096 * 512 * 512, 3 * MIB),
        name="ghost_grads",
    )(edge_count, send, d_edge, w_edge_in)


def call_local(edge_count, send, recv, d_edge, d_node, w_edge_in):
    return pl.pallas_call(
        local_kernel,
        out_shape=shape(d_node.shape, f32),
        in_specs=[scalars(), *inside(5)],
        out_specs=inside(1)[0],
        compiler_params=params(24),
        cost_estimate=cost(2 * 2 * 4096 * 512 * 256, 3 * MIB),
        name="local",
    )(edge_count, send, recv, d_edge, d_node, w_edge_in)


def call_return(place, ghost_count, *arrays):
    owned = arrays[-1].shape[0]
    return pl.pallas_call(
        return_kernel,
        out_shape=shape((owned, LAT), f32),
        in_specs=[scalars(), scalars(), *inside(len(arrays))],
        out_specs=inside(1)[0],
        compiler_params=params(24),
        cost_estimate=cost(2 * 2048 * 512 * 256, 2 * MIB),
        name="returned",
    )(place, ghost_count, *arrays)


def call_scale(scale, sums):
    heights = (2 * LAT, LAT, 2 * LAT, LAT, LAT, LAT)
    return pl.pallas_call(
        lambda *refs: scale_kernel(scale, *refs),
        out_shape=tuple(shape((h, LAT), f32) for h in heights),
        in_specs=inside(1),
        out_specs=tuple(inside(6)),
        compiler_params=params(8),
        name="scaled",
    )(sums)


def ring(n, shift):
    return [(i, (i + shift) % n) for i in range(n)]


def body(
    nodes,
    ghost_rows,
    ghost_count,
    edge_send,
    edge_recv,
    edge_count,
    pool_map,
    w_edge_in,
    w_edge_out,
    w_node_in,
    w_node_out,
    w_coarse_in,
    w_coarse_out,
    d_fine,
    d_coarse,
):
    owned = nodes.shape[0]
    slots = ghost_rows.shape[2]
    coarse = d_coarse.shape[0]
    n_gx, n_gy = lax.axis_size(GX), lax.axis_size("gy")
    place = jnp.stack([lax.axis_index(GX), lax.axis_index("gy"), n_gx, n_gy]).astype(jnp.int32)

    out_up, out_down, out_mid, gcol = call_pick(place, ghost_count, ghost_rows, nodes)
    up = lax.ppermute(out_up, GX, ring(n_gx, 1))
    down = lax.ppermute(out_down, GX, ring(n_gx, -1))
    recvs, rcol = call_own(edge_count, edge_recv, nodes)
    up, down, recvs = lax.optimization_barrier((up, down, recvs))

    yup = lax.ppermute(
        jnp.concatenate(
            [up[2 * slots :], out_mid[slots:], down[2 * slots :], d_coarse[coarse - BAND :]]
        ),
        "gy",
        ring(n_gy, 1),
    )
    ydown = lax.ppermute(
        jnp.concatenate([up[:slots], out_mid[:slots], down[:slots], d_coarse[:BAND]]),
        "gy",
        ring(n_gy, -1),
    )
    sown, scol = call_own(edge_count, edge_send, nodes)

    (senders, act, slope, fine_out, summed, nact, nslope, window, wlow, whigh) = call_forward(
        edge_count,
        edge_recv,
        coarse + 2 * BAND,
        scol,
        rcol,
        sown,
        recvs,
        up,
        down,
        yup,
        ydown,
        nodes,
        pool_map,
        w_edge_in,
        w_edge_out,
        w_node_in,
        w_node_out,
    )

    nlow = lax.ppermute(whigh, "gy", ring(n_gy, 1))
    nhigh = lax.ppermute(wlow, "gy", ring(n_gy, -1))

    coarse_out, d_node, d_edge, grads = call_backward(
        (rcol, senders, recvs, act, slope),
        (
            window,
            nlow,
            nhigh,
            yup[3 * slots :],
            ydown[3 * slots :],
            d_coarse,
            d_fine,
            pool_map,
            nodes,
            summed,
            nact,
            nslope,
            w_edge_in,
            w_edge_out,
            w_node_in,
            w_node_out,
            w_coarse_in,
            w_coarse_out,
        ),
    )
    r_down, r_up, r_own = call_ghost(edge_count, edge_send, d_edge, w_edge_in, owned, slots)
    high = lax.ppermute(r_down, "gy", ring(n_gy, -1))
    low = lax.ppermute(r_up, "gy", ring(n_gy, 1))
    d_own = call_local(edge_count, edge_send, edge_recv, d_edge, d_node, w_edge_in)
    high, low, d_own = lax.optimization_barrier((high, low, d_own))

    ret_up = lax.ppermute(
        jnp.concatenate([low[:slots], r_own[slots:], high[:slots]]), GX, ring(n_gx, -1)
    )
    ret_down = lax.ppermute(
        jnp.concatenate([low[2 * slots :], r_own[:slots], high[2 * slots :]]), GX, ring(n_gx, 1)
    )

    own = scattered(grads)
    own = to_all(own, "gy").astype(f32).sum(axis=0).astype(bf16)
    own, ret_down, ret_up = lax.optimization_barrier((own, ret_down, ret_up))
    sums = to_all(own, GX).reshape(grads.shape)
    grad_nodes = call_return(
        place, ghost_count, ghost_rows, gcol, ret_down, ret_up, low, high, d_own
    )
    scaled = call_scale(1.0 / (owned * n_gx * n_gy) ** 0.5, sums)
    return (fine_out, coarse_out, grad_nodes, *scaled)


def solution(mesh):
    torus = Mesh(mesh.devices.reshape(4, 4, 2, mesh.shape["gy"]), GX_GY)
    in_specs = (
        P(GX_GY, None),
        P(GX_GY, None, None),
        P(GX_GY, None),
        P(GX_GY, None),
        P(GX_GY, None),
        P(GX_GY),
        P(GX_GY, None),
        P(),
        P(),
        P(),
        P(),
        P(),
        P(),
        P(GX_GY, None),
        P(GX_GY, None),
    )
    out_specs = (P(GX_GY, None), P(GX_GY, None), P(GX_GY, None), P(), P(), P(), P(), P(), P())
    return jax.shard_map(body, mesh=torus, in_specs=in_specs, out_specs=out_specs, check_vma=False)
```

time: 97.7 us -> 95.3 us (0.975)
  blocking collectives: 0 us -> 11.3 us
  starting transfers between devices: 43.9 us -> 34.5 us
  local copies, waits for them, and re-layouts: 7.26 us -> 4.53 us
  waiting for transfers between devices: 18.5 us -> 17 us
    all_to_all x0 -> x1, blocking collectives: none -> 11.3 us  [to_all(): return lax.all_to_all(pieces, axis, 0, 0, tiled=True)]
    all_to_all x3 -> x2, starting transfers between devices: 25.2 us -> 17.6 us  [the longest x1 10.8 us: scattered(): got = lax.all_to_all(grads.reshape(n_far, -1, LAT), GX, 0, 0, tiled=True)]
    ppermute x1, waiting for transfers between devices: 7.41 us -> 0.01 us  [body(): lax.ppermute(jnp.concatenate([low[:slots], r_own[slots:], high[:slots]]),...]
    all_to_all x3 -> x2, waiting for transfers between devices: 5.51 us -> 10 us  [the longest x1 6.87 us: to_all(): return lax.all_to_all(pieces, axis, 0, 0, tiled=True)]
    unnamed x42 -> x34, local copies, waits for them, and re-layouts: 5.81 us -> 3.71 us
    ppermute x1, starting transfers between devices: 2.01 us -> 0.26 us  [body(): lax.ppermute(jnp.concatenate([up[2 * slots:], out_mid[slots:], down[2 * s...]
    ppermute x1, starting transfers between devices: 4.23 us -> 5.95 us  [body(): lax.ppermute(jnp.concatenate([up[:slots], out_mid[:slots], down[:slots],...]
    ppermute x1, waiting for transfers between devices: 1.84 us -> 3.45 us  [body(): lax.ppermute(jnp.concatenate([up[2 * slots:], out_mid[slots:], down[2 * s...]
  transfers between devices with their start and end apart: 13 -> 12, of which waited for: 7 -> 6; matrix products, arithmetic and copies ran while one was open for 1% -> 0% of each run, Pallas kernels for 5% -> 8%
where the time goes in v4:
time: 95.3 us; the launch traced here: 94.8 us
  starting transfers between devices  34.5 us (36%)
  Pallas kernels  25.6 us (27%)
  waiting for transfers between devices  17 us (18%)
  blocking collectives  11.3 us (12%)
  local copies, waits for them, and re-layouts  4.53 us (5%)
  between operations  1.63 us (2%)
    all_to_all x1, blocking collectives, to_all(): return lax.all_to_all(pieces, axis, 0, 0, tiled=True)  11.3 us
    all_to_all x1, starting transfers between devices, scattered(): got = lax.all_to_all(grads.reshape(n_far, -1, LAT), GX, 0, 0, tiled=True)  10.8 us
    pallas_call x1, Pallas kernels, call_forward(): pl.pallas_call(forward_kernel, out_shape=outs, in_specs=[scalars(), *insi...  7.86 us
    all_to_all x1, waiting for transfers between devices, to_all(): return lax.all_to_all(pieces, axis, 0, 0, tiled=True)  6.87 us
    all_to_all x1, starting transfers between devices, to_all(): return lax.all_to_all(pieces, axis, 0, 0, tiled=True)  6.78 us
    ppermute x1, starting transfers between devices, body(): lax.ppermute(jnp.concatenate([up[:slots], out_mid[:slots], down[:slots],...  5.95 us
    pallas_call x1, Pallas kernels, call_backward(): pl.pallas_call(backward_kernel, out_shape=(shape((coarse, LAT), bf16), sh...  5.33 us
    unnamed x34, local copies, waits for them, and re-layouts  3.71 us
  transfers between devices with their start and end apart: 12, of which 6 were waited for; matrix products, arithmetic and copies ran while one was open for 0% of the time, Pallas kernels for 8%

profile of v4, /device:TPU:1, one launch (start us, length us, event | category | flops | bytes accessed | tf_op | source)
XLA Modules:
  0.0 94.8 jit_solution(13689751364184435145)
XLA Ops:
  0.6 0.0 copy-start
  0.7 0.0 copy-start.2
  0.7 0.1 pad_add_fusion.place_ref
  0.7 0.6 copy-done
  1.3 0.0 copy-done.2
  1.4 0.9 %copy-done.3 = bf16[1024,128]{1,0:T(8,128)(2,1)S(1)} copy-done((bf16[1024,128]{1,0:T(8,128)(2,1)S(1)}, bf16[1024,128]{1,0:T(8,128)(2,1)}, u32[]{:S(2)}) %copy-start.3) | copy-done | bytes 262168
  2.3 1.4 %pick.1 = (bf16[768,128]{1,0:T(8,128)(2,1)S(1)}, bf16[768,128]{1,0:T(8,128)(2,1)S(1)}, bf16[512,128]{1,0:T(8,128)(2,1)S(1)}, s16[2048,128]{1,0:T(8,128)(2,1)S(1)}) custom-call(s32[4]{0:T(128)S(1)} %pad_add_fusion.place_ref, s32[1,8]{1,0:T(1,128)S(1)} %copy-done.2, s32[1,8,256]{2,1,0:T(8,128)S(1)} %copy-done, bf16[1024,128]{1,0:T(8,128)(2,1)S(1)} %copy-done.3), custom_call_target="tpu_custom_call" | custom-call | flops 536870912 | bytes 1048576 | tf_op jit(solution)/shard_map/pick/pallas_call | solution.py:405
  3.7 2.8 %collective-permute-start = (bf16[768,128]{1,0:T(8,128)(2,1)S(1)}, bf16[768,128]{1,0:T(8,128)(2,1)S(1)}, u32[]{:S(2)}, u32[]{:S(2)}) collective-permute-start(bf16[768,128]{1,0:T(8,128)(2,1)S(1)} %get-tuple-element.52), channel_id=1, source_target_pairs={{0,8},{8,16},{16,24},{24,32},{32,40},{40,48},{48,56},{56,64},{64,7... | collective-permute-start | bytes 589832 | tf_op jit(solution)/shard_map/ppermute | solution.py:558
  6.4 0.7 collective-permute-start.1
  7.8 0.0 copy-start.12
  7.8 0.7 copy-done.12
  8.5 1.3 %own_rows.3 = (bf16[4096,128]{1,0:T(8,128)(2,1)S(1)}, s16[4096,128]{1,0:T(8,128)(2,1)S(1)}) custom-call(s32[1]{0:T(128)S(6)} %copy.24.count_ref.refs_0_, s32[1,4096]{1,0:T(1,128)S(1)} %copy-done.12, bf16[1024,128]{1,0:T(8,128)(2,1)S(1)} %copy-done.3), custom_call_target="tpu_custom_call" | custom-call | flops 1073741824 | bytes 2097152 | tf_op jit(solution)/shard_map/own_rows/pallas_call | solution.py:428
  9.8 0.0 copy-done.1
  9.8 0.0 collective-permute-done.up_ref
  9.8 1.7 %collective-permute-done.1.down_ref = bf16[768,128]{1,0:T(8,128)(2,1)S(1)} collective-permute-done((bf16[768,128]{1,0:T(8,128)(2,1)S(1)}, bf16[768,128]{1,0:T(8,128)(2,1)S(1)}, u32[]{:S(2)}, u32[]{:S(2)}) %collective-permute-start.1) | collective-permute-done | bytes 196640 | tf_op jit(solution)/shard_map/ppermute | solution.py:559
  11.6 6.0 %collective-permute-start.3 = (bf16[800,128]{1,0:T(8,128)(2,1)S(1)}, bf16[800,128]{1,0:T(8,128)(2,1)S(1)}, u32[]{:S(2)}, u32[]{:S(2)}) collective-permute-start(bf16[800,128]{1,0:T(8,128)(2,1)S(1)} %pad_maximum_fusion.1), channel_id=1, source_target_pairs={{0,7},{1,0},{2,1},{3,2},{4,3},{5,4},{6,5},{7,6},{8,15},{9,8},{10,9... | collective-permute-start | bytes 614408 | tf_op jit(solution)/shard_map/ppermute | solution.py:570
  17.6 0.0 copy-start.4
  17.6 0.0 copy-start.6
  17.6 0.0 copy-start.7
  17.6 0.0 copy-start.8
  17.6 0.0 copy-start.9
  17.6 0.3 collective-permute-start.2
  17.9 0.4 copy-done.13
  18.3 1.3 %own_rows.2 = (bf16[4096,128]{1,0:T(8,128)(2,1)S(1)}, s16[4096,128]{1,0:T(8,128)(2,1)S(1)}) custom-call(s32[1]{0:T(128)S(6)} %copy.24.count_ref.refs_0_, s32[1,4096]{1,0:T(1,128)S(1)} %copy-done.13, bf16[1024,128]{1,0:T(8,128)(2,1)S(1)} %copy-done.3), custom_call_target="tpu_custom_call" | custom-call | flops 1073741824 | bytes 2097152 | tf_op jit(solution)/shard_map/own_rows/pallas_call | solution.py:428
  19.6 0.0 copy-start.14
  19.6 0.7 collective-permute-done.3.ydown_ref
  20.2 3.5 %collective-permute-done.2.yup_ref = bf16[800,128]{1,0:T(8,128)(2,1)S(1)} collective-permute-done((bf16[800,128]{1,0:T(8,128)(2,1)S(1)}, bf16[800,128]{1,0:T(8,128)(2,1)S(1)}, u32[]{:S(2)}, u32[]{:S(2)}) %collective-permute-start.2) | collective-permute-done | bytes 204832 | tf_op jit(solution)/shard_map/ppermute | solution.py:563
  23.7 0.0 copy-done.4
  23.7 0.0 copy-done.6
  23.7 0.0 copy-done.7
  23.7 0.0 copy-done.8
  23.7 0.0 copy-done.9
  23.7 0.0 copy-done.14
  23.7 0.0 copy-start.5
  23.8 0.0 copy-start.11
  23.8 7.9 %forward.1 = (bf16[4096,128]{1,0:T(8,128)(2,1)S(1)}, bf16[4096,128]{1,0:T(8,128)(2,1)S(1)}, bf16[4096,128]{1,0:T(8,128)(2,1)S(1)}, bf16[1024,128]{1,0:T(8,128)(2...) custom-call(s32[1]{0:T(128)S(6)} %copy.24.count_ref.refs_0_, ...), custom_call_target="tpu_custom_call" | custom-call | flops 4294967296 | bytes 8388608 | tf_op jit(solution)/shard_map/forward/pallas_call | solution.py:445
  31.6 0.0 collective-permute-start.4
  31.6 2.7 %collective-permute-start.5 = (bf16[64,128]{1,0:T(8,128)(2,1)S(1)}, bf16[64,128]{1,0:T(8,128)(2,1)S(1)}, u32[]{:S(2)}, u32[]{:S(2)}) collective-permute-start(bf16[64,128]{1,0:T(8,128)(2,1)S(1)} %get-tuple-element.65), channel_id=1, source_target_pairs={{0,7},{1,0},{2,1},{3,2},{4,3},{5,4},{6,5},{7,6},{8,15},{9,8},{10,9... | collective-permute-start | bytes 49160 | tf_op jit(solution)/shard_map/ppermute | solution.py:598
  34.3 1.1 %collective-permute-done.4.nlow_ref = bf16[64,128]{1,0:T(8,128)(2,1)S(1)} collective-permute-done((bf16[64,128]{1,0:T(8,128)(2,1)S(1)}, bf16[64,128]{1,0:T(8,128)(2,1)S(1)}, u32[]{:S(2)}, u32[]{:S(2)}) %collective-permute-start.4) | collective-permute-done | bytes 16416 | tf_op jit(solution)/shard_map/ppermute | solution.py:597
  35.4 0.0 collective-permute-done.5.nhigh_ref
  35.4 0.0 copy-done.5
  35.4 0.0 copy-done.11
  35.5 5.3 %backward.1 = (bf16[128,128]{1,0:T(8,128)(2,1)}, f32[1024,128]{1,0:T(8,128)S(1)}, bf16[4096,128]{1,0:T(8,128)(2,1)S(1)}, bf16[1024,128]{1,0:T(8,128)(2,1)}) custom-call(s16[4096,128]{1,0:T(8,128)(2,1)S(1)} %get-tuple-element.50.rcol_ref, bf16[4096,128]{1,0:T(8,128)(2,1)S(1)} %get-tuple-element.60.senders_ref, ...), custom_call_target="tpu_custom_call" | custom-call | flops 2147483648 | bytes 8388608 | tf_op jit(solution)/shard_map/backward/pallas_call | solution.py:460
  40.8 2.7 %ghost_grads.1 = (bf16[768,128]{1,0:T(8,128)(2,1)S(1)}, bf16[768,128]{1,0:T(8,128)(2,1)S(1)}, bf16[512,128]{1,0:T(8,128)(2,1)S(1)}) custom-call(s32[1]{0:T(128)S(6)} %copy.24.count_ref.refs_0_, s32[1,4096]{1,0:T(1,128)S(1)} %copy-done.13, bf16[4096,128]{1,0:T(8,128)(2,1)S(1)} %get-tuple-element.72.refs_2_.dedge_ref, bf16[256,128]{1,0:T(8,128)(2,1)S(1)} %copy-done.7), custom_call_target="tpu_custom_call" | custom-call | flops 2147483648 | bytes 3145728 | tf_op jit(solution)/shard_map/ghost_grads/pallas_call | solution.py:478
  43.5 2.7 %collective-permute-start.6 = (bf16[768,128]{1,0:T(8,128)(2,1)S(1)}, bf16[768,128]{1,0:T(8,128)(2,1)S(1)}, u32[]{:S(2)}, u32[]{:S(2)}) collective-permute-start(bf16[768,128]{1,0:T(8,128)(2,1)S(1)} %get-tuple-element.73), channel_id=1, source_target_pairs={{0,7},{1,0},{2,1},{3,2},{4,3},{5,4},{6,5},{7,6},{8,15},{9,8},{10,9... | collective-permute-start | bytes 589832 | tf_op jit(solution)/shard_map/ppermute | solution.py:624
  46.3 0.0 collective-permute-start.7
  46.3 10.8 %all-to-all-start = ((bf16[32,32,128]{2,1,0:T(8,128)(2,1)}), bf16[32,32,128]{2,1,0:T(8,128)(2,1)S(1)}, u32[]{:S(2)}, u32[]{:S(2)}) async-start(bf16[32,32,128]{2,1,0:T(8,128)(2,1)} %bitcast.2), calls=%async_computation | async-start | bytes 524288 | tf_op jit(solution)/shard_map/all_to_all | solution.py:394
  57.1 0.0 copy-start.16
  57.1 1.0 %copy-done.16 = f32[1024,128]{1,0:T(8,128)S(1)} copy-done((f32[1024,128]{1,0:T(8,128)S(1)}, f32[1024,128]{1,0:T(8,128)}, u32[]{:S(2)}) %copy-start.16) | copy-done | bytes 524312
  58.2 2.8 %local.1.part_ref = f32[1024,128]{1,0:T(8,128)S(1)} custom-call(s32[1]{0:T(128)S(6)} %copy.24.count_ref.refs_0_, s32[1,4096]{1,0:T(1,128)S(1)} %copy-done.13, s32[1,4096]{1,0:T(1,128)S(1)} %copy-done.12, bf16[4096,128]{1,0:T(8,128)(2,1)S(1)} %get-tuple-element.72.refs_2_.dedge_ref, f32[1024,128]{1,0:T(8,128)S(1)} %copy-done.16, bf16[256,128]{1,0:T(8,128)(2,1)S(1)} %copy-done.7), custom_call_target="tpu_custom_call" | custom-call | flops 2147483648 | bytes 3145728 | tf_op jit(solution)/shard_map/local/pallas_call | solution.py:494
  61.0 0.0 collective-permute-done.6.mid_high_ref
  61.0 0.0 collective-permute-done.7.mid_low_ref
  61.0 0.3 collective-permute-start.9
  61.4 1.6 %collective-permute-start.8 = (bf16[768,128]{1,0:T(8,128)(2,1)S(1)}, bf16[768,128]{1,0:T(8,128)(2,1)S(1)}, u32[]{:S(2)}, u32[]{:S(2)}) collective-permute-start(bf16[768,128]{1,0:T(8,128)(2,1)S(1)} %pad_maximum_fusion.2), channel_id=1, source_target_pairs={{0,8},{8,16},{16,24},{24,32},{32,40},{40,48},{48,56},{56,64},{64,7... | collective-permute-start | bytes 589832 | tf_op jit(solution)/shard_map/ppermute | solution.py:632
  63.0 3.1 %all-to-all-done = bf16[32,32,128]{2,1,0:T(8,128)(2,1)S(1)} async-done(((bf16[32,32,128]{2,1,0:T(8,128)(2,1)}), bf16[32,32,128]{2,1,0:T(8,128)(2,1)S(1)}, u32[]{:S(2)}, u32[]{:S(2)}) %all-to-all-start) | async-done | bytes 262176 | tf_op jit(solution)/shard_map/all_to_all | solution.py:394
  66.1 0.1 reduce_sum.24
  66.2 11.3 %all_to_all.15 = bf16[8,32,128]{2,1,0:T(8,128)(2,1)S(1)} all-to-all(bf16[8,32,128]{2,1,0:T(8,128)(2,1)S(1)} %broadcast_in_dim.4), channel_id=1, replica_groups=mesh['gx_0'=4,'gx_1'=4,'gx_2'=2,'gy'=8] {'gy'}, dimensions={0} | all-to-all | bytes 131072 | tf_op jit(solution)/shard_map/all_to_all | solution.py:400
  77.4 0.0 collective-permute-done.9.up_ref
  77.5 0.0 collective-permute-done.8.down_ref
  77.5 0.7 broadcast_in_dim.5
  78.2 6.8 %all-to-all-start.2 = ((bf16[32,32,128]{2,1,0:T(8,128)(2,1)}), bf16[32,32,128]{2,1,0:T(8,128)(2,1)S(1)}, u32[]{:S(2)}, u32[]{:S(2)}) async-start(bf16[32,32,128]{2,1,0:T(8,128)(2,1)} %broadcast_in_dim.5), calls=%async_computation.2 | async-start | bytes 524288 | tf_op jit(solution)/shard_map/all_to_all | solution.py:400
  85.0 2.1 %returned.1 = f32[1024,128]{1,0:T(8,128)} custom-call(s32[4]{0:T(128)S(1)} %pad_add_fusion.place_ref, s32[1,8]{1,0:T(1,128)S(1)} %copy-done.2, s32[1,8,256]{2,1,0:T(8,128)S(1)} %copy-done, s16[2048,128]{1,0:T(8,128)(2,1)S(1)} %get-tuple-element.70.cols_ref, bf16[768,128]{1,0:T(8,128)(2,1)S(1)} %collective-permute-done.8.down_ref, ...), custom_call_target="tpu_custom_call" | custom-call | flops 536870912 | bytes 2097152 | tf_op jit(solution)/shard_map/returned/pallas_call | solution.py:507
  87.1 6.9 %all-to-all-done.2 = bf16[32,32,128]{2,1,0:T(8,128)(2,1)S(1)} async-done(((bf16[32,32,128]{2,1,0:T(8,128)(2,1)}), bf16[32,32,128]{2,1,0:T(8,128)(2,1)S(1)}, u32[]{:S(2)}, u32[]{:S(2)}) %all-to-all-start.2) | async-done | bytes 262176 | tf_op jit(solution)/shard_map/all_to_all | solution.py:400
  94.0 0.8 scaled.1
  (21 shorter events, 0.2 us)
Async XLA Ops:
  0.6 0.7 copy-start
  0.7 0.7 copy-start.2
  1.3 1.0 %copy-start.3 = (bf16[1024,128]{1,0:T(8,128)(2,1)S(1)}, bf16[1024,128]{1,0:T(8,128)(2,1)}, u32[]{:S(2)}) copy-start(bf16[1024,128]{1,0:T(8,128)(2,1)} %nodes_ref.7) | copy-start | bytes 786436
  3.7 6.1 %collective-permute-start = (bf16[768,128]{1,0:T(8,128)(2,1)S(1)}, bf16[768,128]{1,0:T(8,128)(2,1)S(1)}, u32[]{:S(2)}, u32[]{:S(2)}) collective-permute-start(bf16[768,128]{1,0:T(8,128)(2,1)S(1)} %get-tuple-element.52), channel_id=1, source_target_pairs={{0,8},{8,16},{16,24},{24,32},{32,40},{40,48},{48,56},{56,64},{64,7... | collective-permute-start | bytes 589832 | tf_op jit(solution)/shard_map/ppermute | solution.py:558
  6.4 5.1 %collective-permute-start.1 = (bf16[768,128]{1,0:T(8,128)(2,1)S(1)}, bf16[768,128]{1,0:T(8,128)(2,1)S(1)}, u32[]{:S(2)}, u32[]{:S(2)}) collective-permute-start(bf16[768,128]{1,0:T(8,128)(2,1)S(1)} %get-tuple-element.53), channel_id=1, source_target_pairs={{0,248},{8,0},{16,8},{24,16},{32,24},{40,32},{48,40},{56,48},{64,5... | collective-permute-start | bytes 589832 | tf_op jit(solution)/shard_map/ppermute | solution.py:559
  7.8 0.7 copy-start.12
  8.5 1.3 %copy-start.1 = (bf16[128,128]{1,0:T(8,128)(2,1)S(1)}, bf16[128,128]{1,0:T(8,128)(2,1)}, u32[]{:S(2)}) copy-start(bf16[128,128]{1,0:T(8,128)(2,1)} %dcoarse_ref.1) | copy-start | bytes 98308
  11.6 8.7 %collective-permute-start.3 = (bf16[800,128]{1,0:T(8,128)(2,1)S(1)}, bf16[800,128]{1,0:T(8,128)(2,1)S(1)}, u32[]{:S(2)}, u32[]{:S(2)}) collective-permute-start(bf16[800,128]{1,0:T(8,128)(2,1)S(1)} %pad_maximum_fusion.1), channel_id=1, source_target_pairs={{0,7},{1,0},{2,1},{3,2},{4,3},{5,4},{6,5},{7,6},{8,15},{9,8},{10,9... | collective-permute-start | bytes 614408 | tf_op jit(solution)/shard_map/ppermute | solution.py:570
  17.5 0.7 copy-start.13
  17.6 6.1 %copy-start.4 = (bf16[1024,128]{1,0:T(8,128)(2,1)S(1)}, bf16[1024,128]{1,0:T(8,128)(2,1)}, u32[]{:S(2)}) copy-start(bf16[1024,128]{1,0:T(8,128)(2,1)} %nodes_ref.7) | copy-start | bytes 786436
  17.6 6.1 %copy-start.6 = (bf16[256,128]{1,0:T(8,128)(2,1)S(1)}, bf16[256,128]{1,0:T(8,128)(2,1)}, u32[]{:S(2)}) copy-start(bf16[256,128]{1,0:T(8,128)(2,1)} %wni_ref.3) | copy-start | bytes 196612
  17.6 6.1 %copy-start.7 = (bf16[256,128]{1,0:T(8,128)(2,1)S(1)}, bf16[256,128]{1,0:T(8,128)(2,1)}, u32[]{:S(2)}) copy-start(bf16[256,128]{1,0:T(8,128)(2,1)} %wei_ref.5) | copy-start | bytes 196612
  17.6 6.1 %copy-start.8 = (bf16[128,128]{1,0:T(8,128)(2,1)S(1)}, bf16[128,128]{1,0:T(8,128)(2,1)}, u32[]{:S(2)}) copy-start(bf16[128,128]{1,0:T(8,128)(2,1)} %weo_ref.3) | copy-start | bytes 98308
  17.6 6.1 %copy-start.9 = (bf16[128,128]{1,0:T(8,128)(2,1)S(1)}, bf16[128,128]{1,0:T(8,128)(2,1)}, u32[]{:S(2)}) copy-start(bf16[128,128]{1,0:T(8,128)(2,1)} %wno_ref.3) | copy-start | bytes 98308
  17.6 6.1 %collective-permute-start.2 = (bf16[800,128]{1,0:T(8,128)(2,1)S(1)}, bf16[800,128]{1,0:T(8,128)(2,1)S(1)}, u32[]{:S(2)}, u32[]{:S(2)}) collective-permute-start(bf16[800,128]{1,0:T(8,128)(2,1)S(1)} %pad_maximum_fusion), channel_id=1, source_target_pairs={{0,1},{1,2},{2,3},{3,4},{4,5},{5,6},{6,7},{7,0},{8,9},{9,10},{10,1... | collective-permute-start | bytes 614408 | tf_op jit(solution)/shard_map/ppermute | solution.py:563
  19.6 4.2 %copy-start.14 = (s32[1,1024]{1,0:T(1,128)S(1)}, s32[1,1024]{1,0:T(1,128)}, u32[]{:S(2)}) copy-start(s32[1,1024]{1,0:T(1,128)} %pool_ref.3) | copy-start | bytes 12292
  23.7 11.7 %copy-start.5 = (bf16[1024,128]{1,0:T(8,128)(2,1)S(1)}, bf16[1024,128]{1,0:T(8,128)(2,1)}, u32[]{:S(2)}) copy-start(bf16[1024,128]{1,0:T(8,128)(2,1)} %dfine_ref.1) | copy-start | bytes 786436
  23.8 11.7 %copy-start.11 = (bf16[128,128]{1,0:T(8,128)(2,1)S(1)}, bf16[128,128]{1,0:T(8,128)(2,1)}, u32[]{:S(2)}) copy-start(bf16[128,128]{1,0:T(8,128)(2,1)} %wco_ref.1) | copy-start | bytes 98308
  31.6 3.8 %copy-start.10 = (bf16[128,128]{1,0:T(8,128)(2,1)S(1)}, bf16[128,128]{1,0:T(8,128)(2,1)}, u32[]{:S(2)}) copy-start(bf16[128,128]{1,0:T(8,128)(2,1)} %wci_ref.1) | copy-start | bytes 98308
  31.6 3.8 %collective-permute-start.4 = (bf16[64,128]{1,0:T(8,128)(2,1)S(1)}, bf16[64,128]{1,0:T(8,128)(2,1)S(1)}, u32[]{:S(2)}, u32[]{:S(2)}) collective-permute-start(bf16[64,128]{1,0:T(8,128)(2,1)S(1)} %get-tuple-element.64), channel_id=1, source_target_pairs={{0,1},{1,2},{2,3},{3,4},{4,5},{5,6},{6,7},{7,0},{8,9},{9,10},{10,1... | collective-permute-start | bytes 49160 | tf_op jit(solution)/shard_map/ppermute | solution.py:597
  31.6 3.8 %collective-permute-start.5 = (bf16[64,128]{1,0:T(8,128)(2,1)S(1)}, bf16[64,128]{1,0:T(8,128)(2,1)S(1)}, u32[]{:S(2)}, u32[]{:S(2)}) collective-permute-start(bf16[64,128]{1,0:T(8,128)(2,1)S(1)} %get-tuple-element.65), channel_id=1, source_target_pairs={{0,7},{1,0},{2,1},{3,2},{4,3},{5,4},{6,5},{7,6},{8,15},{9,8},{10,9... | collective-permute-start | bytes 49160 | tf_op jit(solution)/shard_map/ppermute | solution.py:598
  40.8 2.7 %copy-start.15 = (f32[1024,128]{1,0:T(8,128)}, f32[1024,128]{1,0:T(8,128)S(1)}, u32[]{:S(2)}) copy-start(f32[1024,128]{1,0:T(8,128)S(1)} %get-tuple-element.75.dnode_ref) | copy-start | bytes 1572868
  43.5 17.4 %collective-permute-start.6 = (bf16[768,128]{1,0:T(8,128)(2,1)S(1)}, bf16[768,128]{1,0:T(8,128)(2,1)S(1)}, u32[]{:S(2)}, u32[]{:S(2)}) collective-permute-start(bf16[768,128]{1,0:T(8,128)(2,1)S(1)} %get-tuple-element.73), channel_id=1, source_target_pairs={{0,7},{1,0},{2,1},{3,2},{4,3},{5,4},{6,5},{7,6},{8,15},{9,8},{10,9... | collective-permute-start | bytes 589832 | tf_op jit(solution)/shard_map/ppermute | solution.py:624
  46.3 14.7 %collective-permute-start.7 = (bf16[768,128]{1,0:T(8,128)(2,1)S(1)}, bf16[768,128]{1,0:T(8,128)(2,1)S(1)}, u32[]{:S(2)}, u32[]{:S(2)}) collective-permute-start(bf16[768,128]{1,0:T(8,128)(2,1)S(1)} %get-tuple-element.74), channel_id=1, source_target_pairs={{0,1},{1,2},{2,3},{3,4},{4,5},{5,6},{6,7},{7,0},{8,9},{9,10},{10,1... | collective-permute-start | bytes 589832 | tf_op jit(solution)/shard_map/ppermute | solution.py:625
  46.3 19.8 %all-to-all-start = ((bf16[32,32,128]{2,1,0:T(8,128)(2,1)}), bf16[32,32,128]{2,1,0:T(8,128)(2,1)S(1)}, u32[]{:S(2)}, u32[]{:S(2)}) async-start(bf16[32,32,128]{2,1,0:T(8,128)(2,1)} %bitcast.2), calls=%async_computation | async-start | bytes 524288 | tf_op jit(solution)/shard_map/all_to_all | solution.py:394
  57.1 1.0 %copy-start.16 = (f32[1024,128]{1,0:T(8,128)S(1)}, f32[1024,128]{1,0:T(8,128)}, u32[]{:S(2)}) copy-start(f32[1024,128]{1,0:T(8,128)} %copy-done.15) | copy-start | bytes 1572868
  61.0 16.4 %collective-permute-start.9 = (bf16[768,128]{1,0:T(8,128)(2,1)S(1)}, bf16[768,128]{1,0:T(8,128)(2,1)S(1)}, u32[]{:S(2)}, u32[]{:S(2)}) collective-permute-start(bf16[768,128]{1,0:T(8,128)(2,1)S(1)} %pad_maximum_fusion.3), channel_id=1, source_target_pairs={{0,248},{8,0},{16,8},{24,16},{32,24},{40,32},{48,40},{56,48},{64,5... | collective-permute-start | bytes 589832 | tf_op jit(solution)/shard_map/ppermute | solution.py:629
  61.4 16.1 %collective-permute-start.8 = (bf16[768,128]{1,0:T(8,128)(2,1)S(1)}, bf16[768,128]{1,0:T(8,128)(2,1)S(1)}, u32[]{:S(2)}, u32[]{:S(2)}) collective-permute-start(bf16[768,128]{1,0:T(8,128)(2,1)S(1)} %pad_maximum_fusion.2), channel_id=1, source_target_pairs={{0,8},{8,16},{16,24},{24,32},{32,40},{40,48},{48,56},{56,64},{64,7... | collective-permute-start | bytes 589832 | tf_op jit(solution)/shard_map/ppermute | solution.py:632
  78.2 15.8 %all-to-all-start.2 = ((bf16[32,32,128]{2,1,0:T(8,128)(2,1)}), bf16[32,32,128]{2,1,0:T(8,128)(2,1)S(1)}, u32[]{:S(2)}, u32[]{:S(2)}) async-start(bf16[32,32,128]{2,1,0:T(8,128)(2,1)} %broadcast_in_dim.5), calls=%async_computation.2 | async-start | bytes 524288 | tf_op jit(solution)/shard_map/all_to_all | solution.py:400

commit v5 on v4

--- a/solution.py
+++ b/solution.py
@@ -12,7 +12,7 @@
 BITS = 9
 CHUNK = 1024
 FWD_CHUNK = 4096
-FWD_MIB = BWD_MIB = 24
+FWD_MIB = BWD_MIB = 20
 GX_GY = ("gx_0", "gx_1", "gx_2", "gy")
 GX = ("gx_0", "gx_1", "gx_2")
 ACROSS = (-1, -1, -1, 0, 0, 1, 1, 1)
@@ -68,12 +68,12 @@
 
 
 def take(col, table):
-    got = mm(one_hot(col & (LOW - 1), LOW), table).astype(bf16)
-    group = col >> BITS
-    total = jnp.zeros((col.shape[0], LAT), bf16)
+    got = mm(one_hot(col & (LOW - 1), LOW), table)
+    group = col.astype(jnp.int32) >> BITS
+    total = jnp.zeros((col.shape[0], LAT), f32)
     for i in range(table.shape[1] // LAT):
         total = jnp.where(group == i, got[:, i * LAT : (i + 1) * LAT], total)
-    return total
+    return total.astype(bf16)
 
 
 def put(row, col, values, groups):
@@ -287,9 +287,10 @@
         d_message = take(rcol_ref[here, :], table[...])
         d_pre = (mm_nt(d_message, weo_ref[...]) * slope_ref[here, :].astype(f32)).astype(bf16)
         dedge_ref[here, :] = d_pre
-        ends = jnp.concatenate([senders_ref[here, :], recvs_ref[here, :]], axis=1)
-        g_ei = g_ei + mm_tn(ends, d_pre)
-        g_eo = g_eo + mm_tn(act_ref[here, :], d_message)
+        ends = jnp.concatenate([senders_ref[here, :], recvs_ref[here, :], act_ref[here, :]], axis=1)
+        both = mm_tn(ends, jnp.concatenate([d_pre, d_message], axis=1))
+        g_ei = g_ei + both[: 2 * LAT, :LAT]
+        g_eo = g_eo + both[2 * LAT :, LAT:]
     grads_ref[: 2 * LAT, :] = g_ei.astype(bf16)
     grads_ref[2 * LAT : 3 * LAT, :] = g_eo.astype(bf16)
 
@@ -430,7 +431,7 @@
         out_shape=(shape((edges, LAT), bf16), shape((edges, LAT), jnp.int16)),
         in_specs=[scalars(), *inside(2)],
         out_specs=tuple(inside(2)),
-        compiler_params=params(24),
+        compiler_params=params(16),
         cost_estimate=cost(2 * 4096 * 512 * 256, 2 * MIB),
         name="own_rows",
     )(edge_count, index, nodes)
@@ -484,7 +485,7 @@
         ),
         in_specs=[scalars(), *inside(3)],
         out_specs=tuple(inside(3)),
-        compiler_params=params(24),
+        compiler_params=params(16),
         cost_estimate=cost(2 * 4096 * 512 * 512, 3 * MIB),
         name="ghost_grads",
     )(edge_count, send, d_edge, w_edge_in)
@@ -496,7 +497,7 @@
         out_shape=shape(d_node.shape, f32),
         in_specs=[scalars(), *inside(5)],
         out_specs=inside(1)[0],
-        compiler_params=params(24),
+        compiler_params=params(16),
         cost_estimate=cost(2 * 2 * 4096 * 512 * 256, 3 * MIB),
         name="local",
     )(edge_count, send, recv, d_edge, d_node, w_edge_in)
@@ -509,7 +510,7 @@
         out_shape=shape((owned, LAT), f32),
         in_specs=[scalars(), scalars(), *inside(len(arrays))],
         out_specs=inside(1)[0],
-        compiler_params=params(24),
+        compiler_params=params(16),
         cost_estimate=cost(2 * 2048 * 512 * 256, 2 * MIB),
         name="returned",
     )(place, ghost_count, *arrays)
@@ -620,22 +621,20 @@
             w_coarse_out,
         ),
     )
+    own = scattered(grads)
     r_down, r_up, r_own = call_ghost(edge_count, edge_send, d_edge, w_edge_in, owned, slots)
+    own, r_down, r_up, r_own = lax.optimization_barrier((own, r_down, r_up, r_own))
     high = lax.ppermute(r_down, "gy", ring(n_gy, -1))
     low = lax.ppermute(r_up, "gy", ring(n_gy, 1))
+    own = to_all(own, "gy").astype(f32).sum(axis=0).astype(bf16)
     d_own = call_local(edge_count, edge_send, edge_recv, d_edge, d_node, w_edge_in)
-    high, low, d_own = lax.optimization_barrier((high, low, d_own))
-
     ret_up = lax.ppermute(
         jnp.concatenate([low[:slots], r_own[slots:], high[:slots]]), GX, ring(n_gx, -1)
     )
     ret_down = lax.ppermute(
         jnp.concatenate([low[2 * slots :], r_own[:slots], high[2 * slots :]]), GX, ring(n_gx, 1)
     )
-
-    own = scattered(grads)
-    own = to_all(own, "gy").astype(f32).sum(axis=0).astype(bf16)
-    own, ret_down, ret_up = lax.optimization_barrier((own, ret_down, ret_up))
+    own, ret_down, ret_up, d_own = lax.optimization_barrier((own, ret_down, ret_up, d_own))
     sums = to_all(own, GX).reshape(grads.shape)
     grad_nodes = call_return(
         place, ghost_count, ghost_rows, gcol, ret_down, ret_up, low, high, d_own

time: 95.3 us -> 93.6 us (0.982)
  blocking collectives: 11.3 us -> 0 us
  starting transfers between devices: 34.5 us -> 39.8 us
  waiting for transfers between devices: 17 us -> 21.9 us
    all_to_all x1 -> x0, blocking collectives: 11.3 us -> none  [to_all(): return lax.all_to_all(pieces, axis, 0, 0, tiled=True)]
    all_to_all x1 -> x2, starting transfers between devices: 6.78 us -> 12.3 us  [to_all(): return lax.all_to_all(pieces, axis, 0, 0, tiled=True)]
    all_to_all x1, waiting for transfers between devices: 3.15 us -> 6.22 us  [scattered(): got = lax.all_to_all(grads.reshape(n_far, -1, LAT), GX, 0, 0, tiled=True)]
    ppermute x1, waiting for transfers between devices: 0.01 us -> 1.06 us  [body(): low = lax.ppermute(r_up, 'gy', ring(n_gy, 1))]
    unnamed x34 -> x32, local copies, waits for them, and re-layouts: 3.71 us -> 2.69 us
    all_to_all x1 -> x2, waiting for transfers between devices: 6.87 us -> 7.65 us  [to_all(): return lax.all_to_all(pieces, axis, 0, 0, tiled=True)]
  transfers between devices with their start and end apart: 12 -> 13, of which waited for: 6 -> 8; matrix products, arithmetic and copies ran while one was open for 0% -> 2% of each run, Pallas kernels for 8% -> 11%
where the time goes in v5:
time: 93.6 us; the launch traced here: 92.9 us
  starting transfers between devices  39.8 us (43%)
  Pallas kernels  24.7 us (26%)
  waiting for transfers between devices  21.9 us (23%)
  local copies, waits for them, and re-layouts  4.12 us (4%)
  between operations  1.62 us (2%)
    all_to_all x2, starting transfers between devices, to_all(): return lax.all_to_all(pieces, axis, 0, 0, tiled=True)  12.3 us
    all_to_all x1, starting transfers between devices, scattered(): got = lax.all_to_all(grads.reshape(n_far, -1, LAT), GX, 0, 0, tiled=True)  10.2 us
    all_to_all x2, waiting for transfers between devices, to_all(): return lax.all_to_all(pieces, axis, 0, 0, tiled=True)  7.65 us
    pallas_call x1, Pallas kernels, call_forward(): pl.pallas_call(forward_kernel, out_shape=outs, in_specs=[scalars(), *insi...  7.57 us
    all_to_all x1, waiting for transfers between devices, scattered(): got = lax.all_to_all(grads.reshape(n_far, -1, LAT), GX, 0, 0, tiled=True)  6.22 us
    ppermute x1, starting transfers between devices, body(): lax.ppermute(jnp.concatenate([up[:slots], out_mid[:slots], down[:slots],...  5.95 us
    pallas_call x1, Pallas kernels, call_backward(): pl.pallas_call(backward_kernel, out_shape=(shape((coarse, LAT), bf16), sh...  4.65 us
    ppermute x1, waiting for transfers between devices, body(): lax.ppermute(jnp.concatenate([up[2 * slots:], out_mid[slots:], down[2 * s...  3.44 us
  transfers between devices with their start and end apart: 13, of which 8 were waited for; matrix products, arithmetic and copies ran while one was open for 2% of the time, Pallas kernels for 11%

profile of v5, /device:TPU:1, one launch (start us, length us, event | category | flops | bytes accessed | tf_op | source)
XLA Modules:
  0.0 92.9 jit_solution(7144303121421913310)
XLA Ops:
  0.6 0.0 copy-start
  0.7 0.0 copy-start.2
  0.7 0.1 pad_add_fusion.place_ref
  0.7 0.6 copy-done
  1.3 0.0 copy-done.2
  1.4 0.9 %copy-done.3 = bf16[1024,128]{1,0:T(8,128)(2,1)S(1)} copy-done((bf16[1024,128]{1,0:T(8,128)(2,1)S(1)}, bf16[1024,128]{1,0:T(8,128)(2,1)}, u32[]{:S(2)}) %copy-start.3) | copy-done | bytes 262168
  2.3 1.4 %pick.1 = (bf16[768,128]{1,0:T(8,128)(2,1)S(1)}, bf16[768,128]{1,0:T(8,128)(2,1)S(1)}, bf16[512,128]{1,0:T(8,128)(2,1)S(1)}, s16[2048,128]{1,0:T(8,128)(2,1)S(1)}) custom-call(s32[4]{0:T(128)S(1)} %pad_add_fusion.place_ref, s32[1,8]{1,0:T(1,128)S(1)} %copy-done.2, s32[1,8,256]{2,1,0:T(8,128)S(1)} %copy-done, bf16[1024,128]{1,0:T(8,128)(2,1)S(1)} %copy-done.3), custom_call_target="tpu_custom_call" | custom-call | flops 536870912 | bytes 1048576 | tf_op jit(solution)/shard_map/pick/pallas_call | solution.py:406
  3.7 2.8 %collective-permute-start = (bf16[768,128]{1,0:T(8,128)(2,1)S(1)}, bf16[768,128]{1,0:T(8,128)(2,1)S(1)}, u32[]{:S(2)}, u32[]{:S(2)}) collective-permute-start(bf16[768,128]{1,0:T(8,128)(2,1)S(1)} %get-tuple-element.54), channel_id=1, source_target_pairs={{0,8},{8,16},{16,24},{24,32},{32,40},{40,48},{48,56},{56,64},{64,7... | collective-permute-start | bytes 589832 | tf_op jit(solution)/shard_map/ppermute | solution.py:559
  6.4 0.6 collective-permute-start.1
  7.7 0.0 copy-start.11
  7.8 0.7 copy-done.11
  8.5 1.3 %own_rows.3 = (bf16[4096,128]{1,0:T(8,128)(2,1)S(1)}, s16[4096,128]{1,0:T(8,128)(2,1)S(1)}) custom-call(s32[1]{0:T(128)S(6)} %copy.24.count_ref.refs_0_, s32[1,4096]{1,0:T(1,128)S(1)} %copy-done.11, bf16[1024,128]{1,0:T(8,128)(2,1)S(1)} %copy-done.3), custom_call_target="tpu_custom_call" | custom-call | flops 1073741824 | bytes 2097152 | tf_op jit(solution)/shard_map/own_rows/pallas_call | solution.py:429
  9.8 0.0 copy-done.1
  9.8 0.0 collective-permute-done.up_ref
  9.8 1.7 %collective-permute-done.1.down_ref = bf16[768,128]{1,0:T(8,128)(2,1)S(1)} collective-permute-done((bf16[768,128]{1,0:T(8,128)(2,1)S(1)}, bf16[768,128]{1,0:T(8,128)(2,1)S(1)}, u32[]{:S(2)}, u32[]{:S(2)}) %collective-permute-start.1) | collective-permute-done | bytes 196640 | tf_op jit(solution)/shard_map/ppermute | solution.py:560
  11.6 5.9 %collective-permute-start.3 = (bf16[800,128]{1,0:T(8,128)(2,1)S(1)}, bf16[800,128]{1,0:T(8,128)(2,1)S(1)}, u32[]{:S(2)}, u32[]{:S(2)}) collective-permute-start(bf16[800,128]{1,0:T(8,128)(2,1)S(1)} %pad_maximum_fusion.1), channel_id=1, source_target_pairs={{0,7},{1,0},{2,1},{3,2},{4,3},{5,4},{6,5},{7,6},{8,15},{9,8},{10,9... | collective-permute-start | bytes 614408 | tf_op jit(solution)/shard_map/ppermute | solution.py:571
  17.5 0.0 copy-start.5
  17.6 0.0 copy-start.6
  17.6 0.0 copy-start.7
  17.6 0.0 copy-start.8
  17.6 0.3 collective-permute-start.2
  17.9 0.4 copy-done.12
  18.2 1.3 %own_rows.2 = (bf16[4096,128]{1,0:T(8,128)(2,1)S(1)}, s16[4096,128]{1,0:T(8,128)(2,1)S(1)}) custom-call(s32[1]{0:T(128)S(6)} %copy.24.count_ref.refs_0_, s32[1,4096]{1,0:T(1,128)S(1)} %copy-done.12, bf16[1024,128]{1,0:T(8,128)(2,1)S(1)} %copy-done.3), custom_call_target="tpu_custom_call" | custom-call | flops 1073741824 | bytes 2097152 | tf_op jit(solution)/shard_map/own_rows/pallas_call | solution.py:429
  19.6 0.0 copy-start.13
  19.6 0.7 collective-permute-done.3.ydown_ref
  20.2 3.4 %collective-permute-done.2.yup_ref = bf16[800,128]{1,0:T(8,128)(2,1)S(1)} collective-permute-done((bf16[800,128]{1,0:T(8,128)(2,1)S(1)}, bf16[800,128]{1,0:T(8,128)(2,1)S(1)}, u32[]{:S(2)}, u32[]{:S(2)}) %collective-permute-start.2) | collective-permute-done | bytes 204832 | tf_op jit(solution)/shard_map/ppermute | solution.py:564
  23.7 0.0 copy-done.5
  23.7 0.0 copy-done.6
  23.7 0.0 copy-done.7
  23.7 0.0 copy-done.8
  23.7 0.0 copy-done.13
  23.7 0.0 copy-start.4
  23.7 0.0 copy-start.10
  23.7 7.6 %forward.1 = (bf16[4096,128]{1,0:T(8,128)(2,1)S(1)}, bf16[4096,128]{1,0:T(8,128)(2,1)S(1)}, bf16[4096,128]{1,0:T(8,128)(2,1)S(1)}, bf16[1024,128]{1,0:T(8,128)(2...) custom-call(s32[1]{0:T(128)S(6)} %copy.24.count_ref.refs_0_, ...), custom_call_target="tpu_custom_call" | custom-call | flops 4294967296 | bytes 8388608 | tf_op jit(solution)/shard_map/forward/pallas_call | solution.py:446
  31.3 0.0 collective-permute-start.4
  31.3 2.7 %collective-permute-start.5 = (bf16[64,128]{1,0:T(8,128)(2,1)S(1)}, bf16[64,128]{1,0:T(8,128)(2,1)S(1)}, u32[]{:S(2)}, u32[]{:S(2)}) collective-permute-start(bf16[64,128]{1,0:T(8,128)(2,1)S(1)} %get-tuple-element.67), channel_id=1, source_target_pairs={{0,7},{1,0},{2,1},{3,2},{4,3},{5,4},{6,5},{7,6},{8,15},{9,8},{10,9... | collective-permute-start | bytes 49160 | tf_op jit(solution)/shard_map/ppermute | solution.py:599
  34.0 1.1 %collective-permute-done.4.nlow_ref = bf16[64,128]{1,0:T(8,128)(2,1)S(1)} collective-permute-done((bf16[64,128]{1,0:T(8,128)(2,1)S(1)}, bf16[64,128]{1,0:T(8,128)(2,1)S(1)}, u32[]{:S(2)}, u32[]{:S(2)}) %collective-permute-start.4) | collective-permute-done | bytes 16416 | tf_op jit(solution)/shard_map/ppermute | solution.py:598
  35.1 0.0 collective-permute-done.5.nhigh_ref
  35.1 0.0 copy-done.4
  35.1 4.7 %backward.1 = (bf16[128,128]{1,0:T(8,128)(2,1)}, f32[1024,128]{1,0:T(8,128)S(1)}, bf16[4096,128]{1,0:T(8,128)(2,1)S(1)}, bf16[1024,128]{1,0:T(8,128)(2,1)}) custom-call(s16[4096,128]{1,0:T(8,128)(2,1)S(1)} %get-tuple-element.52.rcol_ref, bf16[4096,128]{1,0:T(8,128)(2,1)S(1)} %get-tuple-element.62.senders_ref, ...), custom_call_target="tpu_custom_call" | custom-call | flops 2147483648 | bytes 8388608 | tf_op jit(solution)/shard_map/backward/pallas_call | solution.py:461
  39.8 10.2 %all-to-all-start = ((bf16[32,32,128]{2,1,0:T(8,128)(2,1)}), bf16[32,32,128]{2,1,0:T(8,128)(2,1)S(1)}, u32[]{:S(2)}, u32[]{:S(2)}) async-start(bf16[32,32,128]{2,1,0:T(8,128)(2,1)} %bitcast.2), calls=%async_computation | async-start | bytes 524288 | tf_op jit(solution)/shard_map/all_to_all | solution.py:395
  50.0 2.7 %ghost_grads.1 = (bf16[768,128]{1,0:T(8,128)(2,1)S(1)}, bf16[768,128]{1,0:T(8,128)(2,1)S(1)}, bf16[512,128]{1,0:T(8,128)(2,1)S(1)}) custom-call(s32[1]{0:T(128)S(6)} %copy.24.count_ref.refs_0_, s32[1,4096]{1,0:T(1,128)S(1)} %copy-done.12, bf16[4096,128]{1,0:T(8,128)(2,1)S(1)} %get-tuple-element.74.refs_2_.dedge_ref, bf16[256,128]{1,0:T(8,128)(2,1)S(1)} %copy-done.6), custom_call_target="tpu_custom_call" | custom-call | flops 2147483648 | bytes 3145728 | tf_op jit(solution)/shard_map/ghost_grads/pallas_call | solution.py:479
  52.8 6.2 %all-to-all-done = bf16[32,32,128]{2,1,0:T(8,128)(2,1)S(1)} async-done(((bf16[32,32,128]{2,1,0:T(8,128)(2,1)}), bf16[32,32,128]{2,1,0:T(8,128)(2,1)S(1)}, u32[]{:S(2)}, u32[]{:S(2)}) %all-to-all-start) | async-done | bytes 262176 | tf_op jit(solution)/shard_map/all_to_all | solution.py:395
  59.0 0.1 reduce_sum.24
  59.1 0.1 collective-permute-start.6
  59.1 3.0 %collective-permute-start.7 = (bf16[768,128]{1,0:T(8,128)(2,1)S(1)}, bf16[768,128]{1,0:T(8,128)(2,1)S(1)}, u32[]{:S(2)}, u32[]{:S(2)}) collective-permute-start(bf16[768,128]{1,0:T(8,128)(2,1)S(1)} %get-tuple-element.81), channel_id=1, source_target_pairs={{0,7},{1,0},{2,1},{3,2},{4,3},{5,4},{6,5},{7,6},{8,15},{9,8},{10,9... | collective-permute-start | bytes 589832 | tf_op jit(solution)/shard_map/ppermute | solution.py:627
  62.2 0.6 broadcast_in_dim.4
  62.8 3.4 %all-to-all-start.1 = ((bf16[8,32,128]{2,1,0:T(8,128)(2,1)}), bf16[8,32,128]{2,1,0:T(8,128)(2,1)S(1)}, u32[]{:S(2)}, u32[]{:S(2)}) async-start(bf16[8,32,128]{2,1,0:T(8,128)(2,1)} %broadcast_in_dim.4), calls=%async_computation.1 | async-start | bytes 131072 | tf_op jit(solution)/shard_map/all_to_all | solution.py:401
  66.2 1.1 %collective-permute-done.6.mid_low_ref = bf16[768,128]{1,0:T(8,128)(2,1)S(1)} collective-permute-done((bf16[768,128]{1,0:T(8,128)(2,1)S(1)}, bf16[768,128]{1,0:T(8,128)(2,1)S(1)}, u32[]{:S(2)}, u32[]{:S(2)}) %collective-permute-start.6) | collective-permute-done | bytes 196640 | tf_op jit(solution)/shard_map/ppermute | solution.py:628
  67.3 0.0 copy-start.15
  67.3 0.0 collective-permute-done.7.mid_high_ref
  67.3 0.8 collective-permute-start.9
  68.1 0.7 pad_maximum_fusion.2
  68.8 1.1 %collective-permute-start.8 = (bf16[768,128]{1,0:T(8,128)(2,1)}, bf16[768,128]{1,0:T(8,128)(2,1)S(1)}, u32[]{:S(2)}, u32[]{:S(2)}) collective-permute-start(bf16[768,128]{1,0:T(8,128)(2,1)} %pad_maximum_fusion.2), channel_id=1, source_target_pairs={{0,8},{8,16},{16,24},{24,32},{32,40},{40,48},{48,56},{56,64},{64,7... | collective-permute-start | bytes 589832 | tf_op jit(solution)/shard_map/ppermute | solution.py:634
  69.8 0.0 copy-done.15
  69.8 2.8 %local.1.part_ref = f32[1024,128]{1,0:T(8,128)S(1)} custom-call(s32[1]{0:T(128)S(6)} %copy.24.count_ref.refs_0_, s32[1,4096]{1,0:T(1,128)S(1)} %copy-done.12, s32[1,4096]{1,0:T(1,128)S(1)} %copy-done.11, bf16[4096,128]{1,0:T(8,128)(2,1)S(1)} %get-tuple-element.74.refs_2_.dedge_ref, f32[1024,128]{1,0:T(8,128)S(1)} %copy-done.15, bf16[256,128]{1,0:T(8,128)(2,1)S(1)} %copy-done.6), custom_call_target="tpu_custom_call" | custom-call | flops 2147483648 | bytes 3145728 | tf_op jit(solution)/shard_map/local/pallas_call | solution.py:495
  72.6 0.7 all-to-all-done.1
  73.3 0.0 collective-permute-done.9.up_ref
  73.3 0.0 collective-permute-done.8.down_ref
  73.3 0.7 broadcast_in_dim.5
  74.1 8.9 %all-to-all-start.2 = ((bf16[32,32,128]{2,1,0:T(8,128)(2,1)}), bf16[32,32,128]{2,1,0:T(8,128)(2,1)S(1)}, u32[]{:S(2)}, u32[]{:S(2)}) async-start(bf16[32,32,128]{2,1,0:T(8,128)(2,1)} %broadcast_in_dim.5), calls=%async_computation.2 | async-start | bytes 524288 | tf_op jit(solution)/shard_map/all_to_all | solution.py:401
  83.0 2.1 %returned.1 = f32[1024,128]{1,0:T(8,128)} custom-call(s32[4]{0:T(128)S(1)} %pad_add_fusion.place_ref, s32[1,8]{1,0:T(1,128)S(1)} %copy-done.2, s32[1,8,256]{2,1,0:T(8,128)S(1)} %copy-done, s16[2048,128]{1,0:T(8,128)(2,1)S(1)} %get-tuple-element.72.cols_ref, bf16[768,128]{1,0:T(8,128)(2,1)S(1)} %collective-permute-done.8.down_ref, ...), custom_call_target="tpu_custom_call" | custom-call | flops 536870912 | bytes 2097152 | tf_op jit(solution)/shard_map/returned/pallas_call | solution.py:508
  85.1 7.0 %all-to-all-done.2 = bf16[32,32,128]{2,1,0:T(8,128)(2,1)S(1)} async-done(((bf16[32,32,128]{2,1,0:T(8,128)(2,1)}), bf16[32,32,128]{2,1,0:T(8,128)(2,1)S(1)}, u32[]{:S(2)}, u32[]{:S(2)}) %all-to-all-start.2) | async-done | bytes 262176 | tf_op jit(solution)/shard_map/all_to_all | solution.py:401
  92.1 0.8 scaled.1
  (20 shorter events, 0.1 us)
Async XLA Ops:
  0.6 0.7 copy-start
  0.7 0.7 copy-start.2
  1.3 1.0 %copy-start.3 = (bf16[1024,128]{1,0:T(8,128)(2,1)S(1)}, bf16[1024,128]{1,0:T(8,128)(2,1)}, u32[]{:S(2)}) copy-start(bf16[1024,128]{1,0:T(8,128)(2,1)} %nodes_ref.7) | copy-start | bytes 786436
  3.7 6.1 %collective-permute-start = (bf16[768,128]{1,0:T(8,128)(2,1)S(1)}, bf16[768,128]{1,0:T(8,128)(2,1)S(1)}, u32[]{:S(2)}, u32[]{:S(2)}) collective-permute-start(bf16[768,128]{1,0:T(8,128)(2,1)S(1)} %get-tuple-element.54), channel_id=1, source_target_pairs={{0,8},{8,16},{16,24},{24,32},{32,40},{40,48},{48,56},{56,64},{64,7... | collective-permute-start | bytes 589832 | tf_op jit(solution)/shard_map/ppermute | solution.py:559
  6.4 5.1 %collective-permute-start.1 = (bf16[768,128]{1,0:T(8,128)(2,1)S(1)}, bf16[768,128]{1,0:T(8,128)(2,1)S(1)}, u32[]{:S(2)}, u32[]{:S(2)}) collective-permute-start(bf16[768,128]{1,0:T(8,128)(2,1)S(1)} %get-tuple-element.55), channel_id=1, source_target_pairs={{0,248},{8,0},{16,8},{24,16},{32,24},{40,32},{48,40},{56,48},{64,5... | collective-permute-start | bytes 589832 | tf_op jit(solution)/shard_map/ppermute | solution.py:560
  7.7 0.7 copy-start.11
  8.5 1.3 %copy-start.1 = (bf16[128,128]{1,0:T(8,128)(2,1)S(1)}, bf16[128,128]{1,0:T(8,128)(2,1)}, u32[]{:S(2)}) copy-start(bf16[128,128]{1,0:T(8,128)(2,1)} %dcoarse_ref.1) | copy-start | bytes 98308
  11.6 8.7 %collective-permute-start.3 = (bf16[800,128]{1,0:T(8,128)(2,1)S(1)}, bf16[800,128]{1,0:T(8,128)(2,1)S(1)}, u32[]{:S(2)}, u32[]{:S(2)}) collective-permute-start(bf16[800,128]{1,0:T(8,128)(2,1)S(1)} %pad_maximum_fusion.1), channel_id=1, source_target_pairs={{0,7},{1,0},{2,1},{3,2},{4,3},{5,4},{6,5},{7,6},{8,15},{9,8},{10,9... | collective-permute-start | bytes 614408 | tf_op jit(solution)/shard_map/ppermute | solution.py:571
  17.5 0.7 copy-start.12
  17.5 6.1 %copy-start.5 = (bf16[256,128]{1,0:T(8,128)(2,1)S(1)}, bf16[256,128]{1,0:T(8,128)(2,1)}, u32[]{:S(2)}) copy-start(bf16[256,128]{1,0:T(8,128)(2,1)} %wni_ref.3) | copy-start | bytes 196612
  17.6 6.1 %copy-start.6 = (bf16[256,128]{1,0:T(8,128)(2,1)S(1)}, bf16[256,128]{1,0:T(8,128)(2,1)}, u32[]{:S(2)}) copy-start(bf16[256,128]{1,0:T(8,128)(2,1)} %wei_ref.5) | copy-start | bytes 196612
  17.6 6.1 %copy-start.7 = (bf16[128,128]{1,0:T(8,128)(2,1)S(1)}, bf16[128,128]{1,0:T(8,128)(2,1)}, u32[]{:S(2)}) copy-start(bf16[128,128]{1,0:T(8,128)(2,1)} %weo_ref.3) | copy-start | bytes 98308
  17.6 6.1 %copy-start.8 = (bf16[128,128]{1,0:T(8,128)(2,1)S(1)}, bf16[128,128]{1,0:T(8,128)(2,1)}, u32[]{:S(2)}) copy-start(bf16[128,128]{1,0:T(8,128)(2,1)} %wno_ref.3) | copy-start | bytes 98308
  17.6 6.1 %collective-permute-start.2 = (bf16[800,128]{1,0:T(8,128)(2,1)S(1)}, bf16[800,128]{1,0:T(8,128)(2,1)S(1)}, u32[]{:S(2)}, u32[]{:S(2)}) collective-permute-start(bf16[800,128]{1,0:T(8,128)(2,1)S(1)} %pad_maximum_fusion), channel_id=1, source_target_pairs={{0,1},{1,2},{2,3},{3,4},{4,5},{5,6},{6,7},{7,0},{8,9},{9,10},{10,1... | collective-permute-start | bytes 614408 | tf_op jit(solution)/shard_map/ppermute | solution.py:564
  19.6 4.1 %copy-start.13 = (s32[1,1024]{1,0:T(1,128)S(1)}, s32[1,1024]{1,0:T(1,128)}, u32[]{:S(2)}) copy-start(s32[1,1024]{1,0:T(1,128)} %pool_ref.3) | copy-start | bytes 12292
  23.7 11.4 %copy-start.4 = (bf16[1024,128]{1,0:T(8,128)(2,1)S(1)}, bf16[1024,128]{1,0:T(8,128)(2,1)}, u32[]{:S(2)}) copy-start(bf16[1024,128]{1,0:T(8,128)(2,1)} %dfine_ref.1) | copy-start | bytes 786436
  23.7 11.4 %copy-start.10 = (bf16[128,128]{1,0:T(8,128)(2,1)S(1)}, bf16[128,128]{1,0:T(8,128)(2,1)}, u32[]{:S(2)}) copy-start(bf16[128,128]{1,0:T(8,128)(2,1)} %wco_ref.1) | copy-start | bytes 98308
  31.3 3.8 %copy-start.9 = (bf16[128,128]{1,0:T(8,128)(2,1)S(1)}, bf16[128,128]{1,0:T(8,128)(2,1)}, u32[]{:S(2)}) copy-start(bf16[128,128]{1,0:T(8,128)(2,1)} %wci_ref.1) | copy-start | bytes 98308
  31.3 3.8 %collective-permute-start.4 = (bf16[64,128]{1,0:T(8,128)(2,1)S(1)}, bf16[64,128]{1,0:T(8,128)(2,1)S(1)}, u32[]{:S(2)}, u32[]{:S(2)}) collective-permute-start(bf16[64,128]{1,0:T(8,128)(2,1)S(1)} %get-tuple-element.66), channel_id=1, source_target_pairs={{0,1},{1,2},{2,3},{3,4},{4,5},{5,6},{6,7},{7,0},{8,9},{9,10},{10,1... | collective-permute-start | bytes 49160 | tf_op jit(solution)/shard_map/ppermute | solution.py:598
  31.3 3.8 %collective-permute-start.5 = (bf16[64,128]{1,0:T(8,128)(2,1)S(1)}, bf16[64,128]{1,0:T(8,128)(2,1)S(1)}, u32[]{:S(2)}, u32[]{:S(2)}) collective-permute-start(bf16[64,128]{1,0:T(8,128)(2,1)S(1)} %get-tuple-element.67), channel_id=1, source_target_pairs={{0,7},{1,0},{2,1},{3,2},{4,3},{5,4},{6,5},{7,6},{8,15},{9,8},{10,9... | collective-permute-start | bytes 49160 | tf_op jit(solution)/shard_map/ppermute | solution.py:599
  39.8 10.3 %copy-start.14 = (f32[1024,128]{1,0:T(8,128)}, f32[1024,128]{1,0:T(8,128)S(1)}, u32[]{:S(2)}) copy-start(f32[1024,128]{1,0:T(8,128)S(1)} %get-tuple-element.82.dnode_ref) | copy-start | bytes 1572868
  39.8 19.2 %all-to-all-start = ((bf16[32,32,128]{2,1,0:T(8,128)(2,1)}), bf16[32,32,128]{2,1,0:T(8,128)(2,1)S(1)}, u32[]{:S(2)}, u32[]{:S(2)}) async-start(bf16[32,32,128]{2,1,0:T(8,128)(2,1)} %bitcast.2), calls=%async_computation | async-start | bytes 524288 | tf_op jit(solution)/shard_map/all_to_all | solution.py:395
  59.1 8.2 %collective-permute-start.6 = (bf16[768,128]{1,0:T(8,128)(2,1)S(1)}, bf16[768,128]{1,0:T(8,128)(2,1)S(1)}, u32[]{:S(2)}, u32[]{:S(2)}) collective-permute-start(bf16[768,128]{1,0:T(8,128)(2,1)S(1)} %get-tuple-element.79), channel_id=1, source_target_pairs={{0,1},{1,2},{2,3},{3,4},{4,5},{5,6},{6,7},{7,0},{8,9},{9,10},{10,1... | collective-permute-start | bytes 589832 | tf_op jit(solution)/shard_map/ppermute | solution.py:628
  59.1 8.1 %collective-permute-start.7 = (bf16[768,128]{1,0:T(8,128)(2,1)S(1)}, bf16[768,128]{1,0:T(8,128)(2,1)S(1)}, u32[]{:S(2)}, u32[]{:S(2)}) collective-permute-start(bf16[768,128]{1,0:T(8,128)(2,1)S(1)} %get-tuple-element.81), channel_id=1, source_target_pairs={{0,7},{1,0},{2,1},{3,2},{4,3},{5,4},{6,5},{7,6},{8,15},{9,8},{10,9... | collective-permute-start | bytes 589832 | tf_op jit(solution)/shard_map/ppermute | solution.py:627
  62.8 10.5 %all-to-all-start.1 = ((bf16[8,32,128]{2,1,0:T(8,128)(2,1)}), bf16[8,32,128]{2,1,0:T(8,128)(2,1)S(1)}, u32[]{:S(2)}, u32[]{:S(2)}) async-start(bf16[8,32,128]{2,1,0:T(8,128)(2,1)} %broadcast_in_dim.4), calls=%async_computation.1 | async-start | bytes 131072 | tf_op jit(solution)/shard_map/all_to_all | solution.py:401
  67.3 2.6 %copy-start.15 = (f32[1024,128]{1,0:T(8,128)S(1)}, f32[1024,128]{1,0:T(8,128)}, u32[]{:S(2)}) copy-start(f32[1024,128]{1,0:T(8,128)} %copy-done.14) | copy-start | bytes 1572868
  67.3 6.0 %collective-permute-start.9 = (bf16[768,128]{1,0:T(8,128)(2,1)S(1)}, bf16[768,128]{1,0:T(8,128)(2,1)S(1)}, u32[]{:S(2)}, u32[]{:S(2)}) collective-permute-start(bf16[768,128]{1,0:T(8,128)(2,1)S(1)} %pad_maximum_fusion.3), channel_id=1, source_target_pairs={{0,248},{8,0},{16,8},{24,16},{32,24},{40,32},{48,40},{56,48},{64,5... | collective-permute-start | bytes 589832 | tf_op jit(solution)/shard_map/ppermute | solution.py:631
  68.8 4.6 %collective-permute-start.8 = (bf16[768,128]{1,0:T(8,128)(2,1)}, bf16[768,128]{1,0:T(8,128)(2,1)S(1)}, u32[]{:S(2)}, u32[]{:S(2)}) collective-permute-start(bf16[768,128]{1,0:T(8,128)(2,1)} %pad_maximum_fusion.2), channel_id=1, source_target_pairs={{0,8},{8,16},{16,24},{24,32},{32,40},{40,48},{48,56},{56,64},{64,7... | collective-permute-start | bytes 589832 | tf_op jit(solution)/shard_map/ppermute | solution.py:634
  74.1 18.0 %all-to-all-start.2 = ((bf16[32,32,128]{2,1,0:T(8,128)(2,1)}), bf16[32,32,128]{2,1,0:T(8,128)(2,1)S(1)}, u32[]{:S(2)}, u32[]{:S(2)}) async-start(bf16[32,32,128]{2,1,0:T(8,128)(2,1)} %broadcast_in_dim.5), calls=%async_computation.2 | async-start | bytes 524288 | tf_op jit(solution)/shard_map/all_to_all | solution.py:401

commit v6 on v5

--- a/solution.py
+++ b/solution.py
@@ -11,10 +11,12 @@
 LOW = 512
 BITS = 9
 CHUNK = 1024
-FWD_CHUNK = 4096
+FWD_CHUNK = 512
 FWD_MIB = BWD_MIB = 20
 GX_GY = ("gx_0", "gx_1", "gx_2", "gy")
 GX = ("gx_0", "gx_1", "gx_2")
+CHIPS = ("gx_0", "gx_1")
+CORE = "gx_2"
 ACROSS = (-1, -1, -1, 0, 0, 1, 1, 1)
 ALONG = (-1, 0, 1, -1, 1, -1, 0, 1)
 MIB = 1024 * 1024
@@ -163,7 +165,6 @@
     wlow_ref,
     whigh_ref,
     table,
-    message,
 ):
     slots = up_ref.shape[0] // 3
 
@@ -185,18 +186,37 @@
 
     owned = nodes_ref.shape[0]
     edges = recv_ref.shape[1]
-    for first in range(0, edges, FWD_CHUNK):
-        here = slice(first, first + FWD_CHUNK)
+    chunks = [slice(first, first + FWD_CHUNK) for first in range(0, edges, FWD_CHUNK)]
+    recv = live_row(recv_ref[...], 0, count_ref[0])
+
+    def senders_of(here):
         senders = take(scol_ref[here, :] - owned, table[...]) + sown_ref[here, :]
         senders_ref[here, :] = senders
+        return senders
+
+    def messages_of(here, senders):
         pre = mm(jnp.concatenate([senders, recvs_ref[here, :]], axis=1), wei_ref[...])
         act, slope = act_and_slope(pre)
         act = act.astype(bf16)
         act_ref[here, :] = act
         slope_ref[here, :] = slope.astype(bf16)
-        message[here, :] = mm(act, weo_ref[...]).astype(bf16)
-    recv = live_row(recv_ref[...], 0, count_ref[0])
-    summed = tall(put(recv, rcol_ref[...], message[...], owned // LOW)).astype(bf16)
+        return mm(act, weo_ref[...]).astype(bf16)
+
+    def summed_of(here, message):
+        return put(recv[:, here], rcol_ref[here, :], message, owned // LOW)
+
+    total = jnp.zeros((LOW, owned // LOW * LAT), f32)
+    ahead = senders_of(chunks[0])
+    behind = None
+    for i, here in enumerate(chunks):
+        senders = ahead
+        if i + 1 < len(chunks):
+            ahead = senders_of(chunks[i + 1])
+        message = messages_of(here, senders)
+        if behind is not None:
+            total = total + summed_of(*behind)
+        behind = (here, message)
+    summed = tall(total + summed_of(*behind)).astype(bf16)
     summed_ref[...] = summed
     nodes = nodes_ref[...]
     pre = mm(jnp.concatenate([nodes, summed], axis=1), wni_ref[...])
@@ -214,6 +234,7 @@
 
 
 def backward_kernel(
+    place_ref,
     rcol_ref,
     senders_ref,
     recvs_ref,
@@ -240,8 +261,10 @@
     coarse_ref,
     dnode_ref,
     dedge_ref,
+    keep_ref,
+    give_ref,
+    table,
     grads_ref,
-    table,
 ):
     window = window_ref[...]
     rows = window.shape[0]
@@ -274,8 +297,8 @@
     table[...] = wide(back[:, LAT:].astype(bf16))
     g_ni = mm_tn(jnp.concatenate([nodes_ref[...], summed_ref[...]], axis=1), d_node)
     g_no = mm_tn(nact_ref[...], d_out)
-    grads_ref[3 * LAT : 5 * LAT, :] = g_ni.astype(bf16)
-    grads_ref[5 * LAT : 6 * LAT, :] = g_no.astype(bf16)
+    grads_ref[4 * LAT : 6 * LAT, :] = g_ni.astype(bf16)
+    grads_ref[3 * LAT : 4 * LAT, :] = g_no.astype(bf16)
     grads_ref[6 * LAT : 7 * LAT, :] = g_ci.astype(bf16)
     grads_ref[7 * LAT :, :] = g_co.astype(bf16)
 
@@ -293,6 +316,10 @@
         g_eo = g_eo + both[2 * LAT :, LAT:]
     grads_ref[: 2 * LAT, :] = g_ei.astype(bf16)
     grads_ref[2 * LAT : 3 * LAT, :] = g_eo.astype(bf16)
+    half = keep_ref.shape[0]
+    keep = pl.multiple_of(place_ref[4] * half, half)
+    keep_ref[...] = grads_ref[pl.ds(keep, half), :]
+    give_ref[...] = grads_ref[pl.ds(pl.multiple_of(half - keep, half), half), :]
 
 
 def ghost_kernel(count_ref, send_ref, dedge_ref, wei_ref, rdown_ref, rup_ref, rown_ref, *, owned):
@@ -358,12 +385,22 @@
     out_ref[...] = part_ref[...] + tall(total)
 
 
-def scale_kernel(scale, sums_ref, *grad_refs):
-    first = 0
-    for ref in grad_refs:
-        rows = ref.shape[0]
-        ref[...] = sums_ref[first : first + rows, :].astype(f32) * scale
-        first += rows
+def scale_kernel(scale, place_ref, kept_ref, other_ref, *grad_refs):
+    def write(halves):
+        half = kept_ref.shape[0]
+        for ref, first in zip(grad_refs, (0, 2 * LAT, 4 * LAT, 3 * LAT, 6 * LAT, 7 * LAT)):
+            rows = ref.shape[0]
+            source = halves[first // half]
+            start = first % half
+            ref[...] = source[start : start + rows, :].astype(f32) * scale
+
+    @pl.when(place_ref[4] == 0)
+    def _():
+        write((kept_ref, other_ref))
+
+    @pl.when(place_ref[4] != 0)
+    def _():
+        write((other_ref, kept_ref))
 
 
 def scalars():
@@ -391,8 +428,7 @@
 
 
 def scattered(grads):
-    n_far = lax.axis_size(GX)
-    got = lax.all_to_all(grads.reshape(n_far, -1, LAT), GX, 0, 0, tiled=True)
+    got = lax.all_to_all(grads.reshape(lax.axis_size(CHIPS), -1, LAT), CHIPS, 0, 0, tiled=True)
     return got.astype(f32).sum(axis=0).astype(bf16)
 
 
@@ -448,14 +484,14 @@
         out_shape=outs,
         in_specs=[scalars(), *inside(1 + len(plain))],
         out_specs=tuple(inside(len(outs))),
-        scratch_shapes=[pltpu.VMEM((LOW, 4 * LAT), bf16), pltpu.VMEM((edges, LAT), bf16)],
+        scratch_shapes=[pltpu.VMEM((LOW, 4 * LAT), bf16)],
         compiler_params=params(FWD_MIB),
         cost_estimate=cost(2 * 4096 * 512 * 1024, 8 * MIB),
         name="forward",
     )(edge_count, recv, *plain)
 
 
-def call_backward(edge_arrays, plain):
+def call_backward(place, edge_arrays, plain):
     edges = edge_arrays[0].shape[0]
     owned, coarse = plain[8].shape[0], plain[5].shape[0]
     return pl.pallas_call(
@@ -464,15 +500,19 @@
             shape((coarse, LAT), bf16),
             shape((owned, LAT), f32),
             shape((edges, LAT), bf16),
-            shape((8 * LAT, LAT), bf16),
+            shape((4 * LAT, LAT), bf16),
+            shape((4 * LAT, LAT), bf16),
         ),
-        in_specs=inside(len(edge_arrays) + len(plain)),
-        out_specs=tuple(inside(4)),
-        scratch_shapes=[pltpu.VMEM((LOW, owned // LOW * LAT), bf16)],
+        in_specs=[scalars(), *inside(len(edge_arrays) + len(plain))],
+        out_specs=tuple(inside(5)),
+        scratch_shapes=[
+            pltpu.VMEM((LOW, owned // LOW * LAT), bf16),
+            pltpu.VMEM((8 * LAT, LAT), bf16),
+        ],
         compiler_params=params(BWD_MIB),
         cost_estimate=cost(2 * 4096 * 512 * 512, 8 * MIB),
         name="backward",
-    )(*edge_arrays, *plain)
+    )(place, *edge_arrays, *plain)
 
 
 def call_ghost(edge_count, send, d_edge, w_edge_in, owned, slots):
@@ -516,16 +556,16 @@
     )(place, ghost_count, *arrays)
 
 
-def call_scale(scale, sums):
+def call_scale(scale, place, kept, other):
     heights = (2 * LAT, LAT, 2 * LAT, LAT, LAT, LAT)
     return pl.pallas_call(
         lambda *refs: scale_kernel(scale, *refs),
         out_shape=tuple(shape((h, LAT), f32) for h in heights),
-        in_specs=inside(1),
+        in_specs=[scalars(), *inside(2)],
         out_specs=tuple(inside(6)),
         compiler_params=params(8),
         name="scaled",
-    )(sums)
+    )(place, kept, other)
 
 
 def ring(n, shift):
@@ -553,7 +593,9 @@
     slots = ghost_rows.shape[2]
     coarse = d_coarse.shape[0]
     n_gx, n_gy = lax.axis_size(GX), lax.axis_size("gy")
-    place = jnp.stack([lax.axis_index(GX), lax.axis_index("gy"), n_gx, n_gy]).astype(jnp.int32)
+    place = jnp.stack(
+        [lax.axis_index(GX), lax.axis_index("gy"), n_gx, n_gy, lax.axis_index(CORE)]
+    ).astype(jnp.int32)
 
     out_up, out_down, out_mid, gcol = call_pick(place, ghost_count, ghost_rows, nodes)
     up = lax.ppermute(out_up, GX, ring(n_gx, 1))
@@ -598,7 +640,8 @@
     nlow = lax.ppermute(whigh, "gy", ring(n_gy, 1))
     nhigh = lax.ppermute(wlow, "gy", ring(n_gy, -1))
 
-    coarse_out, d_node, d_edge, grads = call_backward(
+    coarse_out, d_node, d_edge, keep, give = call_backward(
+        place,
         (rcol, senders, recvs, act, slope),
         (
             window,
@@ -621,7 +664,9 @@
             w_coarse_out,
         ),
     )
-    own = scattered(grads)
+    swap = ring(lax.axis_size(CORE), 1)
+    got = lax.ppermute(give, CORE, swap)
+    own = scattered((keep.astype(f32) + got.astype(f32)).astype(bf16))
     r_down, r_up, r_own = call_ghost(edge_count, edge_send, d_edge, w_edge_in, owned, slots)
     own, r_down, r_up, r_own = lax.optimization_barrier((own, r_down, r_up, r_own))
     high = lax.ppermute(r_down, "gy", ring(n_gy, -1))
@@ -635,11 +680,12 @@
         jnp.concatenate([low[2 * slots :], r_own[:slots], high[2 * slots :]]), GX, ring(n_gx, 1)
     )
     own, ret_down, ret_up, d_own = lax.optimization_barrier((own, ret_down, ret_up, d_own))
-    sums = to_all(own, GX).reshape(grads.shape)
+    half = to_all(own, CHIPS).reshape(keep.shape)
+    other = lax.ppermute(half, CORE, swap)
     grad_nodes = call_return(
         place, ghost_count, ghost_rows, gcol, ret_down, ret_up, low, high, d_own
     )
-    scaled = call_scale(1.0 / (owned * n_gx * n_gy) ** 0.5, sums)
+    scaled = call_scale(1.0 / (owned * n_gx * n_gy) ** 0.5, place, half, other)
     return (fine_out, coarse_out, grad_nodes, *scaled)
 
 

time: 93.6 us -> 91.6 us (0.979)
  blocking collectives: 0 us -> 11.7 us
  waiting for transfers between devices: 21.9 us -> 12.7 us
  starting transfers between devices: 39.8 us -> 34.3 us
  other arithmetic: 0.87 us -> 2.97 us
    all_to_all x0 -> x1, blocking collectives: none -> 11.7 us  [to_all(): return lax.all_to_all(pieces, axis, 0, 0, tiled=True)]
    all_to_all x2 -> x1, starting transfers between devices: 12.3 us -> 3.97 us  [to_all(): return lax.all_to_all(pieces, axis, 0, 0, tiled=True)]
    ppermute x0 -> x2, starting transfers between devices: none -> 7.24 us  [the longest x1 4.43 us: body(): got = lax.ppermute(give, CORE, swap)]
    all_to_all x2 -> x1, waiting for transfers between devices: 7.65 us -> 0.82 us  [to_all(): return lax.all_to_all(pieces, axis, 0, 0, tiled=True)]
    all_to_all x1, starting transfers between devices: 10.2 us -> 5.48 us  [scattered(): lax.all_to_all(grads.reshape(lax.axis_size(CHIPS), -1, LAT), CHIPS, 0, 0,...]
    all_to_all x1, waiting for transfers between devices: 6.22 us -> 3.94 us  [scattered(): lax.all_to_all(grads.reshape(lax.axis_size(CHIPS), -1, LAT), CHIPS, 0, 0,...]
    ppermute x1, starting transfers between devices: 0.76 us -> 2.07 us  [body(): lax.ppermute(jnp.concatenate([low[:slots], r_own[slots:], high[:slots]]),...]
    pallas_call x1, Pallas kernels: 7.57 us -> 6.49 us  [call_forward(): pl.pallas_call(forward_kernel, out_shape=outs, in_specs=[scalars(), *insi...]
  transfers between devices with their start and end apart: 13 -> 14, of which waited for: 8 -> 7; matrix products, arithmetic and copies ran while one was open for 2% -> 3% of each run, Pallas kernels for 11% -> 11%
where the time goes in v6:
time: 91.6 us; the launch traced here: 91 us
  starting transfers between devices  34.3 us (37%)
  Pallas kernels  24.3 us (27%)
  waiting for transfers between devices  12.7 us (14%)
  blocking collectives  11.7 us (13%)
  local copies, waits for them, and re-layouts  3.48 us (4%)
  other arithmetic  2.97 us (3%)
  between operations  1.61 us (2%)
    all_to_all x1, blocking collectives, to_all(): return lax.all_to_all(pieces, axis, 0, 0, tiled=True)  11.7 us
    pallas_call x1, Pallas kernels, call_forward(): pl.pallas_call(forward_kernel, out_shape=outs, in_specs=[scalars(), *insi...  6.49 us
    ppermute x1, starting transfers between devices, body(): lax.ppermute(jnp.concatenate([up[:slots], out_mid[:slots], down[:slots],...  5.95 us
    all_to_all x1, starting transfers between devices, scattered(): lax.all_to_all(grads.reshape(lax.axis_size(CHIPS), -1, LAT), CHIPS, 0, 0,...  5.48 us
    pallas_call x1, Pallas kernels, call_backward(): pl.pallas_call(backward_kernel, out_shape=(shape((coarse, LAT), bf16), sh...  4.85 us
    ppermute x1, starting transfers between devices, body(): got = lax.ppermute(give, CORE, swap)  4.43 us
    all_to_all x1, starting transfers between devices, to_all(): return lax.all_to_all(pieces, axis, 0, 0, tiled=True)  3.97 us
    all_to_all x1, waiting for transfers between devices, scattered(): lax.all_to_all(grads.reshape(lax.axis_size(CHIPS), -1, LAT), CHIPS, 0, 0,...  3.94 us
  transfers between devices with their start and end apart: 14, of which 7 were waited for; matrix products, arithmetic and copies ran while one was open for 3% of the time, Pallas kernels for 11%

profile of v6, /device:TPU:1, one launch (start us, length us, event | category | flops | bytes accessed | tf_op | source)
XLA Modules:
  0.0 91.0 jit_solution(7646150735287020245)
XLA Ops:
  0.6 0.0 copy-start
  0.7 0.0 copy-start.2
  0.7 0.1 stack.15.place_ref.refs_0_
  0.8 0.6 copy-done
  1.3 0.0 copy-done.2
  1.4 0.9 %copy-done.3 = bf16[1024,128]{1,0:T(8,128)(2,1)S(1)} copy-done((bf16[1024,128]{1,0:T(8,128)(2,1)S(1)}, bf16[1024,128]{1,0:T(8,128)(2,1)}, u32[]{:S(2)}) %copy-start.3) | copy-done | bytes 262168
  2.3 1.4 %pick.1 = (bf16[768,128]{1,0:T(8,128)(2,1)S(1)}, bf16[768,128]{1,0:T(8,128)(2,1)S(1)}, bf16[512,128]{1,0:T(8,128)(2,1)S(1)}, s16[2048,128]{1,0:T(8,128)(2,1)S(1)}) custom-call(s32[5]{0:T(128)S(1)} %stack.15.place_ref.refs_0_, s32[1,8]{1,0:T(1,128)S(1)} %copy-done.2, s32[1,8,256]{2,1,0:T(8,128)S(1)} %copy-done, bf16[1024,128]{1,0:T(8,128)(2,1)S(1)} %copy-done.3), custom_call_target="tpu_custom_call" | custom-call | flops 536870912 | bytes 1048576 | tf_op jit(solution)/shard_map/pick/pallas_call | solution.py:442
  3.7 2.8 %collective-permute-start = (bf16[768,128]{1,0:T(8,128)(2,1)S(1)}, bf16[768,128]{1,0:T(8,128)(2,1)S(1)}, u32[]{:S(2)}, u32[]{:S(2)}) collective-permute-start(bf16[768,128]{1,0:T(8,128)(2,1)S(1)} %get-tuple-element.55), channel_id=1, source_target_pairs={{0,8},{8,16},{16,24},{24,32},{32,40},{40,48},{48,56},{56,64},{64,7... | collective-permute-start | bytes 589832 | tf_op jit(solution)/shard_map/ppermute | solution.py:601
  6.4 0.6 collective-permute-start.1
  7.7 0.0 copy-start.11
  7.8 0.7 copy-done.11
  8.5 1.3 %own_rows.3 = (bf16[4096,128]{1,0:T(8,128)(2,1)S(1)}, s16[4096,128]{1,0:T(8,128)(2,1)S(1)}) custom-call(s32[1]{0:T(128)S(6)} %copy.24.count_ref.refs_0_, s32[1,4096]{1,0:T(1,128)S(1)} %copy-done.11, bf16[1024,128]{1,0:T(8,128)(2,1)S(1)} %copy-done.3), custom_call_target="tpu_custom_call" | custom-call | flops 1073741824 | bytes 2097152 | tf_op jit(solution)/shard_map/own_rows/pallas_call | solution.py:465
  9.8 0.0 copy-done.1
  9.8 0.0 collective-permute-done.up_ref
  9.8 1.7 %collective-permute-done.1.down_ref = bf16[768,128]{1,0:T(8,128)(2,1)S(1)} collective-permute-done((bf16[768,128]{1,0:T(8,128)(2,1)S(1)}, bf16[768,128]{1,0:T(8,128)(2,1)S(1)}, u32[]{:S(2)}, u32[]{:S(2)}) %collective-permute-start.1) | collective-permute-done | bytes 196640 | tf_op jit(solution)/shard_map/ppermute | solution.py:602
  11.6 5.9 %collective-permute-start.3 = (bf16[800,128]{1,0:T(8,128)(2,1)S(1)}, bf16[800,128]{1,0:T(8,128)(2,1)S(1)}, u32[]{:S(2)}, u32[]{:S(2)}) collective-permute-start(bf16[800,128]{1,0:T(8,128)(2,1)S(1)} %pad_maximum_fusion.1), channel_id=1, source_target_pairs={{0,7},{1,0},{2,1},{3,2},{4,3},{5,4},{6,5},{7,6},{8,15},{9,8},{10,9... | collective-permute-start | bytes 614408 | tf_op jit(solution)/shard_map/ppermute | solution.py:613
  17.5 0.0 copy-start.5
  17.6 0.0 copy-start.6
  17.6 0.0 copy-start.7
  17.6 0.0 copy-start.8
  17.6 0.3 collective-permute-start.2
  17.9 0.4 copy-done.12
  18.2 1.3 %own_rows.2 = (bf16[4096,128]{1,0:T(8,128)(2,1)S(1)}, s16[4096,128]{1,0:T(8,128)(2,1)S(1)}) custom-call(s32[1]{0:T(128)S(6)} %copy.24.count_ref.refs_0_, s32[1,4096]{1,0:T(1,128)S(1)} %copy-done.12, bf16[1024,128]{1,0:T(8,128)(2,1)S(1)} %copy-done.3), custom_call_target="tpu_custom_call" | custom-call | flops 1073741824 | bytes 2097152 | tf_op jit(solution)/shard_map/own_rows/pallas_call | solution.py:465
  19.6 0.0 copy-start.13
  19.6 0.7 collective-permute-done.3.ydown_ref
  20.2 3.4 %collective-permute-done.2.yup_ref = bf16[800,128]{1,0:T(8,128)(2,1)S(1)} collective-permute-done((bf16[800,128]{1,0:T(8,128)(2,1)S(1)}, bf16[800,128]{1,0:T(8,128)(2,1)S(1)}, u32[]{:S(2)}, u32[]{:S(2)}) %collective-permute-start.2) | collective-permute-done | bytes 204832 | tf_op jit(solution)/shard_map/ppermute | solution.py:606
  23.7 0.0 copy-done.5
  23.7 0.0 copy-done.6
  23.7 0.0 copy-done.7
  23.7 0.0 copy-done.8
  23.7 0.0 copy-start.4
  23.7 0.0 copy-start.10
  23.7 6.5 %forward.1 = (bf16[4096,128]{1,0:T(8,128)(2,1)S(1)}, bf16[4096,128]{1,0:T(8,128)(2,1)S(1)}, bf16[4096,128]{1,0:T(8,128)(2,1)S(1)}, bf16[1024,128]{1,0:T(8,128)(2...) custom-call(s32[1]{0:T(128)S(6)} %copy.24.count_ref.refs_0_, ...), custom_call_target="tpu_custom_call" | custom-call | flops 4294967296 | bytes 8388608 | tf_op jit(solution)/shard_map/forward/pallas_call | solution.py:482
  30.2 0.0 collective-permute-start.4
  30.2 2.7 %collective-permute-start.5 = (bf16[64,128]{1,0:T(8,128)(2,1)S(1)}, bf16[64,128]{1,0:T(8,128)(2,1)S(1)}, u32[]{:S(2)}, u32[]{:S(2)}) collective-permute-start(bf16[64,128]{1,0:T(8,128)(2,1)S(1)} %get-tuple-element.68), channel_id=1, source_target_pairs={{0,7},{1,0},{2,1},{3,2},{4,3},{5,4},{6,5},{7,6},{8,15},{9,8},{10,9... | collective-permute-start | bytes 49160 | tf_op jit(solution)/shard_map/ppermute | solution.py:641
  32.9 1.1 %collective-permute-done.4.nlow_ref = bf16[64,128]{1,0:T(8,128)(2,1)S(1)} collective-permute-done((bf16[64,128]{1,0:T(8,128)(2,1)S(1)}, bf16[64,128]{1,0:T(8,128)(2,1)S(1)}, u32[]{:S(2)}, u32[]{:S(2)}) %collective-permute-start.4) | collective-permute-done | bytes 16416 | tf_op jit(solution)/shard_map/ppermute | solution.py:640
  34.0 0.0 collective-permute-done.5.nhigh_ref
  34.0 4.8 %backward.1 = (bf16[128,128]{1,0:T(8,128)(2,1)}, f32[1024,128]{1,0:T(8,128)S(1)}, bf16[4096,128]{1,0:T(8,128)(2,1)S(1)}, bf16[512,128]{1,0:T(8,128)(2,1)S(1)}, bf16[512,128]{1,0:T(8,128)(2,1)S(1)}) custom-call(s32[5]{0:T(128)S(1)} %stack.15.place_ref.refs_0_, s16[4096,128]{1,0:T(8,128)(2,1)S(1)} %get-tuple-element.53.rcol_ref, ...), custom_call_target="tpu_custom_call" | custom-call | flops 2147483648 | bytes 8388608 | tf_op jit(solution)/shard_map/backward/pallas_call | solution.py:497
  38.9 4.4 %collective-permute-start.6 = (bf16[512,128]{1,0:T(8,128)(2,1)S(1)}, bf16[512,128]{1,0:T(8,128)(2,1)S(1)}, u32[]{:S(2)}, u32[]{:S(2)}) collective-permute-start(bf16[512,128]{1,0:T(8,128)(2,1)S(1)} %get-tuple-element.75), channel_id=1, source_target_pairs={{0,8},{8,0},{1,9},{9,1},{2,10},{10,2},{3,11},{11,3},{4,12},{12,4},... | collective-permute-start | bytes 393224 | tf_op jit(solution)/shard_map/ppermute | solution.py:668
  43.3 1.0 %collective-permute-done.6 = bf16[512,128]{1,0:T(8,128)(2,1)S(1)} collective-permute-done((bf16[512,128]{1,0:T(8,128)(2,1)S(1)}, bf16[512,128]{1,0:T(8,128)(2,1)S(1)}, u32[]{:S(2)}, u32[]{:S(2)}) %collective-permute-start.6) | collective-permute-done | bytes 131104 | tf_op jit(solution)/shard_map/ppermute | solution.py:668
  44.3 0.7 add_convert_fusion
  45.0 5.5 %all-to-all-start = ((bf16[16,32,128]{2,1,0:T(8,128)(2,1)}), bf16[16,32,128]{2,1,0:T(8,128)(2,1)S(1)}, u32[]{:S(2)}, u32[]{:S(2)}) async-start(bf16[16,32,128]{2,1,0:T(8,128)(2,1)} %bitcast.3), calls=%async_computation | async-start | bytes 262144 | tf_op jit(solution)/shard_map/all_to_all | solution.py:431
  50.5 2.7 %ghost_grads.1 = (bf16[768,128]{1,0:T(8,128)(2,1)S(1)}, bf16[768,128]{1,0:T(8,128)(2,1)S(1)}, bf16[512,128]{1,0:T(8,128)(2,1)S(1)}) custom-call(s32[1]{0:T(128)S(6)} %copy.24.count_ref.refs_0_, s32[1,4096]{1,0:T(1,128)S(1)} %copy-done.12, bf16[4096,128]{1,0:T(8,128)(2,1)S(1)} %get-tuple-element.76.refs_2_.dedge_ref, bf16[256,128]{1,0:T(8,128)(2,1)S(1)} %copy-done.6), custom_call_target="tpu_custom_call" | custom-call | flops 2147483648 | bytes 3145728 | tf_op jit(solution)/shard_map/ghost_grads/pallas_call | solution.py:519
  53.2 3.9 %all-to-all-done = bf16[16,32,128]{2,1,0:T(8,128)(2,1)S(1)} async-done(((bf16[16,32,128]{2,1,0:T(8,128)(2,1)}), bf16[16,32,128]{2,1,0:T(8,128)(2,1)S(1)}, u32[]{:S(2)}, u32[]{:S(2)}) %all-to-all-start) | async-done | bytes 131104 | tf_op jit(solution)/shard_map/all_to_all | solution.py:431
  57.2 0.1 collective-permute-start.7
  57.3 3.0 %collective-permute-start.8 = (bf16[768,128]{1,0:T(8,128)(2,1)S(1)}, bf16[768,128]{1,0:T(8,128)(2,1)S(1)}, u32[]{:S(2)}, u32[]{:S(2)}) collective-permute-start(bf16[768,128]{1,0:T(8,128)(2,1)S(1)} %get-tuple-element.83), channel_id=1, source_target_pairs={{0,7},{1,0},{2,1},{3,2},{4,3},{5,4},{6,5},{7,6},{8,15},{9,8},{10,9... | collective-permute-start | bytes 589832 | tf_op jit(solution)/shard_map/ppermute | solution.py:672
  60.3 0.6 broadcast_in_dim.4
  61.0 4.0 %all-to-all-start.1 = ((bf16[8,32,128]{2,1,0:T(8,128)(2,1)}), bf16[8,32,128]{2,1,0:T(8,128)(2,1)}, u32[]{:S(2)}, u32[]{:S(2)}) async-start(bf16[8,32,128]{2,1,0:T(8,128)(2,1)} %broadcast_in_dim.4), calls=%async_computation.1 | async-start | bytes 131072 | tf_op jit(solution)/shard_map/all_to_all | solution.py:437
  65.0 0.0 collective-permute-done.7.mid_low_ref
  65.0 0.0 collective-permute-done.8.mid_high_ref
  65.0 0.7 pad_maximum_fusion.3
  65.7 2.1 %collective-permute-start.10 = (bf16[768,128]{1,0:T(8,128)(2,1)}, bf16[768,128]{1,0:T(8,128)(2,1)S(1)}, u32[]{:S(2)}, u32[]{:S(2)}) collective-permute-start(bf16[768,128]{1,0:T(8,128)(2,1)} %pad_maximum_fusion.3), channel_id=1, source_target_pairs={{0,248},{8,0},{16,8},{24,16},{32,24},{40,32},{48,40},{56,48},{64,5... | collective-permute-start | bytes 589832 | tf_op jit(solution)/shard_map/ppermute | solution.py:676
  67.8 0.7 pad_maximum_fusion.2
  68.5 0.1 collective-permute-start.9
  68.5 2.8 %local.1.part_ref = f32[1024,128]{1,0:T(8,128)S(1)} custom-call(s32[1]{0:T(128)S(6)} %copy.24.count_ref.refs_0_, s32[1,4096]{1,0:T(1,128)S(1)} %copy-done.12, s32[1,4096]{1,0:T(1,128)S(1)} %copy-done.11, bf16[4096,128]{1,0:T(8,128)(2,1)S(1)} %get-tuple-element.76.refs_2_.dedge_ref, f32[1024,128]{1,0:T(8,128)S(1)} %get-tuple-element.84.dnode_ref, ...), custom_call_target="tpu_custom_call" | custom-call | flops 2147483648 | bytes 3145728 | tf_op jit(solution)/shard_map/local/pallas_call | solution.py:535
  71.3 0.8 all-to-all-done.1
  72.2 0.9 reduce_sum.25
  73.0 0.0 collective-permute-done.10.up_ref
  73.0 0.0 collective-permute-done.9.down_ref
  73.1 11.7 %all_to_all.15 = bf16[16,32,128]{2,1,0:T(8,128)(2,1)S(1)} all-to-all(bf16[16,32,128]{2,1,0:T(8,128)(2,1)S(1)} %broadcast_in_dim.5), channel_id=1, replica_groups=mesh['gx_0'=4,'gx_1'=4,'gx_2'=2,'gy'=8] {'gx_0','gx_1'}, dimensions={0} | all-to-all | bytes 262144 | tf_op jit(solution)/shard_map/all_to_all | solution.py:437
  84.7 2.8 %collective-permute-start.11 = (bf16[512,128]{1,0:T(8,128)(2,1)S(1)}, bf16[512,128]{1,0:T(8,128)(2,1)S(1)}, u32[]{:S(2)}, u32[]{:S(2)}) collective-permute-start(bf16[512,128]{1,0:T(8,128)(2,1)S(1)} %bitcast.5), channel_id=1, source_target_pairs={{0,8},{8,0},{1,9},{9,1},{2,10},{10,2},{3,11},{11,3},{4,12},{12,4},... | collective-permute-start | bytes 393224 | tf_op jit(solution)/shard_map/ppermute | solution.py:684
  87.5 2.1 %returned.1 = f32[1024,128]{1,0:T(8,128)} custom-call(s32[5]{0:T(128)S(1)} %stack.15.place_ref.refs_0_, s32[1,8]{1,0:T(1,128)S(1)} %copy-done.2, s32[1,8,256]{2,1,0:T(8,128)S(1)} %copy-done, s16[2048,128]{1,0:T(8,128)(2,1)S(1)} %get-tuple-element.73.cols_ref, bf16[768,128]{1,0:T(8,128)(2,1)S(1)} %collective-permute-done.9.down_ref, ...), custom_call_target="tpu_custom_call" | custom-call | flops 536870912 | bytes 2097152 | tf_op jit(solution)/shard_map/returned/pallas_call | solution.py:548
  89.6 0.0 collective-permute-done.11.refs_2_
  89.6 1.4 %scaled.1 = (f32[256,128]{1,0:T(8,128)}, f32[128,128]{1,0:T(8,128)}, f32[256,128]{1,0:T(8,128)}, f32[128,128]{1,0:T(8,128)}, f32[128,128]{1,0:T(8,128)}, /*index=5*/f32[128,128]{1,0:T(8,128)}) custom-call(s32[5]{0:T(128)S(1)} %stack.15.place_ref.refs_0_, bf16[512,128]{1,0:T(8,128)(2,1)S(1)} %bitcast.6, bf16[512,128]{1,0:T(8,128)(2,1)S(1)} %collective-permute-done.11.refs_2_), custom_call_target="tpu_custom_call" | custom-call | tf_op jit(solution)/shard_map/scaled/pallas_call | solution.py:561
  (20 shorter events, 0.2 us)
Async XLA Ops:
  0.6 0.7 copy-start
  0.7 0.7 copy-start.2
  1.3 1.0 %copy-start.3 = (bf16[1024,128]{1,0:T(8,128)(2,1)S(1)}, bf16[1024,128]{1,0:T(8,128)(2,1)}, u32[]{:S(2)}) copy-start(bf16[1024,128]{1,0:T(8,128)(2,1)} %nodes_ref.7) | copy-start | bytes 786436
  3.7 6.1 %collective-permute-start = (bf16[768,128]{1,0:T(8,128)(2,1)S(1)}, bf16[768,128]{1,0:T(8,128)(2,1)S(1)}, u32[]{:S(2)}, u32[]{:S(2)}) collective-permute-start(bf16[768,128]{1,0:T(8,128)(2,1)S(1)} %get-tuple-element.55), channel_id=1, source_target_pairs={{0,8},{8,16},{16,24},{24,32},{32,40},{40,48},{48,56},{56,64},{64,7... | collective-permute-start | bytes 589832 | tf_op jit(solution)/shard_map/ppermute | solution.py:601
  6.4 5.1 %collective-permute-start.1 = (bf16[768,128]{1,0:T(8,128)(2,1)S(1)}, bf16[768,128]{1,0:T(8,128)(2,1)S(1)}, u32[]{:S(2)}, u32[]{:S(2)}) collective-permute-start(bf16[768,128]{1,0:T(8,128)(2,1)S(1)} %get-tuple-element.56), channel_id=1, source_target_pairs={{0,248},{8,0},{16,8},{24,16},{32,24},{40,32},{48,40},{56,48},{64,5... | collective-permute-start | bytes 589832 | tf_op jit(solution)/shard_map/ppermute | solution.py:602
  7.7 0.7 copy-start.11
  8.5 1.3 %copy-start.1 = (bf16[128,128]{1,0:T(8,128)(2,1)S(1)}, bf16[128,128]{1,0:T(8,128)(2,1)}, u32[]{:S(2)}) copy-start(bf16[128,128]{1,0:T(8,128)(2,1)} %dcoarse_ref.1) | copy-start | bytes 98308
  11.6 8.7 %collective-permute-start.3 = (bf16[800,128]{1,0:T(8,128)(2,1)S(1)}, bf16[800,128]{1,0:T(8,128)(2,1)S(1)}, u32[]{:S(2)}, u32[]{:S(2)}) collective-permute-start(bf16[800,128]{1,0:T(8,128)(2,1)S(1)} %pad_maximum_fusion.1), channel_id=1, source_target_pairs={{0,7},{1,0},{2,1},{3,2},{4,3},{5,4},{6,5},{7,6},{8,15},{9,8},{10,9... | collective-permute-start | bytes 614408 | tf_op jit(solution)/shard_map/ppermute | solution.py:613
  17.5 0.7 copy-start.12
  17.5 6.1 %copy-start.5 = (bf16[256,128]{1,0:T(8,128)(2,1)S(1)}, bf16[256,128]{1,0:T(8,128)(2,1)}, u32[]{:S(2)}) copy-start(bf16[256,128]{1,0:T(8,128)(2,1)} %wni_ref.3) | copy-start | bytes 196612
  17.6 6.1 %copy-start.6 = (bf16[256,128]{1,0:T(8,128)(2,1)S(1)}, bf16[256,128]{1,0:T(8,128)(2,1)}, u32[]{:S(2)}) copy-start(bf16[256,128]{1,0:T(8,128)(2,1)} %wei_ref.5) | copy-start | bytes 196612
  17.6 6.1 %copy-start.7 = (bf16[128,128]{1,0:T(8,128)(2,1)S(1)}, bf16[128,128]{1,0:T(8,128)(2,1)}, u32[]{:S(2)}) copy-start(bf16[128,128]{1,0:T(8,128)(2,1)} %weo_ref.3) | copy-start | bytes 98308
  17.6 6.1 %copy-start.8 = (bf16[128,128]{1,0:T(8,128)(2,1)S(1)}, bf16[128,128]{1,0:T(8,128)(2,1)}, u32[]{:S(2)}) copy-start(bf16[128,128]{1,0:T(8,128)(2,1)} %wno_ref.3) | copy-start | bytes 98308
  17.6 6.1 %collective-permute-start.2 = (bf16[800,128]{1,0:T(8,128)(2,1)S(1)}, bf16[800,128]{1,0:T(8,128)(2,1)S(1)}, u32[]{:S(2)}, u32[]{:S(2)}) collective-permute-start(bf16[800,128]{1,0:T(8,128)(2,1)S(1)} %pad_maximum_fusion), channel_id=1, source_target_pairs={{0,1},{1,2},{2,3},{3,4},{4,5},{5,6},{6,7},{7,0},{8,9},{9,10},{10,1... | collective-permute-start | bytes 614408 | tf_op jit(solution)/shard_map/ppermute | solution.py:606
  19.6 4.1 %copy-start.13 = (s32[1,1024]{1,0:T(1,128)S(1)}, s32[1,1024]{1,0:T(1,128)}, u32[]{:S(2)}) copy-start(s32[1,1024]{1,0:T(1,128)} %pool_ref.3) | copy-start | bytes 12292
  23.7 10.3 %copy-start.4 = (bf16[1024,128]{1,0:T(8,128)(2,1)S(1)}, bf16[1024,128]{1,0:T(8,128)(2,1)}, u32[]{:S(2)}) copy-start(bf16[1024,128]{1,0:T(8,128)(2,1)} %dfine_ref.1) | copy-start | bytes 786436
  23.7 10.3 %copy-start.10 = (bf16[128,128]{1,0:T(8,128)(2,1)S(1)}, bf16[128,128]{1,0:T(8,128)(2,1)}, u32[]{:S(2)}) copy-start(bf16[128,128]{1,0:T(8,128)(2,1)} %wco_ref.1) | copy-start | bytes 98308
  30.2 3.8 %copy-start.9 = (bf16[128,128]{1,0:T(8,128)(2,1)S(1)}, bf16[128,128]{1,0:T(8,128)(2,1)}, u32[]{:S(2)}) copy-start(bf16[128,128]{1,0:T(8,128)(2,1)} %wci_ref.1) | copy-start | bytes 98308
  30.2 3.8 %collective-permute-start.4 = (bf16[64,128]{1,0:T(8,128)(2,1)S(1)}, bf16[64,128]{1,0:T(8,128)(2,1)S(1)}, u32[]{:S(2)}, u32[]{:S(2)}) collective-permute-start(bf16[64,128]{1,0:T(8,128)(2,1)S(1)} %get-tuple-element.67), channel_id=1, source_target_pairs={{0,1},{1,2},{2,3},{3,4},{4,5},{5,6},{6,7},{7,0},{8,9},{9,10},{10,1... | collective-permute-start | bytes 49160 | tf_op jit(solution)/shard_map/ppermute | solution.py:640
  30.2 3.8 %collective-permute-start.5 = (bf16[64,128]{1,0:T(8,128)(2,1)S(1)}, bf16[64,128]{1,0:T(8,128)(2,1)S(1)}, u32[]{:S(2)}, u32[]{:S(2)}) collective-permute-start(bf16[64,128]{1,0:T(8,128)(2,1)S(1)} %get-tuple-element.68), channel_id=1, source_target_pairs={{0,7},{1,0},{2,1},{3,2},{4,3},{5,4},{6,5},{7,6},{8,15},{9,8},{10,9... | collective-permute-start | bytes 49160 | tf_op jit(solution)/shard_map/ppermute | solution.py:641
  38.9 5.4 %collective-permute-start.6 = (bf16[512,128]{1,0:T(8,128)(2,1)S(1)}, bf16[512,128]{1,0:T(8,128)(2,1)S(1)}, u32[]{:S(2)}, u32[]{:S(2)}) collective-permute-start(bf16[512,128]{1,0:T(8,128)(2,1)S(1)} %get-tuple-element.75), channel_id=1, source_target_pairs={{0,8},{8,0},{1,9},{9,1},{2,10},{10,2},{3,11},{11,3},{4,12},{12,4},... | collective-permute-start | bytes 393224 | tf_op jit(solution)/shard_map/ppermute | solution.py:668
  45.0 12.2 %all-to-all-start = ((bf16[16,32,128]{2,1,0:T(8,128)(2,1)}), bf16[16,32,128]{2,1,0:T(8,128)(2,1)S(1)}, u32[]{:S(2)}, u32[]{:S(2)}) async-start(bf16[16,32,128]{2,1,0:T(8,128)(2,1)} %bitcast.3), calls=%async_computation | async-start | bytes 262144 | tf_op jit(solution)/shard_map/all_to_all | solution.py:431
  57.2 7.8 %collective-permute-start.7 = (bf16[768,128]{1,0:T(8,128)(2,1)S(1)}, bf16[768,128]{1,0:T(8,128)(2,1)S(1)}, u32[]{:S(2)}, u32[]{:S(2)}) collective-permute-start(bf16[768,128]{1,0:T(8,128)(2,1)S(1)} %get-tuple-element.81), channel_id=1, source_target_pairs={{0,1},{1,2},{2,3},{3,4},{4,5},{5,6},{6,7},{7,0},{8,9},{9,10},{10,1... | collective-permute-start | bytes 589832 | tf_op jit(solution)/shard_map/ppermute | solution.py:673
  57.3 7.7 %collective-permute-start.8 = (bf16[768,128]{1,0:T(8,128)(2,1)S(1)}, bf16[768,128]{1,0:T(8,128)(2,1)S(1)}, u32[]{:S(2)}, u32[]{:S(2)}) collective-permute-start(bf16[768,128]{1,0:T(8,128)(2,1)S(1)} %get-tuple-element.83), channel_id=1, source_target_pairs={{0,7},{1,0},{2,1},{3,2},{4,3},{5,4},{6,5},{7,6},{8,15},{9,8},{10,9... | collective-permute-start | bytes 589832 | tf_op jit(solution)/shard_map/ppermute | solution.py:672
  61.0 11.2 %all-to-all-start.1 = ((bf16[8,32,128]{2,1,0:T(8,128)(2,1)}), bf16[8,32,128]{2,1,0:T(8,128)(2,1)}, u32[]{:S(2)}, u32[]{:S(2)}) async-start(bf16[8,32,128]{2,1,0:T(8,128)(2,1)} %broadcast_in_dim.4), calls=%async_computation.1 | async-start | bytes 131072 | tf_op jit(solution)/shard_map/all_to_all | solution.py:437
  65.7 7.3 %collective-permute-start.10 = (bf16[768,128]{1,0:T(8,128)(2,1)}, bf16[768,128]{1,0:T(8,128)(2,1)S(1)}, u32[]{:S(2)}, u32[]{:S(2)}) collective-permute-start(bf16[768,128]{1,0:T(8,128)(2,1)} %pad_maximum_fusion.3), channel_id=1, source_target_pairs={{0,248},{8,0},{16,8},{24,16},{32,24},{40,32},{48,40},{56,48},{64,5... | collective-permute-start | bytes 589832 | tf_op jit(solution)/shard_map/ppermute | solution.py:676
  68.5 4.6 %collective-permute-start.9 = (bf16[768,128]{1,0:T(8,128)(2,1)}, bf16[768,128]{1,0:T(8,128)(2,1)S(1)}, u32[]{:S(2)}, u32[]{:S(2)}) collective-permute-start(bf16[768,128]{1,0:T(8,128)(2,1)} %pad_maximum_fusion.2), channel_id=1, source_target_pairs={{0,8},{8,16},{16,24},{24,32},{32,40},{40,48},{48,56},{56,64},{64,7... | collective-permute-start | bytes 589832 | tf_op jit(solution)/shard_map/ppermute | solution.py:679
  84.7 4.9 %collective-permute-start.11 = (bf16[512,128]{1,0:T(8,128)(2,1)S(1)}, bf16[512,128]{1,0:T(8,128)(2,1)S(1)}, u32[]{:S(2)}, u32[]{:S(2)}) collective-permute-start(bf16[512,128]{1,0:T(8,128)(2,1)S(1)} %bitcast.5), channel_id=1, source_target_pairs={{0,8},{8,0},{1,9},{9,1},{2,10},{10,2},{3,11},{11,3},{4,12},{12,4},... | collective-permute-start | bytes 393224 | tf_op jit(solution)/shard_map/ppermute | solution.py:684

commit v7 on v6

--- a/solution.py
+++ b/solution.py
@@ -681,10 +681,11 @@
     )
     own, ret_down, ret_up, d_own = lax.optimization_barrier((own, ret_down, ret_up, d_own))
     half = to_all(own, CHIPS).reshape(keep.shape)
-    other = lax.ppermute(half, CORE, swap)
     grad_nodes = call_return(
         place, ghost_count, ghost_rows, gcol, ret_down, ret_up, low, high, d_own
     )
+    half, grad_nodes = lax.optimization_barrier((half, grad_nodes))
+    other = lax.ppermute(half, CORE, swap)
     scaled = call_scale(1.0 / (owned * n_gx * n_gy) ** 0.5, place, half, other)
     return (fine_out, coarse_out, grad_nodes, *scaled)
 

time: 91.6 us -> 94.4 us (1.031)
  blocking collectives: 11.7 us -> 0 us
  starting transfers between devices: 34.3 us -> 42.8 us
  waiting for transfers between devices: 12.7 us -> 18.6 us
  other arithmetic: 2.97 us -> 1.46 us
  local copies, waits for them, and re-layouts: 3.48 us -> 4.93 us
    all_to_all x1 -> x0, blocking collectives: 11.7 us -> none  [to_all(): return lax.all_to_all(pieces, axis, 0, 0, tiled=True)]
    all_to_all x1 -> x2, starting transfers between devices: 3.97 us -> 9.89 us  [to_all(): return lax.all_to_all(pieces, axis, 0, 0, tiled=True)]
    all_to_all x1 -> x2, waiting for transfers between devices: 0.82 us -> 4.58 us  [to_all(): return lax.all_to_all(pieces, axis, 0, 0, tiled=True)]
    ppermute x1, starting transfers between devices: 2.81 us -> 4.24 us  [body(): other = lax.ppermute(half, CORE, swap)]
    ppermute x1, starting transfers between devices: 2.07 us -> 3.3 us  [body(): lax.ppermute(jnp.concatenate([low[:slots], r_own[slots:], high[:slots]]),...]
    ppermute x1, waiting for transfers between devices: 0.01 us -> 1.08 us  [body(): low = lax.ppermute(r_up, 'gy', ring(n_gy, 1))]
    ppermute x1, waiting for transfers between devices: 0.01 us -> 0.99 us  [body(): other = lax.ppermute(half, CORE, swap)]
    unnamed x28 -> x32, local copies, waits for them, and re-layouts: 2.67 us -> 3.47 us
  transfers between devices with their start and end apart: 14 -> 15, of which waited for: 7 -> 10; matrix products, arithmetic and copies ran while one was open for 3% -> 2% of each run, Pallas kernels for 11% -> 11%
where the time goes in v7:
time: 94.4 us; the launch traced here: 93.7 us
  starting transfers between devices  42.8 us (45%)
  Pallas kernels  24.3 us (26%)
  waiting for transfers between devices  18.6 us (20%)
  local copies, waits for them, and re-layouts  4.93 us (5%)
  between operations  1.6 us (2%)
  other arithmetic  1.46 us (2%)
    all_to_all x2, starting transfers between devices, to_all(): return lax.all_to_all(pieces, axis, 0, 0, tiled=True)  9.89 us
    pallas_call x1, Pallas kernels, call_forward(): pl.pallas_call(forward_kernel, out_shape=outs, in_specs=[scalars(), *insi...  6.49 us
    ppermute x1, starting transfers between devices, body(): lax.ppermute(jnp.concatenate([up[:slots], out_mid[:slots], down[:slots],...  5.95 us
    all_to_all x1, starting transfers between devices, scattered(): lax.all_to_all(grads.reshape(lax.axis_size(CHIPS), -1, LAT), CHIPS, 0, 0,...  5.48 us
    pallas_call x1, Pallas kernels, call_backward(): pl.pallas_call(backward_kernel, out_shape=(shape((coarse, LAT), bf16), sh...  4.85 us
    all_to_all x2, waiting for transfers between devices, to_all(): return lax.all_to_all(pieces, axis, 0, 0, tiled=True)  4.58 us
    ppermute x1, starting transfers between devices, body(): got = lax.ppermute(give, CORE, swap)  4.43 us
    ppermute x1, starting transfers between devices, body(): other = lax.ppermute(half, CORE, swap)  4.24 us
  transfers between devices with their start and end apart: 15, of which 10 were waited for; matrix products, arithmetic and copies ran while one was open for 2% of the time, Pallas kernels for 11%

profile of v7, /device:TPU:1, one launch (start us, length us, event | category | flops | bytes accessed | tf_op | source)
XLA Modules:
  0.0 93.7 jit_solution(10073937715699058697)
XLA Ops:
  0.6 0.0 copy-start
  0.7 0.0 copy-start.2
  0.7 0.1 stack.15.place_ref.refs_0_
  0.8 0.6 copy-done
  1.3 0.0 copy-done.2
  1.4 0.9 %copy-done.3 = bf16[1024,128]{1,0:T(8,128)(2,1)S(1)} copy-done((bf16[1024,128]{1,0:T(8,128)(2,1)S(1)}, bf16[1024,128]{1,0:T(8,128)(2,1)}, u32[]{:S(2)}) %copy-start.3) | copy-done | bytes 262168
  2.3 1.4 %pick.1 = (bf16[768,128]{1,0:T(8,128)(2,1)S(1)}, bf16[768,128]{1,0:T(8,128)(2,1)S(1)}, bf16[512,128]{1,0:T(8,128)(2,1)S(1)}, s16[2048,128]{1,0:T(8,128)(2,1)S(1)}) custom-call(s32[5]{0:T(128)S(1)} %stack.15.place_ref.refs_0_, s32[1,8]{1,0:T(1,128)S(1)} %copy-done.2, s32[1,8,256]{2,1,0:T(8,128)S(1)} %copy-done, bf16[1024,128]{1,0:T(8,128)(2,1)S(1)} %copy-done.3), custom_call_target="tpu_custom_call" | custom-call | flops 536870912 | bytes 1048576 | tf_op jit(solution)/shard_map/pick/pallas_call | solution.py:442
  3.7 2.8 %collective-permute-start = (bf16[768,128]{1,0:T(8,128)(2,1)S(1)}, bf16[768,128]{1,0:T(8,128)(2,1)S(1)}, u32[]{:S(2)}, u32[]{:S(2)}) collective-permute-start(bf16[768,128]{1,0:T(8,128)(2,1)S(1)} %get-tuple-element.57), channel_id=1, source_target_pairs={{0,8},{8,16},{16,24},{24,32},{32,40},{40,48},{48,56},{56,64},{64,7... | collective-permute-start | bytes 589832 | tf_op jit(solution)/shard_map/ppermute | solution.py:601
  6.4 0.6 collective-permute-start.1
  7.7 0.0 copy-start.11
  7.8 0.7 copy-done.11
  8.5 1.3 %own_rows.3 = (bf16[4096,128]{1,0:T(8,128)(2,1)S(1)}, s16[4096,128]{1,0:T(8,128)(2,1)S(1)}) custom-call(s32[1]{0:T(128)S(6)} %copy.24.count_ref.refs_0_, s32[1,4096]{1,0:T(1,128)S(1)} %copy-done.11, bf16[1024,128]{1,0:T(8,128)(2,1)S(1)} %copy-done.3), custom_call_target="tpu_custom_call" | custom-call | flops 1073741824 | bytes 2097152 | tf_op jit(solution)/shard_map/own_rows/pallas_call | solution.py:465
  9.8 0.0 copy-done.1
  9.8 0.0 collective-permute-done.up_ref
  9.8 1.7 %collective-permute-done.1.down_ref = bf16[768,128]{1,0:T(8,128)(2,1)S(1)} collective-permute-done((bf16[768,128]{1,0:T(8,128)(2,1)S(1)}, bf16[768,128]{1,0:T(8,128)(2,1)S(1)}, u32[]{:S(2)}, u32[]{:S(2)}) %collective-permute-start.1) | collective-permute-done | bytes 196640 | tf_op jit(solution)/shard_map/ppermute | solution.py:602
  11.6 5.9 %collective-permute-start.3 = (bf16[800,128]{1,0:T(8,128)(2,1)S(1)}, bf16[800,128]{1,0:T(8,128)(2,1)S(1)}, u32[]{:S(2)}, u32[]{:S(2)}) collective-permute-start(bf16[800,128]{1,0:T(8,128)(2,1)S(1)} %pad_maximum_fusion.1), channel_id=1, source_target_pairs={{0,7},{1,0},{2,1},{3,2},{4,3},{5,4},{6,5},{7,6},{8,15},{9,8},{10,9... | collective-permute-start | bytes 614408 | tf_op jit(solution)/shard_map/ppermute | solution.py:613
  17.5 0.0 copy-start.5
  17.6 0.0 copy-start.6
  17.6 0.0 copy-start.7
  17.6 0.0 copy-start.8
  17.6 0.3 collective-permute-start.2
  17.9 0.4 copy-done.12
  18.2 1.3 %own_rows.2 = (bf16[4096,128]{1,0:T(8,128)(2,1)S(1)}, s16[4096,128]{1,0:T(8,128)(2,1)S(1)}) custom-call(s32[1]{0:T(128)S(6)} %copy.24.count_ref.refs_0_, s32[1,4096]{1,0:T(1,128)S(1)} %copy-done.12, bf16[1024,128]{1,0:T(8,128)(2,1)S(1)} %copy-done.3), custom_call_target="tpu_custom_call" | custom-call | flops 1073741824 | bytes 2097152 | tf_op jit(solution)/shard_map/own_rows/pallas_call | solution.py:465
  19.6 0.0 copy-start.13
  19.6 0.7 collective-permute-done.3.ydown_ref
  20.2 3.4 %collective-permute-done.2.yup_ref = bf16[800,128]{1,0:T(8,128)(2,1)S(1)} collective-permute-done((bf16[800,128]{1,0:T(8,128)(2,1)S(1)}, bf16[800,128]{1,0:T(8,128)(2,1)S(1)}, u32[]{:S(2)}, u32[]{:S(2)}) %collective-permute-start.2) | collective-permute-done | bytes 204832 | tf_op jit(solution)/shard_map/ppermute | solution.py:606
  23.7 0.0 copy-done.5
  23.7 0.0 copy-start.4
  23.7 0.0 copy-start.10
  23.7 6.5 %forward.1 = (bf16[4096,128]{1,0:T(8,128)(2,1)S(1)}, bf16[4096,128]{1,0:T(8,128)(2,1)S(1)}, bf16[4096,128]{1,0:T(8,128)(2,1)S(1)}, bf16[1024,128]{1,0:T(8,128)(2...) custom-call(s32[1]{0:T(128)S(6)} %copy.24.count_ref.refs_0_, ...), custom_call_target="tpu_custom_call" | custom-call | flops 4294967296 | bytes 8388608 | tf_op jit(solution)/shard_map/forward/pallas_call | solution.py:482
  30.2 0.0 collective-permute-start.4
  30.2 2.7 %collective-permute-start.5 = (bf16[64,128]{1,0:T(8,128)(2,1)S(1)}, bf16[64,128]{1,0:T(8,128)(2,1)S(1)}, u32[]{:S(2)}, u32[]{:S(2)}) collective-permute-start(bf16[64,128]{1,0:T(8,128)(2,1)S(1)} %get-tuple-element.70), channel_id=1, source_target_pairs={{0,7},{1,0},{2,1},{3,2},{4,3},{5,4},{6,5},{7,6},{8,15},{9,8},{10,9... | collective-permute-start | bytes 49160 | tf_op jit(solution)/shard_map/ppermute | solution.py:641
  32.9 1.1 %collective-permute-done.4.nlow_ref = bf16[64,128]{1,0:T(8,128)(2,1)S(1)} collective-permute-done((bf16[64,128]{1,0:T(8,128)(2,1)S(1)}, bf16[64,128]{1,0:T(8,128)(2,1)S(1)}, u32[]{:S(2)}, u32[]{:S(2)}) %collective-permute-start.4) | collective-permute-done | bytes 16416 | tf_op jit(solution)/shard_map/ppermute | solution.py:640
  34.0 0.0 collective-permute-done.5.nhigh_ref
  34.0 0.0 copy-done.4
  34.0 4.8 %backward.1 = (bf16[128,128]{1,0:T(8,128)(2,1)}, f32[1024,128]{1,0:T(8,128)S(1)}, bf16[4096,128]{1,0:T(8,128)(2,1)S(1)}, bf16[512,128]{1,0:T(8,128)(2,1)S(1)}, bf16[512,128]{1,0:T(8,128)(2,1)S(1)}) custom-call(s32[5]{0:T(128)S(1)} %stack.15.place_ref.refs_0_, s16[4096,128]{1,0:T(8,128)(2,1)S(1)} %get-tuple-element.55.rcol_ref, ...), custom_call_target="tpu_custom_call" | custom-call | flops 2147483648 | bytes 8388608 | tf_op jit(solution)/shard_map/backward/pallas_call | solution.py:497
  38.9 0.8 copy-done.14
  39.7 4.4 %collective-permute-start.6 = (bf16[512,128]{1,0:T(8,128)(2,1)S(1)}, bf16[512,128]{1,0:T(8,128)(2,1)S(1)}, u32[]{:S(2)}, u32[]{:S(2)}) collective-permute-start(bf16[512,128]{1,0:T(8,128)(2,1)S(1)} %get-tuple-element.76), channel_id=1, source_target_pairs={{0,8},{8,0},{1,9},{9,1},{2,10},{10,2},{3,11},{11,3},{4,12},{12,4},... | collective-permute-start | bytes 393224 | tf_op jit(solution)/shard_map/ppermute | solution.py:668
  44.1 1.0 %collective-permute-done.6 = bf16[512,128]{1,0:T(8,128)(2,1)S(1)} collective-permute-done((bf16[512,128]{1,0:T(8,128)(2,1)S(1)}, bf16[512,128]{1,0:T(8,128)(2,1)S(1)}, u32[]{:S(2)}, u32[]{:S(2)}) %collective-permute-start.6) | collective-permute-done | bytes 131104 | tf_op jit(solution)/shard_map/ppermute | solution.py:668
  45.1 0.7 add_convert_fusion
  45.8 5.5 %all-to-all-start = ((bf16[16,32,128]{2,1,0:T(8,128)(2,1)}), bf16[16,32,128]{2,1,0:T(8,128)(2,1)S(1)}, u32[]{:S(2)}, u32[]{:S(2)}) async-start(bf16[16,32,128]{2,1,0:T(8,128)(2,1)} %bitcast.3), calls=%async_computation | async-start | bytes 262144 | tf_op jit(solution)/shard_map/all_to_all | solution.py:431
  51.3 2.8 %ghost_grads.1 = (bf16[768,128]{1,0:T(8,128)(2,1)S(1)}, bf16[768,128]{1,0:T(8,128)(2,1)S(1)}, bf16[512,128]{1,0:T(8,128)(2,1)S(1)}) custom-call(s32[1]{0:T(128)S(6)} %copy.24.count_ref.refs_0_, s32[1,4096]{1,0:T(1,128)S(1)} %copy-done.12, bf16[4096,128]{1,0:T(8,128)(2,1)S(1)} %get-tuple-element.77.refs_2_.dedge_ref, bf16[256,128]{1,0:T(8,128)(2,1)S(1)} %copy-done.6), custom_call_target="tpu_custom_call" | custom-call | flops 2147483648 | bytes 3145728 | tf_op jit(solution)/shard_map/ghost_grads/pallas_call | solution.py:519
  54.0 3.9 %all-to-all-done = bf16[16,32,128]{2,1,0:T(8,128)(2,1)S(1)} async-done(((bf16[16,32,128]{2,1,0:T(8,128)(2,1)}), bf16[16,32,128]{2,1,0:T(8,128)(2,1)S(1)}, u32[]{:S(2)}, u32[]{:S(2)}) %all-to-all-start) | async-done | bytes 131104 | tf_op jit(solution)/shard_map/all_to_all | solution.py:431
  58.0 3.0 %collective-permute-start.8 = (bf16[768,128]{1,0:T(8,128)(2,1)S(1)}, bf16[768,128]{1,0:T(8,128)(2,1)S(1)}, u32[]{:S(2)}, u32[]{:S(2)}) collective-permute-start(bf16[768,128]{1,0:T(8,128)(2,1)S(1)} %get-tuple-element.84), channel_id=1, source_target_pairs={{0,7},{1,0},{2,1},{3,2},{4,3},{5,4},{6,5},{7,6},{8,15},{9,8},{10,9... | collective-permute-start | bytes 589832 | tf_op jit(solution)/shard_map/ppermute | solution.py:672
  61.0 0.0 collective-permute-start.7
  61.0 0.6 broadcast_in_dim.4
  61.7 3.9 %all-to-all-start.1 = ((bf16[8,32,128]{2,1,0:T(8,128)(2,1)}), bf16[8,32,128]{2,1,0:T(8,128)(2,1)S(1)}, u32[]{:S(2)}, u32[]{:S(2)}) async-start(bf16[8,32,128]{2,1,0:T(8,128)(2,1)} %broadcast_in_dim.4), calls=%async_computation.1 | async-start | bytes 131072 | tf_op jit(solution)/shard_map/all_to_all | solution.py:437
  65.6 0.0 collective-permute-done.8.mid_high_ref
  65.7 0.0 copy-start.15
  65.7 1.1 %collective-permute-done.7.mid_low_ref = bf16[768,128]{1,0:T(8,128)(2,1)S(1)} collective-permute-done((bf16[768,128]{1,0:T(8,128)(2,1)S(1)}, bf16[768,128]{1,0:T(8,128)(2,1)S(1)}, u32[]{:S(2)}, u32[]{:S(2)}) %collective-permute-start.7) | collective-permute-done | bytes 196640 | tf_op jit(solution)/shard_map/ppermute | solution.py:673
  66.8 3.3 %collective-permute-start.10 = (bf16[768,128]{1,0:T(8,128)(2,1)S(1)}, bf16[768,128]{1,0:T(8,128)(2,1)S(1)}, u32[]{:S(2)}, u32[]{:S(2)}) collective-permute-start(bf16[768,128]{1,0:T(8,128)(2,1)S(1)} %pad_maximum_fusion.3), channel_id=1, source_target_pairs={{0,248},{8,0},{16,8},{24,16},{32,24},{40,32},{48,40},{56,48},{64,5... | collective-permute-start | bytes 589832 | tf_op jit(solution)/shard_map/ppermute | solution.py:676
  70.1 0.7 pad_maximum_fusion.2
  70.8 0.1 collective-permute-start.9
  70.9 2.8 %local.1.part_ref = f32[1024,128]{1,0:T(8,128)S(1)} custom-call(s32[1]{0:T(128)S(6)} %copy.24.count_ref.refs_0_, s32[1,4096]{1,0:T(1,128)S(1)} %copy-done.12, s32[1,4096]{1,0:T(1,128)S(1)} %copy-done.11, bf16[4096,128]{1,0:T(8,128)(2,1)S(1)} %get-tuple-element.77.refs_2_.dedge_ref, f32[1024,128]{1,0:T(8,128)S(1)} %copy-done.15, bf16[256,128]{1,0:T(8,128)(2,1)S(1)} %copy-done.6), custom_call_target="tpu_custom_call" | custom-call | flops 2147483648 | bytes 3145728 | tf_op jit(solution)/shard_map/local/pallas_call | solution.py:535
  73.7 0.0 all-to-all-done.1
  73.7 0.1 collective-permute-done.10.up_ref
  73.8 0.0 collective-permute-done.9.down_ref
  73.8 0.7 broadcast_in_dim.5
  74.5 5.9 %all-to-all-start.2 = ((bf16[16,32,128]{2,1,0:T(8,128)(2,1)}), bf16[16,32,128]{2,1,0:T(8,128)(2,1)S(1)}, u32[]{:S(2)}, u32[]{:S(2)}) async-start(bf16[16,32,128]{2,1,0:T(8,128)(2,1)} %broadcast_in_dim.5), calls=%async_computation.2 | async-start | bytes 262144 | tf_op jit(solution)/shard_map/all_to_all | solution.py:437
  80.4 2.1 %returned.1 = f32[1024,128]{1,0:T(8,128)} custom-call(s32[5]{0:T(128)S(1)} %stack.15.place_ref.refs_0_, s32[1,8]{1,0:T(1,128)S(1)} %copy-done.2, s32[1,8,256]{2,1,0:T(8,128)S(1)} %copy-done, s16[2048,128]{1,0:T(8,128)(2,1)S(1)} %get-tuple-element.87.cols_ref, bf16[768,128]{1,0:T(8,128)(2,1)S(1)} %collective-permute-done.9.down_ref, ...), custom_call_target="tpu_custom_call" | custom-call | flops 536870912 | bytes 2097152 | tf_op jit(solution)/shard_map/returned/pallas_call | solution.py:548
  82.6 4.6 %all-to-all-done.2 = bf16[16,32,128]{2,1,0:T(8,128)(2,1)S(1)} async-done(((bf16[16,32,128]{2,1,0:T(8,128)(2,1)}), bf16[16,32,128]{2,1,0:T(8,128)(2,1)S(1)}, u32[]{:S(2)}, u32[]{:S(2)}) %all-to-all-start.2) | async-done | bytes 131104 | tf_op jit(solution)/shard_map/all_to_all | solution.py:437
  87.1 4.2 %collective-permute-start.11 = (bf16[512,128]{1,0:T(8,128)(2,1)S(1)}, bf16[512,128]{1,0:T(8,128)(2,1)S(1)}, u32[]{:S(2)}, u32[]{:S(2)}) collective-permute-start(bf16[512,128]{1,0:T(8,128)(2,1)S(1)} %bitcast.5), channel_id=1, source_target_pairs={{0,8},{8,0},{1,9},{9,1},{2,10},{10,2},{3,11},{11,3},{4,12},{12,4},... | collective-permute-start | bytes 393224 | tf_op jit(solution)/shard_map/ppermute | solution.py:688
  91.4 1.0 %collective-permute-done.11.refs_2_ = bf16[512,128]{1,0:T(8,128)(2,1)S(1)} collective-permute-done((bf16[512,128]{1,0:T(8,128)(2,1)S(1)}, bf16[512,128]{1,0:T(8,128)(2,1)S(1)}, u32[]{:S(2)}, u32[]{:S(2)}) %collective-permute-start.11) | collective-permute-done | bytes 131104 | tf_op jit(solution)/shard_map/ppermute | solution.py:688
  92.4 1.4 %scaled.1 = (f32[256,128]{1,0:T(8,128)}, f32[128,128]{1,0:T(8,128)}, f32[256,128]{1,0:T(8,128)}, f32[128,128]{1,0:T(8,128)}, f32[128,128]{1,0:T(8,128)}, /*index=5*/f32[128,128]{1,0:T(8,128)}) custom-call(s32[5]{0:T(128)S(1)} %stack.15.place_ref.refs_0_, bf16[512,128]{1,0:T(8,128)(2,1)S(1)} %bitcast.6, bf16[512,128]{1,0:T(8,128)(2,1)S(1)} %collective-permute-done.11.refs_2_), custom_call_target="tpu_custom_call" | custom-call | tf_op jit(solution)/shard_map/scaled/pallas_call | solution.py:561
  (25 shorter events, 0.2 us)
Async XLA Ops:
  0.6 0.7 copy-start
  0.7 0.7 copy-start.2
  1.4 1.0 %copy-start.3 = (bf16[1024,128]{1,0:T(8,128)(2,1)S(1)}, bf16[1024,128]{1,0:T(8,128)(2,1)}, u32[]{:S(2)}) copy-start(bf16[1024,128]{1,0:T(8,128)(2,1)} %nodes_ref.7) | copy-start | bytes 786436
  3.7 6.1 %collective-permute-start = (bf16[768,128]{1,0:T(8,128)(2,1)S(1)}, bf16[768,128]{1,0:T(8,128)(2,1)S(1)}, u32[]{:S(2)}, u32[]{:S(2)}) collective-permute-start(bf16[768,128]{1,0:T(8,128)(2,1)S(1)} %get-tuple-element.57), channel_id=1, source_target_pairs={{0,8},{8,16},{16,24},{24,32},{32,40},{40,48},{48,56},{56,64},{64,7... | collective-permute-start | bytes 589832 | tf_op jit(solution)/shard_map/ppermute | solution.py:601
  6.4 5.1 %collective-permute-start.1 = (bf16[768,128]{1,0:T(8,128)(2,1)S(1)}, bf16[768,128]{1,0:T(8,128)(2,1)S(1)}, u32[]{:S(2)}, u32[]{:S(2)}) collective-permute-start(bf16[768,128]{1,0:T(8,128)(2,1)S(1)} %get-tuple-element.58), channel_id=1, source_target_pairs={{0,248},{8,0},{16,8},{24,16},{32,24},{40,32},{48,40},{56,48},{64,5... | collective-permute-start | bytes 589832 | tf_op jit(solution)/shard_map/ppermute | solution.py:602
  7.7 0.7 copy-start.11
  8.5 1.3 %copy-start.1 = (bf16[128,128]{1,0:T(8,128)(2,1)S(1)}, bf16[128,128]{1,0:T(8,128)(2,1)}, u32[]{:S(2)}) copy-start(bf16[128,128]{1,0:T(8,128)(2,1)} %dcoarse_ref.1) | copy-start | bytes 98308
  11.6 8.7 %collective-permute-start.3 = (bf16[800,128]{1,0:T(8,128)(2,1)S(1)}, bf16[800,128]{1,0:T(8,128)(2,1)S(1)}, u32[]{:S(2)}, u32[]{:S(2)}) collective-permute-start(bf16[800,128]{1,0:T(8,128)(2,1)S(1)} %pad_maximum_fusion.1), channel_id=1, source_target_pairs={{0,7},{1,0},{2,1},{3,2},{4,3},{5,4},{6,5},{7,6},{8,15},{9,8},{10,9... | collective-permute-start | bytes 614408 | tf_op jit(solution)/shard_map/ppermute | solution.py:613
  17.5 0.7 copy-start.12
  17.5 6.1 %copy-start.5 = (bf16[256,128]{1,0:T(8,128)(2,1)S(1)}, bf16[256,128]{1,0:T(8,128)(2,1)}, u32[]{:S(2)}) copy-start(bf16[256,128]{1,0:T(8,128)(2,1)} %wni_ref.3) | copy-start | bytes 196612
  17.6 6.1 %copy-start.6 = (bf16[256,128]{1,0:T(8,128)(2,1)S(1)}, bf16[256,128]{1,0:T(8,128)(2,1)}, u32[]{:S(2)}) copy-start(bf16[256,128]{1,0:T(8,128)(2,1)} %wei_ref.5) | copy-start | bytes 196612
  17.6 6.1 %copy-start.7 = (bf16[128,128]{1,0:T(8,128)(2,1)S(1)}, bf16[128,128]{1,0:T(8,128)(2,1)}, u32[]{:S(2)}) copy-start(bf16[128,128]{1,0:T(8,128)(2,1)} %weo_ref.3) | copy-start | bytes 98308
  17.6 6.1 %copy-start.8 = (bf16[128,128]{1,0:T(8,128)(2,1)S(1)}, bf16[128,128]{1,0:T(8,128)(2,1)}, u32[]{:S(2)}) copy-start(bf16[128,128]{1,0:T(8,128)(2,1)} %wno_ref.3) | copy-start | bytes 98308
  17.6 6.1 %collective-permute-start.2 = (bf16[800,128]{1,0:T(8,128)(2,1)S(1)}, bf16[800,128]{1,0:T(8,128)(2,1)S(1)}, u32[]{:S(2)}, u32[]{:S(2)}) collective-permute-start(bf16[800,128]{1,0:T(8,128)(2,1)S(1)} %pad_maximum_fusion), channel_id=1, source_target_pairs={{0,1},{1,2},{2,3},{3,4},{4,5},{5,6},{6,7},{7,0},{8,9},{9,10},{10,1... | collective-permute-start | bytes 614408 | tf_op jit(solution)/shard_map/ppermute | solution.py:606
  19.6 4.1 %copy-start.13 = (s32[1,1024]{1,0:T(1,128)S(1)}, s32[1,1024]{1,0:T(1,128)}, u32[]{:S(2)}) copy-start(s32[1,1024]{1,0:T(1,128)} %pool_ref.3) | copy-start | bytes 12292
  23.7 10.3 %copy-start.4 = (bf16[1024,128]{1,0:T(8,128)(2,1)S(1)}, bf16[1024,128]{1,0:T(8,128)(2,1)}, u32[]{:S(2)}) copy-start(bf16[1024,128]{1,0:T(8,128)(2,1)} %dfine_ref.1) | copy-start | bytes 786436
  23.7 10.3 %copy-start.10 = (bf16[128,128]{1,0:T(8,128)(2,1)S(1)}, bf16[128,128]{1,0:T(8,128)(2,1)}, u32[]{:S(2)}) copy-start(bf16[128,128]{1,0:T(8,128)(2,1)} %wco_ref.1) | copy-start | bytes 98308
  30.2 3.8 %copy-start.9 = (bf16[128,128]{1,0:T(8,128)(2,1)S(1)}, bf16[128,128]{1,0:T(8,128)(2,1)}, u32[]{:S(2)}) copy-start(bf16[128,128]{1,0:T(8,128)(2,1)} %wci_ref.1) | copy-start | bytes 98308
  30.2 3.8 %collective-permute-start.4 = (bf16[64,128]{1,0:T(8,128)(2,1)S(1)}, bf16[64,128]{1,0:T(8,128)(2,1)S(1)}, u32[]{:S(2)}, u32[]{:S(2)}) collective-permute-start(bf16[64,128]{1,0:T(8,128)(2,1)S(1)} %get-tuple-element.69), channel_id=1, source_target_pairs={{0,1},{1,2},{2,3},{3,4},{4,5},{5,6},{6,7},{7,0},{8,9},{9,10},{10,1... | collective-permute-start | bytes 49160 | tf_op jit(solution)/shard_map/ppermute | solution.py:640
  30.2 3.8 %collective-permute-start.5 = (bf16[64,128]{1,0:T(8,128)(2,1)S(1)}, bf16[64,128]{1,0:T(8,128)(2,1)S(1)}, u32[]{:S(2)}, u32[]{:S(2)}) collective-permute-start(bf16[64,128]{1,0:T(8,128)(2,1)S(1)} %get-tuple-element.70), channel_id=1, source_target_pairs={{0,7},{1,0},{2,1},{3,2},{4,3},{5,4},{6,5},{7,6},{8,15},{9,8},{10,9... | collective-permute-start | bytes 49160 | tf_op jit(solution)/shard_map/ppermute | solution.py:641
  38.9 0.8 copy-start.14
  39.7 5.4 %collective-permute-start.6 = (bf16[512,128]{1,0:T(8,128)(2,1)S(1)}, bf16[512,128]{1,0:T(8,128)(2,1)S(1)}, u32[]{:S(2)}, u32[]{:S(2)}) collective-permute-start(bf16[512,128]{1,0:T(8,128)(2,1)S(1)} %get-tuple-element.76), channel_id=1, source_target_pairs={{0,8},{8,0},{1,9},{9,1},{2,10},{10,2},{3,11},{11,3},{4,12},{12,4},... | collective-permute-start | bytes 393224 | tf_op jit(solution)/shard_map/ppermute | solution.py:668
  45.8 12.2 %all-to-all-start = ((bf16[16,32,128]{2,1,0:T(8,128)(2,1)}), bf16[16,32,128]{2,1,0:T(8,128)(2,1)S(1)}, u32[]{:S(2)}, u32[]{:S(2)}) async-start(bf16[16,32,128]{2,1,0:T(8,128)(2,1)} %bitcast.3), calls=%async_computation | async-start | bytes 262144 | tf_op jit(solution)/shard_map/all_to_all | solution.py:431
  58.0 7.6 %collective-permute-start.8 = (bf16[768,128]{1,0:T(8,128)(2,1)S(1)}, bf16[768,128]{1,0:T(8,128)(2,1)S(1)}, u32[]{:S(2)}, u32[]{:S(2)}) collective-permute-start(bf16[768,128]{1,0:T(8,128)(2,1)S(1)} %get-tuple-element.84), channel_id=1, source_target_pairs={{0,7},{1,0},{2,1},{3,2},{4,3},{5,4},{6,5},{7,6},{8,15},{9,8},{10,9... | collective-permute-start | bytes 589832 | tf_op jit(solution)/shard_map/ppermute | solution.py:672
  61.0 5.7 %collective-permute-start.7 = (bf16[768,128]{1,0:T(8,128)(2,1)S(1)}, bf16[768,128]{1,0:T(8,128)(2,1)S(1)}, u32[]{:S(2)}, u32[]{:S(2)}) collective-permute-start(bf16[768,128]{1,0:T(8,128)(2,1)S(1)} %get-tuple-element.82), channel_id=1, source_target_pairs={{0,1},{1,2},{2,3},{3,4},{4,5},{5,6},{6,7},{7,0},{8,9},{9,10},{10,1... | collective-permute-start | bytes 589832 | tf_op jit(solution)/shard_map/ppermute | solution.py:673
  61.7 12.0 %all-to-all-start.1 = ((bf16[8,32,128]{2,1,0:T(8,128)(2,1)}), bf16[8,32,128]{2,1,0:T(8,128)(2,1)S(1)}, u32[]{:S(2)}, u32[]{:S(2)}) async-start(bf16[8,32,128]{2,1,0:T(8,128)(2,1)} %broadcast_in_dim.4), calls=%async_computation.1 | async-start | bytes 131072 | tf_op jit(solution)/shard_map/all_to_all | solution.py:437
  65.7 5.2 %copy-start.15 = (f32[1024,128]{1,0:T(8,128)S(1)}, f32[1024,128]{1,0:T(8,128)}, u32[]{:S(2)}) copy-start(f32[1024,128]{1,0:T(8,128)} %copy-done.14) | copy-start | bytes 1572868
  66.8 7.0 %collective-permute-start.10 = (bf16[768,128]{1,0:T(8,128)(2,1)S(1)}, bf16[768,128]{1,0:T(8,128)(2,1)S(1)}, u32[]{:S(2)}, u32[]{:S(2)}) collective-permute-start(bf16[768,128]{1,0:T(8,128)(2,1)S(1)} %pad_maximum_fusion.3), channel_id=1, source_target_pairs={{0,248},{8,0},{16,8},{24,16},{32,24},{40,32},{48,40},{56,48},{64,5... | collective-permute-start | bytes 589832 | tf_op jit(solution)/shard_map/ppermute | solution.py:676
  70.8 3.1 %collective-permute-start.9 = (bf16[768,128]{1,0:T(8,128)(2,1)}, bf16[768,128]{1,0:T(8,128)(2,1)S(1)}, u32[]{:S(2)}, u32[]{:S(2)}) collective-permute-start(bf16[768,128]{1,0:T(8,128)(2,1)} %pad_maximum_fusion.2), channel_id=1, source_target_pairs={{0,8},{8,16},{16,24},{24,32},{32,40},{40,48},{48,56},{56,64},{64,7... | collective-permute-start | bytes 589832 | tf_op jit(solution)/shard_map/ppermute | solution.py:679
  74.5 12.6 %all-to-all-start.2 = ((bf16[16,32,128]{2,1,0:T(8,128)(2,1)}), bf16[16,32,128]{2,1,0:T(8,128)(2,1)S(1)}, u32[]{:S(2)}, u32[]{:S(2)}) async-start(bf16[16,32,128]{2,1,0:T(8,128)(2,1)} %broadcast_in_dim.5), calls=%async_computation.2 | async-start | bytes 262144 | tf_op jit(solution)/shard_map/all_to_all | solution.py:437
  87.1 5.2 %collective-permute-start.11 = (bf16[512,128]{1,0:T(8,128)(2,1)S(1)}, bf16[512,128]{1,0:T(8,128)(2,1)S(1)}, u32[]{:S(2)}, u32[]{:S(2)}) collective-permute-start(bf16[512,128]{1,0:T(8,128)(2,1)S(1)} %bitcast.5), channel_id=1, source_target_pairs={{0,8},{8,0},{1,9},{9,1},{2,10},{10,2},{3,11},{11,3},{4,12},{12,4},... | collective-permute-start | bytes 393224 | tf_op jit(solution)/shard_map/ppermute | solution.py:688
